TPU v7x, 32 devices: a whole 2x2x4 slice. The times are simulated.
32 devices in a mesh: pipe: 2 (over x), dp: 4 (over z), mp: 4 (over y, core).
Axes of the slice: x: 2, y: 2, z: 4, core: 2. Of those that a mesh axis runs over, the one named last changes fastest.
Arguments:
- layer_input: bfloat16 [2, 1024, 16384], P('pipe', 'dp', 'mp'), may hold values from -6 to 6
- kv_cotangent: bfloat16 [2, 1024, 2, 1024], P('pipe', 'dp', None, 'mp'), may hold values from -6 to 6
- kv_weight: bfloat16 [2, 16384, 2, 1024], P('pipe', 'dp', None, 'mp'), may hold values from -0.046875 to 0.046875
Outputs:
- input_grad: bfloat16 [2, 1024, 16384], P('pipe', None, ('dp', 'mp'))
- grad_mantissa: bfloat16 [2, 16384, 2, 1024], P('pipe', 'dp', None, 'mp')
- grad_scale: float32 [2, 16384, 2, 8], P('pipe', 'dp', None, 'mp')
All inputs are finite; a program needn't handle non-finite values. Where the computation divides by a largest or mean magnitude, that divisor is 1e-20 or more.
Results may differ from a plain program's by a relative error of at most 0.018.
Values may be sent and summed in bfloat16 or wider, within the bound.
No kernel may reach another device: no remote copies, remote signals or barrier semaphores. Data moves between devices by JAX's collectives and lax.ppermute only.
A program may use at most 192 MiB of HBM per device.

v0:
```python
import jax
import jax.numpy as jnp
from jax import lax
from jax.sharding import PartitionSpec as P

BLOCK = 128


def passed_along(x, axis, by):
    devices = lax.axis_size(axis)
    pairs = [(i, i + by) for i in range(devices) if 0 <= i + by < devices]
    return lax.ppermute(x, axis, pairs)


def on_device(layer_input, kv_cotangent, kv_weight):
    features = layer_input[0]
    grads = kv_cotangent[0]
    weights = kv_weight[0]
    row_count = grads.shape[0]
    columns = 2 * grads.shape[2]
    flat_grad = grads.reshape(row_count, columns)
    flat_weight = weights.reshape(weights.shape[0], columns)
    weight_grad = lax.dot_general(
        lax.all_gather(features, "mp", axis=1, tiled=True),
        flat_grad,
        (((0,), (0,)), ((), ())),
        preferred_element_type=jnp.float32,
    )
    piece = lax.all_gather(grads, "dp", axis=0, tiled=True)
    flat_piece = piece.reshape(piece.shape[0], columns)
    partial_sum = lax.dot_general(
        flat_piece, flat_weight, (((1,), (1,)), ((), ())), preferred_element_type=jnp.float32
    )
    summed = lax.psum_scatter(
        partial_sum.astype(jnp.bfloat16), "mp", scatter_dimension=1, tiled=True
    )
    arrived = passed_along(summed, "pipe", -1)
    row_total = weight_grad.shape[0]
    blocked = weight_grad.reshape(row_total, columns // BLOCK, BLOCK)
    local_max = jnp.max(jnp.abs(blocked), axis=2)
    block_scale = lax.pmax(local_max.astype(jnp.bfloat16), "dp").astype(local_max.dtype) + 1e-06
    scaled = (blocked / block_scale[:, :, None]).astype(jnp.bfloat16).astype(jnp.float32)
    totals = lax.psum_scatter(
        scaled.reshape(row_total, columns).astype(jnp.bfloat16),
        "dp",
        scatter_dimension=0,
        tiled=True,
    ).astype(jnp.float32)
    share = totals.shape[0]
    mantissa = totals.astype(jnp.bfloat16).reshape(share, 2, columns // 2)
    own_scale = lax.dynamic_slice_in_dim(block_scale, lax.axis_index("dp") * share, share, 0)
    own_scale = own_scale.reshape(share, 2, columns // (2 * BLOCK))
    return (arrived[None], mantissa[None], own_scale[None])


def solution(mesh):
    in_specs = (P("pipe", "dp", "mp"), P("pipe", "dp", None, "mp"), P("pipe", "dp", None, "mp"))
    out_specs = (
        P("pipe", None, ("dp", "mp")),
        P("pipe", "dp", None, "mp"),
        P("pipe", "dp", None, "mp"),
    )
    return jax.shard_map(
        on_device, mesh=mesh, in_specs=in_specs, out_specs=out_specs, check_vma=False
    )
```

profile of v0, /device:TPU:0, one launch (start us, length us, event | category | flops | bytes accessed | tf_op | source)
XLA Modules:
  0.0 527.1 jit_solution(6426386224492153107)
XLA Ops:
  7.2 0.0 all-gather.5.cloned.1.call-start
  7.2 0.7 all-gather.5.cloned.1.call-update
  7.9 0.0 all-gather.7.cloned.1.call-start
  7.9 0.7 all-gather.7.cloned.1.call-update
  8.6 0.0 all-reduce.2.cloned.1.call-start
  8.7 1.0 copy.14
  9.7 0.1 copy.9
  9.8 4.9 copy.13
  14.8 25.5 %all-gather.5.cloned.1.call-done = bf16[1,1024,2,256]{3,2,0,1:T(2,128)(2,1)} async-done(((bf16[1,256,2,256]{3,2,0,1:T(2,128)(2,1)}), bf16[1,1024,2,256]{3,2,0,1:T(2,128)(2,1)}) %all-gather.5.cloned.1.call-update) | async-done | bytes 1048592 | tf_op jit(solution)/shard_map/all_gather | solution.py:29
  40.2 1.4 copy.12
  41.7 57.9 %all-gather.7.cloned.1.call-done = bf16[1,256,16384]{2,1,0:T(8,128)(2,1)} async-done(((bf16[1,256,4096]{2,1,0:T(8,128)(2,1)}), bf16[1,256,16384]{2,1,0:T(8,128)(2,1)}) %all-gather.7.cloned.1.call-update) | async-done | bytes 8388624 | tf_op jit(solution)/shard_map/all_gather | solution.py:24
  99.6 17.3 %abs_reduce_fusion = (bf16[16384,4]{0,1:T(4,128)(2,1)}, f32[16384,4,128]{0,2,1:T(8,128)}) fusion(bf16[4,128,256]{2,1,0:T(8,128)(2,1)S(1)} %bitcast.33, bf16[1,256,16384]{2,1,0:T(8,128)(2,1)} %all-gather.7.cloned.1.call-done), kind=kOutput, calls=%fused_computation.1 | convolution fusion | flops 4320067584 | bytes 42336256 | tf_op jit(solution)/shard_map/dot_general | solution.py:23
  116.9 0.0 all-reduce.2.cloned.1.call-update
  116.9 0.0 reduce-scatter.3.cloned.1.call-start
  117.0 8.9 %convolution_convert_fusion = bf16[1024,4096]{1,0:T(8,128)(2,1)} fusion(bf16[1024,512]{1,0:T(8,128)(2,1)S(1)} %bitcast.35, bf16[4096,512]{1,0:T(8,128)(2,1)} %bitcast.31), kind=kOutput, calls=%fused_computation.4 | convolution fusion | flops 4299161600 | bytes 13631488 | tf_op jit(solution)/shard_map/dot_general | solution.py:31
  125.9 0.0 reduce-scatter.3.cloned.1.call-update
  125.9 0.0 reduce-scatter.5.cloned.1.call-start
  126.0 25.6 %all-reduce.2.cloned.1.call-done = bf16[16384,4]{0,1:T(4,128)(2,1)} async-done(((bf16[16384,4]{0,1:T(4,128)(2,1)}), bf16[16384,4]{0,1:T(4,128)(2,1)}) %all-reduce.2.cloned.1.call-update) | async-done | bytes 131088 | tf_op jit(solution)/shard_map/pmax | solution.py:41
  151.6 1.0 convert_add_fusion
  152.5 20.5 %divide_convert_fusion = bf16[16384,4,128]{0,2,1:T(8,128)(2,1)} fusion(f32[16384,4,128]{0,2,1:T(8,128)} %get-tuple-element.4, f32[16384,4]{0,1:T(4,128)S(1)} %convert_add_fusion), kind=kLoop, calls=%fused_computation | loop fusion | flops 16777216 | bytes 50593792 | tf_op jit(solution)/shard_map/convert_element_type | solution.py:42
  173.0 0.0 reduce-scatter.5.cloned.1.call-update
  173.0 52.5 %reduce-scatter.3.cloned.1.call-done = bf16[1024,1024]{1,0:T(8,128)(2,1)} async-done(((bf16[1024,4096]{1,0:T(8,128)(2,1)}), bf16[1024,1024]{1,0:T(8,128)(2,1)}) %reduce-scatter.3.cloned.1.call-update) | async-done | bytes 2097168 | tf_op jit(solution)/shard_map/reduce_scatter | solution.py:34
  225.6 1.3 collective-permute-start
  226.9 0.7 broadcast_in_dim_reshape.7
  227.6 47.4 %collective-permute-done = bf16[1024,1024]{1,0:T(8,128)(2,1)S(1)} collective-permute-done((bf16[1024,1024]{1,0:T(8,128)(2,1)}, bf16[1024,1024]{1,0:T(8,128)(2,1)S(1)}, u32[]{:S(2)}, u32[]{:S(2)}) %collective-permute-start) | collective-permute-done | bytes 2097184 | tf_op jit(solution)/shard_map/ppermute | solution.py:12
  275.0 233.1 %reduce-scatter.5.cloned.1.call-done = bf16[4096,512]{0,1:T(8,128)(2,1)} async-done(((bf16[16384,512]{0,1:T(8,128)(2,1)}), bf16[4096,512]{0,1:T(8,128)(2,1)}) %reduce-scatter.5.cloned.1.call-update) | async-done | bytes 4194320 | tf_op jit(solution)/shard_map/reduce_scatter | solution.py:43
  508.1 11.1 %copy.11 = bf16[1,4096,2,256]{3,2,1,0:T(2,128)(2,1)} copy(bf16[1,4096,2,256]{1,3,2,0:T(8,128)(2,1)} %bitcast.30) | data formatting | bytes 8388608 | tf_op jit(solution)/shard_map/broadcast_in_dim;reshape | solution.py:53
  519.2 1.3 copy.17
  (1 shorter events, 0.0 us)
Async XLA Ops:
  7.2 33.1 %all-gather.5.cloned.1.call-start = ((), (), s32[]{:S(2)}) async-start(), calls=%async_computation.5 | async-start | bytes 1310720 | tf_op jit(solution)/shard_map/all_gather | solution.py:29
  7.9 91.7 %all-gather.7.cloned.1.call-start = ((), (), s32[]{:S(2)}) async-start(), calls=%async_computation.6 | async-start | bytes 10485760 | tf_op jit(solution)/shard_map/all_gather | solution.py:24
  8.6 142.9 %all-reduce.2.cloned.1.call-start = ((), (), s32[]{:S(2)}) async-start(), calls=%async_computation.3 | async-start | bytes 262144 | tf_op jit(solution)/shard_map/pmax | solution.py:41
  116.9 108.7 %reduce-scatter.3.cloned.1.call-start = ((), (), s32[]{:S(2)}) async-start(), calls=%async_computation.2 | async-start | bytes 10485760 | tf_op jit(solution)/shard_map/reduce_scatter | solution.py:34
  125.9 382.2 %reduce-scatter.5.cloned.1.call-start = ((), (), s32[]{:S(2)}) async-start(), calls=%async_computation.4 | async-start | bytes 20971520 | tf_op jit(solution)/shard_map/reduce_scatter | solution.py:43
  225.6 49.4 %collective-permute-start = (bf16[1024,1024]{1,0:T(8,128)(2,1)}, bf16[1024,1024]{1,0:T(8,128)(2,1)S(1)}, u32[]{:S(2)}, u32[]{:S(2)}) collective-permute-start(bf16[1024,1024]{1,0:T(8,128)(2,1)} %reduce-scatter.3.cloned.1.call-done), channel_id=1, source_target_pairs={{16,0},{17,1},{18,2},{19,3},{20,4},{21,5},{22,6},{23,7},{24,8},{25... | collective-permute-start | bytes 6291464 | tf_op jit(solution)/shard_map/ppermute | solution.py:12
Sparse Core Ops, SparseCore 0:
  9.6 30.6 all-gather.4
  41.8 57.7 all-gather.6
  117.0 34.5 all-reduce.1
  154.2 71.3 reduce-scatter.2
  227.8 280.2 reduce-scatter.4
where the time goes:
time: 528 us; the launch traced here: 527 us
  waiting for transfers between devices  444 us (84%)
  matrix products  26.2 us (5%)
  other arithmetic  21.4 us (4%)
  local copies, waits for them, and re-layouts  20.6 us (4%)
  between operations  13.8 us (3%)
    reduce_scatter x1, waiting for transfers between devices, on_device(): lax.psum_scatter(scaled.reshape(row_total, columns).astype(jnp.bfloat16),...  233 us
    all_gather x1, waiting for transfers between devices, on_device(): lax.all_gather(features, 'mp', axis=1, tiled=True)  57.9 us
    reduce_scatter x1, waiting for transfers between devices, on_device(): lax.psum_scatter(partial_sum.astype(jnp.bfloat16), 'mp', scatter_dimensio...  52.5 us
    ppermute x1, waiting for transfers between devices, passed_along(): return lax.ppermute(x, axis, pairs)  47.4 us
    pmax x1, waiting for transfers between devices, on_device(): lax.pmax(local_max.astype(jnp.bfloat16), 'dp').astype(local_max.dtype)  25.6 us
    all_gather x1, waiting for transfers between devices, on_device(): piece = lax.all_gather(grads, 'dp', axis=0, tiled=True)  25.5 us
    convert_element_type x1, other arithmetic, on_device(): (blocked / block_scale[:, :, None]).astype(jnp.bfloat16).astype(jnp.float32)  20.5 us
    dot_general x1, matrix products, on_device(): lax.dot_general(lax.all_gather(features, 'mp', axis=1, tiled=True), flat_...  17.3 us
  transfers between devices with their start and end apart: 6, of which 6 were waited for; matrix products, arithmetic and copies ran while one was open for 7% of the time, Pallas kernels for 0%

commit v1 on v0

v1 whole, which is shorter than its diff:
```python
import functools

import jax
import jax.numpy as jnp
from jax import lax
from jax.experimental import pallas as pl
from jax.experimental.pallas import tpu as pltpu
from jax.sharding import PartitionSpec as P

BLOCK = 128
TILE = 256


def weight_grad_kernel(picks, *refs):
    lefts, grads_ref, mantissa_ref, scale_ref = refs[:4], refs[4], refs[-2], refs[-1]
    parts = []
    top = None
    for i, left in enumerate(lefts):
        part = jnp.dot(grads_ref[picks[i]], left[...], preferred_element_type=jnp.float32)
        parts.append(part)
        top = jnp.abs(part) if top is None else jnp.maximum(top, jnp.abs(part))
    columns, rows = top.shape
    scale = jnp.max(top.reshape(columns // BLOCK, BLOCK, rows), axis=1) + 1e-6
    scale_ref[...] = scale
    inverse = 1.0 / scale
    inverse = jnp.broadcast_to(inverse[:, None, :], (columns // BLOCK, BLOCK, rows)).reshape(columns, rows)
    total = None
    for part in parts:
        term = (part * inverse).astype(jnp.bfloat16).astype(jnp.float32)
        total = term if total is None else total + term
    mantissa_ref[...] = total.T.astype(jnp.bfloat16)


def weight_grad(picks, lefts, grads, into, first, row_total):
    columns = grads.shape[1]
    tokens, rows = lefts[0].shape
    start = first // TILE
    in_specs = [pl.BlockSpec((tokens, TILE), lambda i, picks: (0, i)) for _ in lefts]
    in_specs.append(pl.BlockSpec(grads.shape, lambda i, picks: (0, 0, 0)))
    operands = [*lefts, grads]
    aliases = {}
    if into is not None:
        for n, held in enumerate(into):
            in_specs.append(pl.BlockSpec(memory_space=pl.ANY))
            operands.append(held)
            aliases[len(operands)] = n
    return pl.pallas_call(
        weight_grad_kernel,
        grid_spec=pltpu.PrefetchScalarGridSpec(
            num_scalar_prefetch=1,
            grid=(rows // TILE,),
            in_specs=in_specs,
            out_specs=[
                pl.BlockSpec((TILE, columns), lambda i, picks: (start + i, 0)),
                pl.BlockSpec((columns // BLOCK, TILE), lambda i, picks: (0, start + i)),
            ],
        ),
        out_shape=[
            jax.ShapeDtypeStruct((row_total, columns), jnp.bfloat16),
            jax.ShapeDtypeStruct((columns // BLOCK, row_total), jnp.float32),
        ],
        input_output_aliases=aliases,
        compiler_params=pltpu.CompilerParams(vmem_limit_bytes=32 * 1024 * 1024),
        cost_estimate=pl.CostEstimate(
            flops=2 * 4 * tokens * rows * columns, bytes_accessed=2 * rows * (4 * tokens + columns), transcendentals=0
        ),
    )(picks, *operands)


def on_device(layer_input, kv_cotangent, kv_weight):
    n_pipe, n_dp, n_mp = (lax.axis_size(a) for a in ("pipe", "dp", "mp"))
    p, m = lax.axis_index("dp"), lax.axis_index("mp")
    features = layer_input[0]
    tokens, width = features.shape
    columns = 2 * kv_cotangent.shape[3]
    rows = kv_weight.shape[1]
    share = rows // n_mp

    def move(x, where):
        pairs = []
        for i in range(n_dp):
            for j in range(n_mp):
                to = where(i, j)
                if to is not None:
                    pairs.append((i * n_mp + j, to[0] * n_mp + to[1]))
        return lax.ppermute(x, ("dp", "mp"), pairs)

    def across(x):
        return move(x, lambda i, j: (i, j ^ 2))

    def other_core(x):
        return move(x, lambda i, j: (i, j ^ 1))

    own_grad = kv_cotangent[0].reshape(tokens, columns)
    grads = [own_grad] + [move(own_grad, lambda i, j, k=k: (i ^ k, j)) for k in range(1, n_dp)]

    half = width // 2
    first, second = features[:, :half], features[:, half:]

    def along(x, near, crossed):
        def where(i, j):
            q = j ^ 2 if crossed else j
            if (q // 2 == i // 2) != near:
                return None
            return (q, 2 * (j // 2) + i % 2)

        return move(x, where)

    own_side = (m // 2) == (p // 2)
    second = across(second)
    blocks = []
    for x, crossed in ((first, False), (second, True)):
        here = own_side if not crossed else jnp.logical_not(own_side)
        got = []
        for near in (False, True):
            direct = along(x, near, crossed)
            got.append(jnp.where(here, direct, across(direct)))
        far, near = got
        blocks.append((near, far, other_core(near), other_core(far)))

    quarters = kv_weight[0].reshape(n_mp, share, columns)

    def quarter(k):
        return lax.dynamic_index_in_dim(quarters, m ^ k, 0, keepdims=False)

    w = [quarter(k) for k in range(n_mp)]

    def times(g, k):
        return lax.dot_general(g, w[k], (((1,), (1,)), ((), ())), preferred_element_type=jnp.float32)

    total = jnp.zeros((n_dp * tokens, share), jnp.bfloat16)
    for k, g in enumerate(grads):
        to_other = other_core(times(g, 3).astype(jnp.bfloat16))
        to_own = other_core(times(g, 1).astype(jnp.bfloat16))
        crossing = across((times(g, 2) + to_other.astype(jnp.float32)).astype(jnp.bfloat16))
        mine = times(g, 0) + to_own.astype(jnp.float32)
        mine = (mine + crossing.astype(jnp.float32)).astype(jnp.bfloat16)
        arrived = lax.ppermute(mine, "pipe", [(i, i - 1) for i in range(1, n_pipe)])
        total = lax.dynamic_update_slice_in_dim(total, arrived, (p ^ k) * tokens, 0)

    turned = jnp.stack([g.T for g in grads])
    same = (m ^ p) & 1
    picks = jnp.stack([same, 2 + same, 1 - same, 3 - same]).astype(jnp.int32)
    into = None
    for n, four in enumerate(blocks):
        into = weight_grad(picks, four, turned, into, n * half, rows)
    mantissa, scale = into
    mantissa = mantissa.reshape(rows, 2, columns // 2)
    scale = scale.T.reshape(rows, 2, columns // (2 * BLOCK))
    return (total[None], mantissa[None], scale[None])


def solution(mesh):
    in_specs = (P("pipe", "dp", "mp"), P("pipe", "dp", None, "mp"), P("pipe", "dp", None, "mp"))
    out_specs = (
        P("pipe", None, ("dp", "mp")),
        P("pipe", "dp", None, "mp"),
        P("pipe", "dp", None, "mp"),
    )
    return jax.shard_map(on_device, mesh=mesh, in_specs=in_specs, out_specs=out_specs, check_vma=False)
```

time: 528 us -> 242 us (0.46)
  waiting for transfers between devices: 444 us -> 120 us
  starting transfers between devices: 1.48 us -> 42.4 us
  local copies, waits for them, and re-layouts: 20.6 us -> 38.7 us
  Pallas kernels: 0 us -> 17.8 us
  other arithmetic: 21.4 us -> 4.93 us
  between operations: 13.8 us -> 1.08 us
  matrix products: 26.2 us -> 15.5 us
    reduce_scatter x2 -> x0, waiting for transfers between devices: 286 us -> none  [the longest x1 233 us: on_device(): lax.psum_scatter(scaled.reshape(row_total, columns).astype(jnp.bfloat16),...]
    all_gather x2 -> x0, waiting for transfers between devices: 83.4 us -> none  [the longest x1 57.9 us: on_device(): lax.all_gather(features, 'mp', axis=1, tiled=True)]
    ppermute x1 -> x32, waiting for transfers between devices: 47.4 us -> 120 us  [the longest x28 120 us: move(): return lax.ppermute(x, ('dp', 'mp'), pairs)]
    ppermute x1 -> x32, starting transfers between devices: 1.28 us -> 42.4 us  [the longest x28 37.1 us: move(): return lax.ppermute(x, ('dp', 'mp'), pairs)]
    pmax x1 -> x0, waiting for transfers between devices: 25.6 us -> none  [on_device(): lax.pmax(local_max.astype(jnp.bfloat16), 'dp').astype(local_max.dtype)]
    convert_element_type x1, other arithmetic: 20.5 us -> 1.2 us  [on_device(): mine = (mine + crossing.astype(jnp.float32)).astype(jnp.bfloat16)]
    pallas_call x0 -> x2, Pallas kernels: none -> 17.8 us  [weight_grad(): pl.pallas_call(weight_grad_kernel, grid_spec=pltpu.PrefetchScalarGridSpec...]
    dot_general x2 -> x16, matrix products: 26.2 us -> 15.5 us  [times(): lax.dot_general(g, w[k], (((1,), (1,)), ((), ())), preferred_element_type...]
  transfers between devices with their start and end apart: 6 -> 32, of which waited for: 6 -> 9; matrix products, arithmetic and copies ran while one was open for 7% -> 20% of each run, Pallas kernels for 0% -> 4%
where the time goes in v1:
time: 242 us; the launch traced here: 240 us
  waiting for transfers between devices  120 us (50%)
  starting transfers between devices  42.4 us (18%)
  local copies, waits for them, and re-layouts  38.7 us (16%)
  Pallas kernels  17.8 us (7%)
  matrix products  15.5 us (6%)
  other arithmetic  4.93 us (2%)
    ppermute x28, waiting for transfers between devices, move(): return lax.ppermute(x, ('dp', 'mp'), pairs)  120 us
    ppermute x28, starting transfers between devices, move(): return lax.ppermute(x, ('dp', 'mp'), pairs)  37.1 us
    pallas_call x2, Pallas kernels, weight_grad(): pl.pallas_call(weight_grad_kernel, grid_spec=pltpu.PrefetchScalarGridSpec...  17.8 us
    dot_general x16, matrix products, times(): lax.dot_general(g, w[k], (((1,), (1,)), ((), ())), preferred_element_type...  15.5 us
    broadcast_in_dim x5, local copies, waits for them, and re-layouts, on_device(): return (total[None], mantissa[None], scale[None])  9.82 us
    another operation x1, local copies, waits for them, and re-layouts, on_device(): quarters = kv_weight[0].reshape(n_mp, share, columns)  7.73 us
    another operation x2, local copies, waits for them, and re-layouts, on_device(): return (total[None], mantissa[None], scale[None])  7.56 us
    dynamic_update_slice x4, local copies, waits for them, and re-layouts, on_device(): total = lax.dynamic_update_slice_in_dim(total, arrived, (p ^ k) * tokens, 0)  7.47 us
  transfers between devices with their start and end apart: 32, of which 9 were waited for; matrix products, arithmetic and copies ran while one was open for 20% of the time, Pallas kernels for 4%

profile of v1, /device:TPU:0, one launch (start us, length us, event | category | flops | bytes accessed | tf_op | source)
XLA Modules:
  0.0 240.3 jit_solution(14801445932064613864)
XLA Ops:
  1.7 3.1 %collective-permute-start.4 = (bf16[256,512]{0,1:T(8,128)(2,1)S(1)}, bf16[256,512]{0,1:T(8,128)(2,1)S(1)}, u32[]{:S(2)}, u32[]{:S(2)}) collective-permute-start(bf16[256,512]{0,1:T(8,128)(2,1)S(1)} %bitcast.145), channel_id=1, source_target_pairs={{0,4},{1,5},{2,6},{3,7},{4,0},{5,1},{6,2},{7,3},{8,12},{9,13},{10,... | collective-permute-start | bytes 786440 | tf_op jit(solution)/shard_map/ppermute | solution.py:86
  4.8 2.6 %collective-permute-start.9 = (bf16[256,512]{0,1:T(8,128)(2,1)S(1)}, bf16[256,512]{0,1:T(8,128)(2,1)S(1)}, u32[]{:S(2)}, u32[]{:S(2)}) collective-permute-start(bf16[256,512]{0,1:T(8,128)(2,1)S(1)} %bitcast.146), channel_id=1, source_target_pairs={{0,8},{1,9},{2,10},{3,11},{4,12},{5,13},{6,14},{7,15},{8,0},{9,1},... | collective-permute-start | bytes 786440 | tf_op jit(solution)/shard_map/ppermute | solution.py:86
  7.4 7.7 %reshape_squeeze.6 = bf16[4,1024,512]{2,1,0:T(8,128)(2,1)} reshape(bf16[1,4096,2,256]{3,2,1,0:T(2,128)(2,1)} %param.5) | data formatting | bytes 8388608 | tf_op jit(solution)/shard_map/reshape;squeeze | solution.py:121
  15.2 2.5 %fusion.16 = bf16[256,1024]{0,1:T(8,128)(2,1)} fusion(bf16[256,512]{0,1:T(8,128)(2,1)S(1)} %bitcast.148, bf16[4,1024,512]{2,1,0:T(8,128)(2,1)} %reshape_squeeze.6, s32[]{:T(128)S(6)} %select_n.58), kind=kOutput, calls=%fused_computation.32 | convolution fusion | flops 268697600 | bytes 1835012 | tf_op jit(solution)/shard_map/dot_general | solution.py:129
  17.6 2.5 %fusion.15 = bf16[256,1024]{0,1:T(8,128)(2,1)} fusion(bf16[256,512]{0,1:T(8,128)(2,1)S(1)} %bitcast.149, bf16[4,1024,512]{2,1,0:T(8,128)(2,1)} %reshape_squeeze.6, s32[]{:T(128)S(6)} %select_n.56), kind=kOutput, calls=%fused_computation.31 | convolution fusion | flops 268697600 | bytes 1835012 | tf_op jit(solution)/shard_map/dot_general | solution.py:129
  20.6 1.5 fusion.73
  22.1 1.8 convolution_bitcast_fusion.7
  23.9 2.3 collective-permute-done.9
  26.2 1.8 fusion.20
  31.8 1.6 collective-permute-start.19
  35.2 1.5 add_convert_fusion.1
  36.7 1.7 collective-permute-start.2
  38.8 1.3 collective-permute-start.28
  40.6 3.9 %collective-permute-start.12 = (bf16[256,1024]{0,1:T(8,128)(2,1)S(1)}, bf16[256,1024]{0,1:T(8,128)(2,1)S(1)}, u32[]{:S(2)}, u32[]{:S(2)}) collective-permute-start(bf16[256,1024]{0,1:T(8,128)(2,1)S(1)} %fusion.11), channel_id=1, source_target_pairs={{0,2},{1,3},{2,0},{3,1},{4,6},{5,7},{6,4},{7,5},{8,10},{9,11},{10,... | collective-permute-start | bytes 1572872 | tf_op jit(solution)/shard_map/ppermute | solution.py:86
  45.0 11.5 %collective-permute-done.19 = bf16[256,2048]{1,0:T(8,128)(2,1)S(1)} collective-permute-done((bf16[256,2048]{1,0:T(8,128)(2,1)S(1)}, bf16[256,2048]{1,0:T(8,128)(2,1)S(1)}, u32[]{:S(2)}, u32[]{:S(2)}) %collective-permute-start.19) | collective-permute-done | bytes 1048608 | tf_op jit(solution)/shard_map/ppermute | solution.py:86
  56.6 2.5 %collective-permute-start.27 = (bf16[256,2048]{1,0:T(8,128)(2,1)S(1)}, bf16[256,2048]{1,0:T(8,128)(2,1)S(1)}, u32[]{:S(2)}, u32[]{:S(2)}) collective-permute-start(bf16[256,2048]{1,0:T(8,128)(2,1)S(1)} %collective-permute-done.26), channel_id=1, source_target_pairs={{0,2},{1,3},{2,0},{3,1},{4,6},{5,7},{6,4},{7,5},{8,10},{9,11},{10,... | collective-permute-start | bytes 3145736 | tf_op jit(solution)/shard_map/ppermute | solution.py:86
  59.0 8.8 %collective-permute-done.2 = bf16[256,1024]{0,1:T(8,128)(2,1)S(1)} collective-permute-done((bf16[256,1024]{0,1:T(8,128)(2,1)S(1)}, bf16[256,1024]{0,1:T(8,128)(2,1)S(1)}, u32[]{:S(2)}, u32[]{:S(2)}) %collective-permute-start.2) | collective-permute-done | bytes 524320 | tf_op jit(solution)/shard_map/ppermute | solution.py:86
  69.7 9.3 %collective-permute-done.12 = bf16[256,1024]{0,1:T(8,128)(2,1)S(1)} collective-permute-done((bf16[256,1024]{0,1:T(8,128)(2,1)S(1)}, bf16[256,1024]{0,1:T(8,128)(2,1)S(1)}, u32[]{:S(2)}, u32[]{:S(2)}) %collective-permute-start.12) | collective-permute-done | bytes 524320 | tf_op jit(solution)/shard_map/ppermute | solution.py:86
  79.0 2.5 %collective-permute-start.17 = (bf16[256,1024]{0,1:T(8,128)(2,1)S(1)}, bf16[256,1024]{0,1:T(8,128)(2,1)S(1)}, u32[]{:S(2)}, u32[]{:S(2)}) collective-permute-start(bf16[256,1024]{0,1:T(8,128)(2,1)S(1)} %fusion.9), channel_id=1, source_target_pairs={{0,2},{1,3},{2,0},{3,1},{4,6},{5,7},{6,4},{7,5},{8,10},{9,11},{10,... | collective-permute-start | bytes 1572872 | tf_op jit(solution)/shard_map/ppermute | solution.py:86
  82.0 7.1 %collective-permute-done.28 = bf16[256,2048]{1,0:T(8,128)(2,1)S(1)} collective-permute-done((bf16[256,2048]{1,0:T(8,128)(2,1)S(1)}, bf16[256,2048]{1,0:T(8,128)(2,1)S(1)}, u32[]{:S(2)}, u32[]{:S(2)}) %collective-permute-start.28) | collective-permute-done | bytes 1048608 | tf_op jit(solution)/shard_map/ppermute | solution.py:86
  89.0 1.5 collective-permute-start.22
  90.6 2.2 collective-permute-start.29
  93.2 30.8 %collective-permute-done.17 = bf16[256,1024]{0,1:T(8,128)(2,1)S(1)} collective-permute-done((bf16[256,1024]{0,1:T(8,128)(2,1)S(1)}, bf16[256,1024]{0,1:T(8,128)(2,1)S(1)}, u32[]{:S(2)}, u32[]{:S(2)}) %collective-permute-start.17) | collective-permute-done | bytes 524320 | tf_op jit(solution)/shard_map/ppermute | solution.py:86
  124.0 1.3 collective-permute-start.3
  125.3 1.2 fusion.10
  126.5 1.3 collective-permute-start.13
  127.8 2.6 %collective-permute-start.21 = (bf16[256,2048]{1,0:T(8,128)(2,1)S(1)}, bf16[256,2048]{1,0:T(8,128)(2,1)S(1)}, u32[]{:S(2)}, u32[]{:S(2)}) collective-permute-start(bf16[256,2048]{1,0:T(8,128)(2,1)S(1)} %collective-permute-done.20), channel_id=1, source_target_pairs={{0,2},{1,3},{2,0},{3,1},{4,6},{5,7},{6,4},{7,5},{8,10},{9,11},{10,... | collective-permute-start | bytes 3145736 | tf_op jit(solution)/shard_map/ppermute | solution.py:86
  131.4 15.0 %collective-permute-done.29 = bf16[256,2048]{1,0:T(8,128)(2,1)S(1)} collective-permute-done((bf16[256,2048]{1,0:T(8,128)(2,1)S(1)}, bf16[256,2048]{1,0:T(8,128)(2,1)S(1)}, u32[]{:S(2)}, u32[]{:S(2)}) %collective-permute-start.29) | collective-permute-done | bytes 1048608 | tf_op jit(solution)/shard_map/ppermute | solution.py:86
  146.4 1.3 collective-permute-start.8
  147.7 2.5 %collective-permute-start.23 = (bf16[256,2048]{1,0:T(8,128)(2,1)S(1)}, bf16[256,2048]{1,0:T(8,128)(2,1)S(1)}, u32[]{:S(2)}, u32[]{:S(2)}) collective-permute-start(bf16[256,2048]{1,0:T(8,128)(2,1)S(1)} %collective-permute-done.22), channel_id=1, source_target_pairs={{0,2},{1,3},{2,0},{3,1},{4,6},{5,7},{6,4},{7,5},{8,10},{9,11},{10,... | collective-permute-start | bytes 3145736 | tf_op jit(solution)/shard_map/ppermute | solution.py:86
  151.4 17.5 %collective-permute-done.21 = bf16[256,2048]{1,0:T(8,128)(2,1)S(1)} collective-permute-done((bf16[256,2048]{1,0:T(8,128)(2,1)S(1)}, bf16[256,2048]{1,0:T(8,128)(2,1)S(1)}, u32[]{:S(2)}, u32[]{:S(2)}) %collective-permute-start.21) | collective-permute-done | bytes 1048608 | tf_op jit(solution)/shard_map/ppermute | solution.py:86
  168.9 1.5 collective-permute-start.18
  170.5 3.3 %collective-permute-start.30 = (bf16[256,2048]{1,0:T(8,128)(2,1)}, bf16[256,2048]{1,0:T(8,128)(2,1)}, u32[]{:S(2)}, u32[]{:S(2)}) collective-permute-start(bf16[256,2048]{1,0:T(8,128)(2,1)} %broadcast_select_fusion.1.refs_0_), channel_id=1, source_target_pairs={{0,1},{1,0},{2,3},{3,2},{4,5},{5,4},{6,7},{7,6},{8,9},{9,8},{10,11... | collective-permute-start | bytes 3145736 | tf_op jit(solution)/shard_map/ppermute | solution.py:86
  173.8 17.6 %collective-permute-done.23 = bf16[256,2048]{1,0:T(8,128)(2,1)S(1)} collective-permute-done((bf16[256,2048]{1,0:T(8,128)(2,1)S(1)}, bf16[256,2048]{1,0:T(8,128)(2,1)S(1)}, u32[]{:S(2)}, u32[]{:S(2)}) %collective-permute-start.23) | collective-permute-done | bytes 1048608 | tf_op jit(solution)/shard_map/ppermute | solution.py:86
  194.3 1.2 pad_maximum_fusion.refs_4_
  195.6 2.1 copy.9
  197.7 1.6 broadcast_in_dim.12
  199.3 1.9 constant_dynamic-update-slice_fusion.3
  201.1 2.1 copy.11
  203.2 2.0 copy.10
  205.2 2.0 copy.12
  207.3 1.9 constant_dynamic-update-slice_fusion.2
  209.2 1.9 constant_dynamic-update-slice_fusion.1
  211.0 1.9 constant_dynamic-update-slice_fusion
  212.9 9.0 %shard_map.58 = (bf16[4096,512]{1,0:T(8,128)(2,1)S(1)}, f32[4,4096]{1,0:T(4,128)S(1)}) custom-call(s32[4]{0:T(128)S(1)} %pad_add_fusion.picks, bf16[256,2048]{1,0:T(8,128)(2,1)} %broadcast_select_fusion.1.refs_0_, bf16[256,2048]{1,0:T(8,128)(2,1)} %broadcast_select_fusion.refs_1_, bf16[256,2048]{1,0:T(8,128)(2,1)} %collective-permute-done.30.refs_2_, ...), custom_call_target="tpu_custom_call" | custom-call | flops 2147483648 | bytes 6291456 | tf_op jit(solution)/shard_map/pallas_call | solution.py:47
  222.0 8.8 %shard_map.59 = (bf16[4096,512]{1,0:T(8,128)(2,1)S(1)}, f32[4,4096]{1,0:T(4,128)S(1)}) custom-call(s32[4]{0:T(128)S(1)} %pad_add_fusion.picks, bf16[256,2048]{1,0:T(8,128)(2,1)S(1)} %broadcast_select_fusion.3.refs_0_, bf16[256,2048]{1,0:T(8,128)(2,1)S(1)} %broadcast_select_fusion.2.refs_1_, ...), custom_call_target="tpu_custom_call", output_to_operand_aliasing={{0}: (6, {}), {1}: (7, {})} | custom-call | flops 2147483648 | bytes 6291456 | tf_op jit(solution)/shard_map/pallas_call | solution.py:47
  230.7 2.0 copy-done
  232.7 6.9 %broadcast_in_dim_reshape.6 = bf16[1,4096,2,256]{3,2,1,0:T(2,128)(2,1)} reshape(bf16[4096,512]{1,0:T(8,128)(2,1)} %copy-done) | data formatting | bytes 8388608 | tf_op jit(solution)/shard_map/broadcast_in_dim;reshape | solution.py:150
  (77 shorter events, 17.3 us)
Async XLA Ops:
  1.7 26.8 %collective-permute-start.4 = (bf16[256,512]{0,1:T(8,128)(2,1)S(1)}, bf16[256,512]{0,1:T(8,128)(2,1)S(1)}, u32[]{:S(2)}, u32[]{:S(2)}) collective-permute-start(bf16[256,512]{0,1:T(8,128)(2,1)S(1)} %bitcast.145), channel_id=1, source_target_pairs={{0,4},{1,5},{2,6},{3,7},{4,0},{5,1},{6,2},{7,3},{8,12},{9,13},{10,... | collective-permute-start | bytes 786440 | tf_op jit(solution)/shard_map/ppermute | solution.py:86
  4.8 21.4 %collective-permute-start.9 = (bf16[256,512]{0,1:T(8,128)(2,1)S(1)}, bf16[256,512]{0,1:T(8,128)(2,1)S(1)}, u32[]{:S(2)}, u32[]{:S(2)}) collective-permute-start(bf16[256,512]{0,1:T(8,128)(2,1)S(1)} %bitcast.146), channel_id=1, source_target_pairs={{0,8},{1,9},{2,10},{3,11},{4,12},{5,13},{6,14},{7,15},{8,0},{9,1},... | collective-permute-start | bytes 786440 | tf_op jit(solution)/shard_map/ppermute | solution.py:86
  7.4 22.1 %collective-permute-start.14 = (bf16[256,512]{0,1:T(8,128)(2,1)S(1)}, bf16[256,512]{0,1:T(8,128)(2,1)S(1)}, u32[]{:S(2)}, u32[]{:S(2)}) collective-permute-start(bf16[256,512]{0,1:T(8,128)(2,1)S(1)} %bitcast.147), channel_id=1, source_target_pairs={{0,12},{1,13},{2,14},{3,15},{4,8},{5,9},{6,10},{7,11},{8,4},{9,5},... | collective-permute-start | bytes 786440 | tf_op jit(solution)/shard_map/ppermute | solution.py:86
  7.4 13.2 %copy-start.5 = (bf16[1,256,4096]{2,1,0:T(8,128)(2,1)S(1)}, bf16[1,256,4096]{2,1,0:T(8,128)(2,1)}, u32[]{:S(2)}) copy-start(bf16[1,256,4096]{2,1,0:T(8,128)(2,1)} %param.3) | copy-start | bytes 6291460
  17.6 12.4 %collective-permute-start.1 = (bf16[256,1024]{0,1:T(8,128)(2,1)}, bf16[256,1024]{0,1:T(8,128)(2,1)}, u32[]{:S(2)}, u32[]{:S(2)}) collective-permute-start(bf16[256,1024]{0,1:T(8,128)(2,1)} %fusion.16), channel_id=1, source_target_pairs={{0,1},{1,0},{2,3},{3,2},{4,5},{5,4},{6,7},{7,6},{8,9},{9,8},{10,11... | collective-permute-start | bytes 1572872 | tf_op jit(solution)/shard_map/ppermute | solution.py:86
  20.1 10.9 %collective-permute-start = (bf16[256,1024]{0,1:T(8,128)(2,1)}, bf16[256,1024]{0,1:T(8,128)(2,1)}, u32[]{:S(2)}, u32[]{:S(2)}) collective-permute-start(bf16[256,1024]{0,1:T(8,128)(2,1)} %fusion.15), channel_id=1, source_target_pairs={{0,1},{1,0},{2,3},{3,2},{4,5},{5,4},{6,7},{7,6},{8,9},{9,8},{10,11... | collective-permute-start | bytes 1572872 | tf_op jit(solution)/shard_map/ppermute | solution.py:86
  22.1 5.9 %copy-start.1 = (bf16[4,1024,512]{2,1,0:T(8,128)(2,1)S(1)}, bf16[4,1024,512]{2,1,0:T(8,128)(2,1)}, u32[]{:S(2)}) copy-start(bf16[4,1024,512]{2,1,0:T(8,128)(2,1)} %reshape_squeeze.6) | copy-start | bytes 12582916
  23.9 7.1 %copy-start.6 = (bf16[256,2048]{1,0:T(8,128)(2,1)S(1)}, bf16[256,2048]{1,0:T(8,128)(2,1)}, u32[]{:S(2)}) copy-start(bf16[256,2048]{1,0:T(8,128)(2,1)} %get-tuple-element.11) | copy-start | bytes 3145732
  23.9 7.9 %copy-start.7 = (bf16[256,2048]{1,0:T(8,128)(2,1)S(1)}, bf16[256,2048]{1,0:T(8,128)(2,1)}, u32[]{:S(2)}) copy-start(bf16[256,2048]{1,0:T(8,128)(2,1)} %get-tuple-element.12) | copy-start | bytes 3145732
  26.2 55.8 %copy-start.3 = (bf16[256,512]{0,1:T(8,128)(2,1)}, bf16[256,512]{0,1:T(8,128)(2,1)S(1)}, u32[]{:S(2)}) copy-start(bf16[256,512]{0,1:T(8,128)(2,1)S(1)} %collective-permute-done.9) | copy-start | bytes 786436
  28.0 3.8 %collective-permute-start.11 = (bf16[256,1024]{0,1:T(8,128)(2,1)S(1)}, bf16[256,1024]{0,1:T(8,128)(2,1)S(1)}, u32[]{:S(2)}, u32[]{:S(2)}) collective-permute-start(bf16[256,1024]{0,1:T(8,128)(2,1)S(1)} %fusion.20), channel_id=1, source_target_pairs={{0,1},{1,0},{2,3},{3,2},{4,5},{5,4},{6,7},{7,6},{8,9},{9,8},{10,11... | collective-permute-start | bytes 1572872 | tf_op jit(solution)/shard_map/ppermute | solution.py:86
  28.5 64.2 %copy-start.2 = (bf16[256,512]{0,1:T(8,128)(2,1)}, bf16[256,512]{0,1:T(8,128)(2,1)S(1)}, u32[]{:S(2)}) copy-start(bf16[256,512]{0,1:T(8,128)(2,1)S(1)} %collective-permute-done.4) | copy-start | bytes 786436
  28.5 4.9 %collective-permute-start.10 = (bf16[256,1024]{0,1:T(8,128)(2,1)S(1)}, bf16[256,1024]{0,1:T(8,128)(2,1)S(1)}, u32[]{:S(2)}, u32[]{:S(2)}) collective-permute-start(bf16[256,1024]{0,1:T(8,128)(2,1)S(1)} %fusion.19), channel_id=1, source_target_pairs={{0,1},{1,0},{2,3},{3,2},{4,5},{5,4},{6,7},{7,6},{8,9},{9,8},{10,11... | collective-permute-start | bytes 1572872 | tf_op jit(solution)/shard_map/ppermute | solution.py:86
  29.5 95.8 %copy-start.4 = (bf16[256,512]{0,1:T(8,128)(2,1)}, bf16[256,512]{0,1:T(8,128)(2,1)S(1)}, u32[]{:S(2)}) copy-start(bf16[256,512]{0,1:T(8,128)(2,1)S(1)} %collective-permute-done.14) | copy-start | bytes 786436
  29.5 5.6 %collective-permute-start.6 = (bf16[256,1024]{0,1:T(8,128)(2,1)S(1)}, bf16[256,1024]{0,1:T(8,128)(2,1)S(1)}, u32[]{:S(2)}, u32[]{:S(2)}) collective-permute-start(bf16[256,1024]{0,1:T(8,128)(2,1)S(1)} %fusion.18), channel_id=1, source_target_pairs={{0,1},{1,0},{2,3},{3,2},{4,5},{5,4},{6,7},{7,6},{8,9},{9,8},{10,11... | collective-permute-start | bytes 1572872 | tf_op jit(solution)/shard_map/ppermute | solution.py:86
  30.1 6.6 %collective-permute-start.5 = (bf16[256,1024]{0,1:T(8,128)(2,1)S(1)}, bf16[256,1024]{0,1:T(8,128)(2,1)S(1)}, u32[]{:S(2)}, u32[]{:S(2)}) collective-permute-start(bf16[256,1024]{0,1:T(8,128)(2,1)S(1)} %fusion.17), channel_id=1, source_target_pairs={{0,1},{1,0},{2,3},{3,2},{4,5},{5,4},{6,7},{7,6},{8,9},{9,8},{10,11... | collective-permute-start | bytes 1572872 | tf_op jit(solution)/shard_map/ppermute | solution.py:86
  31.1 13.9 %collective-permute-start.26 = (bf16[256,2048]{1,0:T(8,128)(2,1)S(1)}, bf16[256,2048]{1,0:T(8,128)(2,1)S(1)}, u32[]{:S(2)}, u32[]{:S(2)}) collective-permute-start(bf16[256,2048]{1,0:T(8,128)(2,1)S(1)} %copy-done.6), channel_id=1, source_target_pairs={{0,0},{1,4},{4,1},{5,5},{10,10},{11,14},{14,11},{15,15},{16,16},{1... | collective-permute-start | bytes 3145736 | tf_op jit(solution)/shard_map/ppermute | solution.py:86
  31.8 24.7 %collective-permute-start.19 = (bf16[256,2048]{1,0:T(8,128)(2,1)S(1)}, bf16[256,2048]{1,0:T(8,128)(2,1)S(1)}, u32[]{:S(2)}, u32[]{:S(2)}) collective-permute-start(bf16[256,2048]{1,0:T(8,128)(2,1)S(1)} %copy-done.7), channel_id=1, source_target_pairs={{0,2},{1,3},{2,0},{3,1},{4,6},{5,7},{6,4},{7,5},{8,10},{9,11},{10,... | collective-permute-start | bytes 3145736 | tf_op jit(solution)/shard_map/ppermute | solution.py:86
  33.4 5.4 %collective-permute-start.16 = (bf16[256,1024]{0,1:T(8,128)(2,1)S(1)}, bf16[256,1024]{0,1:T(8,128)(2,1)S(1)}, u32[]{:S(2)}, u32[]{:S(2)}) collective-permute-start(bf16[256,1024]{0,1:T(8,128)(2,1)S(1)} %fusion.22), channel_id=1, source_target_pairs={{0,1},{1,0},{2,3},{3,2},{4,5},{5,4},{6,7},{7,6},{8,9},{9,8},{10,11... | collective-permute-start | bytes 1572872 | tf_op jit(solution)/shard_map/ppermute | solution.py:86
  35.1 5.5 %collective-permute-start.15 = (bf16[256,1024]{0,1:T(8,128)(2,1)S(1)}, bf16[256,1024]{0,1:T(8,128)(2,1)S(1)}, u32[]{:S(2)}, u32[]{:S(2)}) collective-permute-start(bf16[256,1024]{0,1:T(8,128)(2,1)S(1)} %fusion.21), channel_id=1, source_target_pairs={{0,1},{1,0},{2,3},{3,2},{4,5},{5,4},{6,7},{7,6},{8,9},{9,8},{10,11... | collective-permute-start | bytes 1572872 | tf_op jit(solution)/shard_map/ppermute | solution.py:86
  36.7 31.1 %collective-permute-start.2 = (bf16[256,1024]{0,1:T(8,128)(2,1)S(1)}, bf16[256,1024]{0,1:T(8,128)(2,1)S(1)}, u32[]{:S(2)}, u32[]{:S(2)}) collective-permute-start(bf16[256,1024]{0,1:T(8,128)(2,1)S(1)} %add_convert_fusion.1), channel_id=1, source_target_pairs={{0,2},{1,3},{2,0},{3,1},{4,6},{5,7},{6,4},{7,5},{8,10},{9,11},{10,... | collective-permute-start | bytes 1572872 | tf_op jit(solution)/shard_map/ppermute | solution.py:86
  38.8 50.2 %collective-permute-start.28 = (bf16[256,2048]{1,0:T(8,128)(2,1)S(1)}, bf16[256,2048]{1,0:T(8,128)(2,1)S(1)}, u32[]{:S(2)}, u32[]{:S(2)}) collective-permute-start(bf16[256,2048]{1,0:T(8,128)(2,1)S(1)} %copy-done.6), channel_id=1, source_target_pairs={{2,10},{3,14},{6,11},{7,15},{8,0},{9,4},{12,1},{13,5},{18,26},{19,... | collective-permute-start | bytes 3145736 | tf_op jit(solution)/shard_map/ppermute | solution.py:86
  40.6 38.4 %collective-permute-start.12 = (bf16[256,1024]{0,1:T(8,128)(2,1)S(1)}, bf16[256,1024]{0,1:T(8,128)(2,1)S(1)}, u32[]{:S(2)}, u32[]{:S(2)}) collective-permute-start(bf16[256,1024]{0,1:T(8,128)(2,1)S(1)} %fusion.11), channel_id=1, source_target_pairs={{0,2},{1,3},{2,0},{3,1},{4,6},{5,7},{6,4},{7,5},{8,10},{9,11},{10,... | collective-permute-start | bytes 1572872 | tf_op jit(solution)/shard_map/ppermute | solution.py:86
  44.9 45.6 %collective-permute-start.7 = (bf16[256,1024]{0,1:T(8,128)(2,1)S(1)}, bf16[256,1024]{0,1:T(8,128)(2,1)S(1)}, u32[]{:S(2)}, u32[]{:S(2)}) collective-permute-start(bf16[256,1024]{0,1:T(8,128)(2,1)S(1)} %fusion.13), channel_id=1, source_target_pairs={{0,2},{1,3},{2,0},{3,1},{4,6},{5,7},{6,4},{7,5},{8,10},{9,11},{10,... | collective-permute-start | bytes 1572872 | tf_op jit(solution)/shard_map/ppermute | solution.py:86
  56.6 70.0 %collective-permute-start.27 = (bf16[256,2048]{1,0:T(8,128)(2,1)S(1)}, bf16[256,2048]{1,0:T(8,128)(2,1)S(1)}, u32[]{:S(2)}, u32[]{:S(2)}) collective-permute-start(bf16[256,2048]{1,0:T(8,128)(2,1)S(1)} %collective-permute-done.26), channel_id=1, source_target_pairs={{0,2},{1,3},{2,0},{3,1},{4,6},{5,7},{6,4},{7,5},{8,10},{9,11},{10,... | collective-permute-start | bytes 3145736 | tf_op jit(solution)/shard_map/ppermute | solution.py:86
  67.8 60.0 %collective-permute-start.20 = (bf16[256,2048]{1,0:T(8,128)(2,1)S(1)}, bf16[256,2048]{1,0:T(8,128)(2,1)S(1)}, u32[]{:S(2)}, u32[]{:S(2)}) collective-permute-start(bf16[256,2048]{1,0:T(8,128)(2,1)S(1)} %collective-permute-done.19), channel_id=1, source_target_pairs={{2,2},{3,6},{6,3},{7,7},{8,8},{9,12},{12,9},{13,13},{18,18},{19,22... | collective-permute-start | bytes 3145736 | tf_op jit(solution)/shard_map/ppermute | solution.py:86
  79.0 44.9 %collective-permute-start.17 = (bf16[256,1024]{0,1:T(8,128)(2,1)S(1)}, bf16[256,1024]{0,1:T(8,128)(2,1)S(1)}, u32[]{:S(2)}, u32[]{:S(2)}) collective-permute-start(bf16[256,1024]{0,1:T(8,128)(2,1)S(1)} %fusion.9), channel_id=1, source_target_pairs={{0,2},{1,3},{2,0},{3,1},{4,6},{5,7},{6,4},{7,5},{8,10},{9,11},{10,... | collective-permute-start | bytes 1572872 | tf_op jit(solution)/shard_map/ppermute | solution.py:86
  89.0 58.7 %collective-permute-start.22 = (bf16[256,2048]{1,0:T(8,128)(2,1)S(1)}, bf16[256,2048]{1,0:T(8,128)(2,1)S(1)}, u32[]{:S(2)}, u32[]{:S(2)}) collective-permute-start(bf16[256,2048]{1,0:T(8,128)(2,1)S(1)} %collective-permute-done.19), channel_id=1, source_target_pairs={{0,8},{1,12},{4,9},{5,13},{10,2},{11,6},{14,3},{15,7},{16,24},{17,... | collective-permute-start | bytes 3145736 | tf_op jit(solution)/shard_map/ppermute | solution.py:86
  90.6 55.9 %collective-permute-start.29 = (bf16[256,2048]{1,0:T(8,128)(2,1)S(1)}, bf16[256,2048]{1,0:T(8,128)(2,1)S(1)}, u32[]{:S(2)}, u32[]{:S(2)}) collective-permute-start(bf16[256,2048]{1,0:T(8,128)(2,1)S(1)} %collective-permute-done.28), channel_id=1, source_target_pairs={{0,2},{1,3},{2,0},{3,1},{4,6},{5,7},{6,4},{7,5},{8,10},{9,11},{10,... | collective-permute-start | bytes 3145736 | tf_op jit(solution)/shard_map/ppermute | solution.py:86
  124.0 46.5 %collective-permute-start.3 = (bf16[256,1024]{0,1:T(8,128)(2,1)S(1)}, bf16[256,1024]{0,1:T(8,128)(2,1)S(1)}, u32[]{:S(2)}, u32[]{:S(2)}) collective-permute-start(bf16[256,1024]{0,1:T(8,128)(2,1)S(1)} %add_convert_fusion), channel_id=1, source_target_pairs={{16,0},{17,1},{18,2},{19,3},{20,4},{21,5},{22,6},{23,7},{24,8},{25... | collective-permute-start | bytes 1572872 | tf_op jit(solution)/shard_map/ppermute | solution.py:138
  126.5 66.2 %collective-permute-start.13 = (bf16[256,1024]{0,1:T(8,128)(2,1)S(1)}, bf16[256,1024]{0,1:T(8,128)(2,1)S(1)}, u32[]{:S(2)}, u32[]{:S(2)}) collective-permute-start(bf16[256,1024]{0,1:T(8,128)(2,1)S(1)} %fusion.12), channel_id=1, source_target_pairs={{16,0},{17,1},{18,2},{19,3},{20,4},{21,5},{22,6},{23,7},{24,8},{25... | collective-permute-start | bytes 1572872 | tf_op jit(solution)/shard_map/ppermute | solution.py:138
  127.8 41.1 %collective-permute-start.21 = (bf16[256,2048]{1,0:T(8,128)(2,1)S(1)}, bf16[256,2048]{1,0:T(8,128)(2,1)S(1)}, u32[]{:S(2)}, u32[]{:S(2)}) collective-permute-start(bf16[256,2048]{1,0:T(8,128)(2,1)S(1)} %collective-permute-done.20), channel_id=1, source_target_pairs={{0,2},{1,3},{2,0},{3,1},{4,6},{5,7},{6,4},{7,5},{8,10},{9,11},{10,... | collective-permute-start | bytes 3145736 | tf_op jit(solution)/shard_map/ppermute | solution.py:86
  146.4 47.0 %collective-permute-start.8 = (bf16[256,1024]{0,1:T(8,128)(2,1)S(1)}, bf16[256,1024]{0,1:T(8,128)(2,1)S(1)}, u32[]{:S(2)}, u32[]{:S(2)}) collective-permute-start(bf16[256,1024]{0,1:T(8,128)(2,1)S(1)} %fusion.14), channel_id=1, source_target_pairs={{16,0},{17,1},{18,2},{19,3},{20,4},{21,5},{22,6},{23,7},{24,8},{25... | collective-permute-start | bytes 1572872 | tf_op jit(solution)/shard_map/ppermute | solution.py:138
  147.7 43.6 %collective-permute-start.23 = (bf16[256,2048]{1,0:T(8,128)(2,1)S(1)}, bf16[256,2048]{1,0:T(8,128)(2,1)S(1)}, u32[]{:S(2)}, u32[]{:S(2)}) collective-permute-start(bf16[256,2048]{1,0:T(8,128)(2,1)S(1)} %collective-permute-done.22), channel_id=1, source_target_pairs={{0,2},{1,3},{2,0},{3,1},{4,6},{5,7},{6,4},{7,5},{8,10},{9,11},{10,... | collective-permute-start | bytes 3145736 | tf_op jit(solution)/shard_map/ppermute | solution.py:86
  168.9 36.3 %collective-permute-start.18 = (bf16[256,1024]{0,1:T(8,128)(2,1)}, bf16[256,1024]{0,1:T(8,128)(2,1)}, u32[]{:S(2)}, u32[]{:S(2)}) collective-permute-start(bf16[256,1024]{0,1:T(8,128)(2,1)} %fusion.10), channel_id=1, source_target_pairs={{16,0},{17,1},{18,2},{19,3},{20,4},{21,5},{22,6},{23,7},{24,8},{25... | collective-permute-start | bytes 1572872 | tf_op jit(solution)/shard_map/ppermute | solution.py:138
  170.5 23.8 %copy-start.8 = (bf16[256,1024]{0,1:T(8,128)(2,1)}, bf16[256,1024]{0,1:T(8,128)(2,1)S(1)}, u32[]{:S(2)}) copy-start(bf16[256,1024]{0,1:T(8,128)(2,1)S(1)} %collective-permute-done.3) | copy-start | bytes 1572868
  170.5 42.4 %collective-permute-start.30 = (bf16[256,2048]{1,0:T(8,128)(2,1)}, bf16[256,2048]{1,0:T(8,128)(2,1)}, u32[]{:S(2)}, u32[]{:S(2)}) collective-permute-start(bf16[256,2048]{1,0:T(8,128)(2,1)} %broadcast_select_fusion.1.refs_0_), channel_id=1, source_target_pairs={{0,1},{1,0},{2,3},{3,2},{4,5},{5,4},{6,7},{7,6},{8,9},{9,8},{10,11... | collective-permute-start | bytes 3145736 | tf_op jit(solution)/shard_map/ppermute | solution.py:86
  191.4 21.5 %collective-permute-start.31 = (bf16[256,2048]{1,0:T(8,128)(2,1)}, bf16[256,2048]{1,0:T(8,128)(2,1)}, u32[]{:S(2)}, u32[]{:S(2)}) collective-permute-start(bf16[256,2048]{1,0:T(8,128)(2,1)} %broadcast_select_fusion.refs_1_), channel_id=1, source_target_pairs={{0,1},{1,0},{2,3},{3,2},{4,5},{5,4},{6,7},{7,6},{8,9},{9,8},{10,11... | collective-permute-start | bytes 3145736 | tf_op jit(solution)/shard_map/ppermute | solution.py:86
  192.7 0.8 copy-start.9
  192.7 29.2 %collective-permute-start.24 = (bf16[256,2048]{1,0:T(8,128)(2,1)S(1)}, bf16[256,2048]{1,0:T(8,128)(2,1)}, u32[]{:S(2)}, u32[]{:S(2)}) collective-permute-start(bf16[256,2048]{1,0:T(8,128)(2,1)S(1)} %broadcast_select_fusion.3.refs_0_), channel_id=1, source_target_pairs={{0,1},{1,0},{2,3},{3,2},{4,5},{5,4},{6,7},{7,6},{8,9},{9,8},{10,11... | collective-permute-start | bytes 3145736 | tf_op jit(solution)/shard_map/ppermute | solution.py:86
  193.5 0.8 copy-start.10
  194.3 27.7 %collective-permute-start.25 = (bf16[256,2048]{1,0:T(8,128)(2,1)S(1)}, bf16[256,2048]{1,0:T(8,128)(2,1)}, u32[]{:S(2)}, u32[]{:S(2)}) collective-permute-start(bf16[256,2048]{1,0:T(8,128)(2,1)S(1)} %broadcast_select_fusion.2.refs_1_), channel_id=1, source_target_pairs={{0,1},{1,0},{2,3},{3,2},{4,5},{5,4},{6,7},{7,6},{8,9},{9,8},{10,11... | collective-permute-start | bytes 3145736 | tf_op jit(solution)/shard_map/ppermute | solution.py:86
  230.7 2.0 copy-start

commit v2 on v1

v2 whole, which is shorter than its diff:
```python
import jax
import jax.numpy as jnp
from jax import lax
from jax.experimental import pallas as pl
from jax.experimental.pallas import tpu as pltpu
from jax.sharding import PartitionSpec as P

BLOCK = 128
TILE = 512
RUNS = 2
MIB = 1024 * 1024


def weight_grad_kernel(picks, *refs):
    lefts, grads_ref = refs[:4], refs[4]
    mantissa_ref, scale_ref, turned = refs[-3:]

    @pl.when(pl.program_id(0) == 0)
    def _():
        for i in range(4):
            turned[i] = grads_ref[picks[i]].T

    top = total = None
    for i, left in enumerate(lefts):
        part = jnp.dot(turned[i], left[...], preferred_element_type=jnp.float32)
        total = part if total is None else total + part
        top = jnp.abs(part) if top is None else jnp.maximum(top, jnp.abs(part))
    columns, rows = top.shape
    blocks = columns // BLOCK
    scale = jnp.max(top.reshape(blocks, BLOCK, rows), axis=1) + 1e-6
    scale_ref[...] = scale
    inverse = 1.0 / scale
    scaled = [
        (total[b * BLOCK : (b + 1) * BLOCK] * inverse[b : b + 1]).astype(jnp.bfloat16) for b in range(blocks)
    ]
    half = blocks // 2
    mantissa_ref[:, 0, :] = jnp.concatenate(scaled[:half], axis=0).T
    mantissa_ref[:, 1, :] = jnp.concatenate(scaled[half:], axis=0).T


def weight_grad(picks, lefts, grads, into, row_total):
    columns = grads.shape[2]
    tokens, rows = lefts[0].shape
    in_specs = [pl.BlockSpec((tokens, TILE), lambda i, picks: (0, i)) for _ in lefts]
    in_specs.append(pl.BlockSpec(grads.shape, lambda i, picks: (0, 0, 0)))
    operands = [*lefts, grads]
    aliases = {}
    for n, held in enumerate(into):
        in_specs.append(pl.BlockSpec(memory_space=pl.ANY))
        operands.append(held)
        aliases[len(operands)] = n
    return pl.pallas_call(
        weight_grad_kernel,
        grid_spec=pltpu.PrefetchScalarGridSpec(
            num_scalar_prefetch=1,
            grid=(rows // TILE,),
            in_specs=in_specs,
            out_specs=[
                pl.BlockSpec((TILE, 2, columns // 2), lambda i, picks: (picks[4] + i, 0, 0)),
                pl.BlockSpec((columns // BLOCK, TILE), lambda i, picks: (0, picks[4] + i)),
            ],
            scratch_shapes=[pltpu.VMEM((4, columns, tokens), jnp.bfloat16)],
        ),
        out_shape=[
            jax.ShapeDtypeStruct((row_total, 2, columns // 2), jnp.bfloat16),
            jax.ShapeDtypeStruct((columns // BLOCK, row_total), jnp.float32),
        ],
        input_output_aliases=aliases,
        compiler_params=pltpu.CompilerParams(vmem_limit_bytes=32 * MIB),
        cost_estimate=pl.CostEstimate(
            flops=2 * 4 * tokens * rows * columns, bytes_accessed=2 * rows * (4 * tokens + columns), transcendentals=0
        ),
    )(picks, *operands)


def placed_kernel(group, *refs):
    terms, out_ref = refs[: len(refs) - 2], refs[-1]
    if len(terms) == 1:
        out_ref[...] = terms[0][...]
    else:
        out_ref[...] = (terms[0][...].astype(jnp.float32) + terms[1][...].astype(jnp.float32)).astype(jnp.bfloat16)


def first_placed_kernel(group, *refs):
    placed_kernel(group, *refs[:-1], None, refs[-1])


def placed(group, terms, into, groups):
    tokens, width = terms[0].shape
    in_specs = [pl.BlockSpec((tokens, width), lambda i, group: (0, 0)) for _ in terms]
    operands = list(terms)
    aliases = {}
    if into is not None:
        in_specs.append(pl.BlockSpec(memory_space=pl.ANY))
        operands.append(into)
        aliases[len(operands)] = 0
    return pl.pallas_call(
        placed_kernel if into is not None else first_placed_kernel,
        grid_spec=pltpu.PrefetchScalarGridSpec(
            num_scalar_prefetch=1,
            grid=(1,),
            in_specs=in_specs,
            out_specs=pl.BlockSpec((tokens, width), lambda i, group: (group[0], 0)),
        ),
        out_shape=jax.ShapeDtypeStruct((groups * tokens, width), jnp.bfloat16),
        input_output_aliases=aliases,
        cost_estimate=pl.CostEstimate(flops=tokens * width, bytes_accessed=6 * tokens * width, transcendentals=0),
    )(jnp.reshape(group, (1,)).astype(jnp.int32), *operands)


def on_device(layer_input, kv_cotangent, kv_weight):
    n_pipe, n_dp, n_mp = (lax.axis_size(a) for a in ("pipe", "dp", "mp"))
    p, m = lax.axis_index("dp"), lax.axis_index("mp")
    features = layer_input[0]
    tokens, width = features.shape
    columns = 2 * kv_cotangent.shape[3]
    rows = kv_weight.shape[1]
    share = rows // n_mp

    def move(x, where):
        pairs = []
        for s in range(n_pipe):
            for i in range(n_dp):
                for j in range(n_mp):
                    to = where(s, i, j)
                    if to is not None:
                        pairs.append(((s * n_dp + i) * n_mp + j, (to[0] * n_dp + to[1]) * n_mp + to[2]))
        return lax.ppermute(x, ("pipe", "dp", "mp"), pairs)

    def across(x):
        return move(x, lambda s, i, j: (s, i, j ^ 2))

    def other_core(x):
        return move(x, lambda s, i, j: (s, i, j ^ 1))

    def near(x):
        return move(x, lambda s, i, j: (s, 2 * (i // 2) + j % 2, 2 * (j // 2) + i % 2))

    def far(x):
        return move(x, lambda s, i, j: (s, 2 * (1 - i // 2) + j % 2, 2 * (j // 2) + i % 2))

    own_grad = kv_cotangent[0].reshape(tokens, columns)
    grads = [own_grad] + [move(own_grad, lambda s, i, j, k=k: (s, i ^ k, j)) for k in range(1, n_dp)]

    own_side = (m // 2) == (p // 2)
    half = width // 2
    run = half // RUNS
    direct, crossed = [], []
    for n in range(RUNS):
        here = features[:, n * run : (n + 1) * run]
        there = across(features[:, half + n * run : half + (n + 1) * run])
        a = near(jnp.where(own_side, here, there))
        b = far(jnp.where(own_side, there, here))
        direct.append((a, b, other_core(a), other_core(b)))
        a, b = across(a), across(b)
        crossed.append((a, b, other_core(a), other_core(b)))

    quarters = kv_weight[0].reshape(n_mp, share, columns)
    w = [lax.dynamic_index_in_dim(quarters, m ^ k, 0, keepdims=False) for k in range(n_mp)]

    def times(g, k):
        return lax.dot_general(g, w[k], (((1,), (1,)), ((), ())), preferred_element_type=jnp.float32)

    def behind(x):
        return move(x, lambda s, i, j: (s - 1, i, j) if s else None)

    total = None
    for k, g in enumerate(grads):
        to_other = other_core(times(g, 3).astype(jnp.bfloat16))
        to_own = other_core(times(g, 1).astype(jnp.bfloat16))
        for_across = (times(g, 2) + to_other.astype(jnp.float32)).astype(jnp.bfloat16)
        mine = times(g, 0) + to_own.astype(jnp.float32)
        if k < n_dp // 2:
            terms = (
                behind(mine.astype(jnp.bfloat16)),
                move(for_across, lambda s, i, j: (s - 1, i, j ^ 2) if s else None),
            )
        else:
            summed = mine + move(for_across, lambda s, i, j: (s, i, j ^ 2) if s else None).astype(jnp.float32)
            terms = (behind(summed.astype(jnp.bfloat16)),)
        total = placed(p ^ k, terms, total, n_dp)

    grads = jnp.stack(grads)
    same = (m ^ p) & 1
    out = ()
    for n in range(RUNS):
        for four, first in ((direct[n], (m // 2) != (p // 2)), (crossed[n], own_side)):
            at = (first.astype(jnp.int32) * half + n * run) // TILE
            picks = jnp.stack([same, 2 + same, 1 - same, 3 - same, at]).astype(jnp.int32)
            out = weight_grad(picks, four, grads, out, rows)
    mantissa, scale = out
    scale = scale.T.reshape(rows, 2, columns // (2 * BLOCK))
    return (total[None], mantissa[None], scale[None])


def solution(mesh):
    in_specs = (P("pipe", "dp", "mp"), P("pipe", "dp", None, "mp"), P("pipe", "dp", None, "mp"))
    out_specs = (
        P("pipe", None, ("dp", "mp")),
        P("pipe", "dp", None, "mp"),
        P("pipe", "dp", None, "mp"),
    )
    return jax.shard_map(on_device, mesh=mesh, in_specs=in_specs, out_specs=out_specs, check_vma=False)
```

time: 242 us -> 178 us (0.74)
  waiting for transfers between devices: 120 us -> 72.7 us
  local copies, waits for them, and re-layouts: 38.7 us -> 17.7 us
  Pallas kernels: 17.8 us -> 28.5 us
  other arithmetic: 4.93 us -> 1.42 us
    ppermute x32 -> x37, waiting for transfers between devices: 120 us -> 72.7 us  [move(): return lax.ppermute(x, ('pipe', 'dp', 'mp'), pairs)]
    broadcast_in_dim x5 -> x0, local copies, waits for them, and re-layouts: 9.82 us -> none  [on_device(): return (total[None], mantissa[None], scale[None])]
    pallas_call x0 -> x4, Pallas kernels: none -> 7.96 us  [placed(): pl.pallas_call(placed_kernel if into is not None else first_placed_kernel...]
    dynamic_update_slice x4 -> x0, local copies, waits for them, and re-layouts: 7.47 us -> none  [on_device(): total = lax.dynamic_update_slice_in_dim(total, arrived, (p ^ k) * tokens, 0)]
    another operation x2 -> x1, local copies, waits for them, and re-layouts: 7.56 us -> 0.68 us  [on_device(): return (total[None], mantissa[None], scale[None])]
    pallas_call x2 -> x4, Pallas kernels: 17.8 us -> 20.5 us  [weight_grad(): pl.pallas_call(weight_grad_kernel, grid_spec=pltpu.PrefetchScalarGridSpec...]
    unnamed x23 -> x41, local copies, waits for them, and re-layouts: 4.58 us -> 7.19 us
    ppermute x32 -> x37, starting transfers between devices: 42.4 us -> 42.1 us  [move(): return lax.ppermute(x, ('pipe', 'dp', 'mp'), pairs)]
  transfers between devices with their start and end apart: 32 -> 37, of which waited for: 9 -> 9; matrix products, arithmetic and copies ran while one was open for 20% -> 14% of each run, Pallas kernels for 4% -> 13%
where the time goes in v2:
time: 178 us; the launch traced here: 177 us
  waiting for transfers between devices  72.7 us (41%)
  starting transfers between devices  42.1 us (24%)
  Pallas kernels  28.5 us (16%)
  local copies, waits for them, and re-layouts  17.7 us (10%)
  matrix products  13.6 us (8%)
    ppermute x37, waiting for transfers between devices, move(): return lax.ppermute(x, ('pipe', 'dp', 'mp'), pairs)  72.7 us
    ppermute x37, starting transfers between devices, move(): return lax.ppermute(x, ('pipe', 'dp', 'mp'), pairs)  42.1 us
    pallas_call x4, Pallas kernels, weight_grad(): pl.pallas_call(weight_grad_kernel, grid_spec=pltpu.PrefetchScalarGridSpec...  20.5 us
    dot_general x16, matrix products, times(): lax.dot_general(g, w[k], (((1,), (1,)), ((), ())), preferred_element_type...  13.6 us
    pallas_call x4, Pallas kernels, placed(): pl.pallas_call(placed_kernel if into is not None else first_placed_kernel...  7.96 us
    another operation x1, local copies, waits for them, and re-layouts, on_device(): quarters = kv_weight[0].reshape(n_mp, share, columns)  7.58 us
    unnamed x41, local copies, waits for them, and re-layouts  7.19 us
  transfers between devices with their start and end apart: 37, of which 9 were waited for; matrix products, arithmetic and copies ran while one was open for 14% of the time, Pallas kernels for 13%

profile of v2, /device:TPU:0, one launch (start us, length us, event | category | flops | bytes accessed | tf_op | source)
XLA Modules:
  0.0 177.1 jit_solution(2978872377521747596)
XLA Ops:
  0.6 1.0 copy.47
  1.6 3.1 %collective-permute-start.10 = (bf16[256,512]{1,0:T(8,128)(2,1)S(1)}, bf16[256,512]{1,0:T(8,128)(2,1)S(1)}, u32[]{:S(2)}, u32[]{:S(2)}) collective-permute-start(bf16[256,512]{1,0:T(8,128)(2,1)S(1)} %bitcast.147), channel_id=1, source_target_pairs={{0,4},{1,5},{2,6},{3,7},{4,0},{5,1},{6,2},{7,3},{8,12},{9,13},{10,... | collective-permute-start | bytes 786440 | tf_op jit(solution)/shard_map/ppermute | solution.py:128
  4.7 2.6 %collective-permute-start.5 = (bf16[256,512]{1,0:T(8,128)(2,1)S(1)}, bf16[256,512]{1,0:T(8,128)(2,1)S(1)}, u32[]{:S(2)}, u32[]{:S(2)}) collective-permute-start(bf16[256,512]{1,0:T(8,128)(2,1)S(1)} %bitcast.148), channel_id=1, source_target_pairs={{0,8},{1,9},{2,10},{3,11},{4,12},{5,13},{6,14},{7,15},{8,0},{9,1},... | collective-permute-start | bytes 786440 | tf_op jit(solution)/shard_map/ppermute | solution.py:128
  7.3 1.1 slice.19
  8.4 1.8 %collective-permute-start.28 = (bf16[256,1024]{1,0:T(8,128)(2,1)S(1)}, bf16[256,1024]{1,0:T(8,128)(2,1)S(1)}, u32[]{:S(2)}, u32[]{:S(2)}) collective-permute-start(bf16[256,1024]{1,0:T(8,128)(2,1)S(1)} %slice.19), channel_id=1, source_target_pairs={{0,2},{1,3},{2,0},{3,1},{4,6},{5,7},{6,4},{7,5},{8,10},{9,11},{10,... | collective-permute-start | bytes 1572872 | tf_op jit(solution)/shard_map/ppermute | solution.py:128
  10.2 7.6 %reshape_squeeze.6 = bf16[4,1024,512]{2,1,0:T(8,128)(2,1)} reshape(bf16[1,4096,2,256]{3,2,1,0:T(2,128)(2,1)} %param.5) | data formatting | bytes 8388608 | tf_op jit(solution)/shard_map/reshape;squeeze | solution.py:158
  17.8 2.5 %fusion.21 = bf16[256,1024]{1,0:T(8,128)(2,1)} fusion(bf16[256,512]{1,0:T(8,128)(2,1)S(1)} %bitcast.150, bf16[4,1024,512]{2,1,0:T(8,128)(2,1)} %reshape_squeeze.6, s32[]{:T(128)S(6)} %select_n.60), kind=kOutput, calls=%fused_computation.37 | convolution fusion | flops 268697600 | bytes 1835012 | tf_op jit(solution)/shard_map/dot_general | solution.py:162
  20.3 1.8 %fusion.20 = bf16[256,1024]{1,0:T(8,128)(2,1)S(1)} fusion(bf16[256,512]{1,0:T(8,128)(2,1)S(1)} %bitcast.151, bf16[4,1024,512]{2,1,0:T(8,128)(2,1)} %reshape_squeeze.6, s32[]{:T(128)S(6)} %select_n.58), kind=kOutput, calls=%fused_computation.36 | convolution fusion | flops 268697600 | bytes 1835012 | tf_op jit(solution)/shard_map/dot_general | solution.py:162
  22.7 1.7 fusion.19
  24.4 1.8 %fusion.18 = bf16[256,1024]{1,0:T(8,128)(2,1)S(1)} fusion(bf16[256,512]{1,0:T(8,128)(2,1)S(1)} %collective-permute-done.10, bf16[4,1024,512]{2,1,0:T(8,128)(2,1)} %reshape_squeeze.6, s32[]{:T(128)S(6)} %select_n.58), kind=kOutput, calls=%fused_computation.34 | convolution fusion | flops 268697600 | bytes 1835012 | tf_op jit(solution)/shard_map/dot_general | solution.py:162
  31.8 4.1 %collective-permute-start.31 = (bf16[256,1024]{1,0:T(8,128)(2,1)S(1)}, bf16[256,1024]{1,0:T(8,128)(2,1)S(1)}, u32[]{:S(2)}, u32[]{:S(2)}) collective-permute-start(bf16[256,1024]{1,0:T(8,128)(2,1)S(1)} %get-tuple-element.19), channel_id=1, source_target_pairs={{0,8},{1,12},{2,10},{3,14},{4,9},{5,13},{6,11},{7,15},{8,0},{9,4},... | collective-permute-start | bytes 1572872 | tf_op jit(solution)/shard_map/ppermute | solution.py:128
  36.0 1.5 collective-permute-start.19
  38.0 1.3 collective-permute-start.18
  39.3 1.3 collective-permute-start.16
  41.1 1.3 collective-permute-start.14
  42.9 16.2 %collective-permute-done.31.refs_1_ = bf16[256,1024]{1,0:T(8,128)(2,1)S(1)} collective-permute-done((bf16[256,1024]{1,0:T(8,128)(2,1)S(1)}, bf16[256,1024]{1,0:T(8,128)(2,1)S(1)}, u32[]{:S(2)}, u32[]{:S(2)}) %collective-permute-start.31) | collective-permute-done | bytes 524320 | tf_op jit(solution)/shard_map/ppermute | solution.py:128
  59.0 1.3 collective-permute-start.12
  62.4 1.9 %collective-permute-done.16.refs_0_ = bf16[256,1024]{1,0:T(8,128)(2,1)S(1)} collective-permute-done((bf16[256,1024]{1,0:T(8,128)(2,1)S(1)}, bf16[256,1024]{1,0:T(8,128)(2,1)S(1)}, u32[]{:S(2)}, u32[]{:S(2)}) %collective-permute-start.16) | collective-permute-done | bytes 524320 | tf_op jit(solution)/shard_map/ppermute | solution.py:128
  64.3 3.4 %collective-permute-start.35 = (bf16[256,1024]{1,0:T(8,128)(2,1)S(1)}, bf16[256,1024]{1,0:T(8,128)(2,1)S(1)}, u32[]{:S(2)}, u32[]{:S(2)}) collective-permute-start(bf16[256,1024]{1,0:T(8,128)(2,1)S(1)} %collective-permute-done.29.refs_0_), channel_id=1, source_target_pairs={{0,1},{1,0},{2,3},{3,2},{4,5},{5,4},{6,7},{7,6},{8,9},{9,8},{10,11... | collective-permute-start | bytes 1572872 | tf_op jit(solution)/shard_map/ppermute | solution.py:128
  67.7 8.9 %collective-permute-done.14.refs_1_ = bf16[256,1024]{1,0:T(8,128)(2,1)} collective-permute-done((bf16[256,1024]{1,0:T(8,128)(2,1)S(1)}, bf16[256,1024]{1,0:T(8,128)(2,1)}, u32[]{:S(2)}, u32[]{:S(2)}) %collective-permute-start.14) | collective-permute-done | bytes 524320 | tf_op jit(solution)/shard_map/ppermute | solution.py:128
  76.6 3.0 %collective-permute-start.36 = (bf16[256,1024]{1,0:T(8,128)(2,1)S(1)}, bf16[256,1024]{1,0:T(8,128)(2,1)S(1)}, u32[]{:S(2)}, u32[]{:S(2)}) collective-permute-start(bf16[256,1024]{1,0:T(8,128)(2,1)S(1)} %collective-permute-done.31.refs_1_), channel_id=1, source_target_pairs={{0,1},{1,0},{2,3},{3,2},{4,5},{5,4},{6,7},{7,6},{8,9},{9,8},{10,11... | collective-permute-start | bytes 1572872 | tf_op jit(solution)/shard_map/ppermute | solution.py:128
  79.7 7.1 %collective-permute-done.12.refs_0_ = bf16[256,1024]{1,0:T(8,128)(2,1)S(1)} collective-permute-done((bf16[256,1024]{1,0:T(8,128)(2,1)S(1)}, bf16[256,1024]{1,0:T(8,128)(2,1)S(1)}, u32[]{:S(2)}, u32[]{:S(2)}) %collective-permute-start.12) | collective-permute-done | bytes 524320 | tf_op jit(solution)/shard_map/ppermute | solution.py:128
  87.5 1.3 collective-permute-start.22
  88.8 1.5 collective-permute-start.30
  91.4 1.3 collective-permute-start.9
  93.2 8.7 %collective-permute-done.30.refs_0_ = bf16[256,1024]{1,0:T(8,128)(2,1)S(1)} collective-permute-done((bf16[256,1024]{1,0:T(8,128)(2,1)S(1)}, bf16[256,1024]{1,0:T(8,128)(2,1)S(1)}, u32[]{:S(2)}, u32[]{:S(2)}) %collective-permute-start.30) | collective-permute-done | bytes 524320 | tf_op jit(solution)/shard_map/ppermute | solution.py:128
  102.0 1.5 collective-permute-start.4
  103.4 9.8 %collective-permute-done.32.refs_1_ = bf16[256,1024]{1,0:T(8,128)(2,1)S(1)} collective-permute-done((bf16[256,1024]{1,0:T(8,128)(2,1)S(1)}, bf16[256,1024]{1,0:T(8,128)(2,1)S(1)}, u32[]{:S(2)}, u32[]{:S(2)}) %collective-permute-start.32) | collective-permute-done | bytes 524320 | tf_op jit(solution)/shard_map/ppermute | solution.py:128
  113.2 1.8 %collective-permute-start.33 = (bf16[256,1024]{1,0:T(8,128)(2,1)S(1)}, bf16[256,1024]{1,0:T(8,128)(2,1)S(1)}, u32[]{:S(2)}, u32[]{:S(2)}) collective-permute-start(bf16[256,1024]{1,0:T(8,128)(2,1)S(1)} %collective-permute-done.30.refs_0_), channel_id=1, source_target_pairs={{0,1},{1,0},{2,3},{3,2},{4,5},{5,4},{6,7},{7,6},{8,9},{9,8},{10,11... | collective-permute-start | bytes 1572872 | tf_op jit(solution)/shard_map/ppermute | solution.py:128
  115.0 1.5 collective-permute-start.21
  117.5 2.1 %collective-permute-start.26 = (bf16[256,1024]{1,0:T(8,128)(2,1)S(1)}, bf16[256,1024]{1,0:T(8,128)(2,1)}, u32[]{:S(2)}, u32[]{:S(2)}) collective-permute-start(bf16[256,1024]{1,0:T(8,128)(2,1)S(1)} %collective-permute-done.20.refs_0_), channel_id=1, source_target_pairs={{0,1},{1,0},{2,3},{3,2},{4,5},{5,4},{6,7},{7,6},{8,9},{9,8},{10,11... | collective-permute-start | bytes 1572872 | tf_op jit(solution)/shard_map/ppermute | solution.py:128
  120.5 9.4 %collective-permute-done.21.refs_0_ = bf16[256,1024]{1,0:T(8,128)(2,1)} collective-permute-done((bf16[256,1024]{1,0:T(8,128)(2,1)S(1)}, bf16[256,1024]{1,0:T(8,128)(2,1)}, u32[]{:S(2)}, u32[]{:S(2)}) %collective-permute-start.21) | collective-permute-done | bytes 524320 | tf_op jit(solution)/shard_map/ppermute | solution.py:128
  129.9 10.3 %collective-permute-done.23.refs_1_ = bf16[256,1024]{1,0:T(8,128)(2,1)} collective-permute-done((bf16[256,1024]{1,0:T(8,128)(2,1)S(1)}, bf16[256,1024]{1,0:T(8,128)(2,1)}, u32[]{:S(2)}, u32[]{:S(2)}) %collective-permute-start.23) | collective-permute-done | bytes 524320 | tf_op jit(solution)/shard_map/ppermute | solution.py:128
  140.3 0.9 stack_reshape_squeeze.3
  141.5 1.2 pad_maximum_fusion.refs_4_
  142.7 2.1 %shard_map.58.refs_2_ = bf16[1024,1024]{1,0:T(8,128)(2,1)} custom-call(s32[1]{0:T(128)} %bitcast.19.group, bf16[256,1024]{1,0:T(8,128)(2,1)} %copy-done.18, bf16[256,1024]{1,0:T(8,128)(2,1)} %copy-done.17), custom_call_target="tpu_custom_call" | custom-call | flops 262144 | bytes 1572864 | tf_op jit(solution)/shard_map/pallas_call | solution.py:97
  144.9 2.1 %shard_map.59.refs_1_ = bf16[1024,1024]{1,0:T(8,128)(2,1)} custom-call(s32[1]{0:T(128)} %bitcast.14.group, bf16[256,1024]{1,0:T(8,128)(2,1)} %copy-done.19, bf16[256,1024]{1,0:T(8,128)(2,1)} %collective-permute-done.14.refs_1_, bf16[1024,1024]{1,0:T(8,128)(2,1)} %shard_map.58.refs_2_), custom_call_target="tpu_custom_call", output_to_operand_aliasing={{}: (3, {})} | custom-call | flops 262144 | bytes 1572864 | tf_op jit(solution)/shard_map/pallas_call | solution.py:97
  147.0 1.0 copy-done.3
  148.0 1.0 copy-done.5
  149.1 1.0 copy-done.7
  150.1 1.0 copy-done.9
  151.1 4.4 %shard_map.62 = (bf16[4096,2,256]{2,1,0:T(2,128)(2,1)}, f32[4,4096]{1,0:T(4,128)S(1)}) custom-call(s32[5]{0:T(128)S(1)} %stack.75.picks, bf16[256,1024]{1,0:T(8,128)(2,1)S(1)} %copy-done.3, bf16[256,1024]{1,0:T(8,128)(2,1)S(1)} %copy-done.5, bf16[256,1024]{1,0:T(8,128)(2,1)S(1)} %copy-done.7, bf16[256,1024]{1,0:T(8,128)(2,1)S(1)} %copy-done.9, ...), custom_call_target="tpu_custom_call" | custom-call | flops 1073741824 | bytes 3145728 | tf_op jit(solution)/shard_map/pallas_call | solution.py:52
  155.6 1.9 %shard_map.60.refs_1_ = bf16[1024,1024]{1,0:T(8,128)(2,1)} custom-call(s32[1]{0:T(128)} %bitcast.9.group, bf16[256,1024]{1,0:T(8,128)(2,1)} %copy-done.15, bf16[1024,1024]{1,0:T(8,128)(2,1)} %shard_map.59.refs_1_), custom_call_target="tpu_custom_call", output_to_operand_aliasing={{}: (2, {})} | custom-call | flops 262144 | bytes 1572864 | tf_op jit(solution)/shard_map/pallas_call | solution.py:97
  157.4 1.9 %shard_map.61 = bf16[1024,1024]{1,0:T(8,128)(2,1)} custom-call(s32[1]{0:T(128)} %bitcast.group, bf16[256,1024]{1,0:T(8,128)(2,1)} %copy-done.16, bf16[1024,1024]{1,0:T(8,128)(2,1)} %shard_map.60.refs_1_), custom_call_target="tpu_custom_call", output_to_operand_aliasing={{}: (2, {})} | custom-call | flops 262144 | bytes 1572864 | tf_op jit(solution)/shard_map/pallas_call | solution.py:97
  159.3 1.0 copy-done.1
  160.4 5.3 %shard_map.63 = (bf16[4096,2,256]{2,1,0:T(2,128)(2,1)}, f32[4,4096]{1,0:T(4,128)S(1)}) custom-call(s32[5]{0:T(128)S(1)} %stack.73.picks, bf16[256,1024]{1,0:T(8,128)(2,1)S(1)} %collective-permute-done.30.refs_0_, bf16[256,1024]{1,0:T(8,128)(2,1)S(1)} %collective-permute-done.32.refs_1_, ...), custom_call_target="tpu_custom_call", output_to_operand_aliasing={{0}: (6, {}), {1}: (7, {})} | custom-call | flops 1073741824 | bytes 3145728 | tf_op jit(solution)/shard_map/pallas_call | solution.py:52
  165.6 5.3 %shard_map.64 = (bf16[4096,2,256]{2,1,0:T(2,128)(2,1)}, f32[4,4096]{1,0:T(4,128)S(1)}) custom-call(s32[5]{0:T(128)S(1)} %stack.71.picks, bf16[256,1024]{1,0:T(8,128)(2,1)S(1)} %collective-permute-done.20.refs_0_, bf16[256,1024]{1,0:T(8,128)(2,1)S(1)} %collective-permute-done.22.refs_1_, ...), custom_call_target="tpu_custom_call", output_to_operand_aliasing={{0}: (6, {}), {1}: (7, {})} | custom-call | flops 1073741824 | bytes 3145728 | tf_op jit(solution)/shard_map/pallas_call | solution.py:52
  171.0 5.5 %shard_map.65 = (bf16[4096,2,256]{2,1,0:T(2,128)(2,1)}, f32[4,4096]{1,0:T(4,128)S(1)}) custom-call(s32[5]{0:T(128)S(1)} %stack.65.picks, bf16[256,1024]{1,0:T(8,128)(2,1)} %collective-permute-done.21.refs_0_, bf16[256,1024]{1,0:T(8,128)(2,1)} %collective-permute-done.23.refs_1_, ...), custom_call_target="tpu_custom_call", output_to_operand_aliasing={{0}: (6, {}), {1}: (7, {})} | custom-call | flops 1073741824 | bytes 3145728 | tf_op jit(solution)/shard_map/pallas_call | solution.py:52
  (102 shorter events, 14.9 us)
Async XLA Ops:
  1.6 20.5 %collective-permute-start.10 = (bf16[256,512]{1,0:T(8,128)(2,1)S(1)}, bf16[256,512]{1,0:T(8,128)(2,1)S(1)}, u32[]{:S(2)}, u32[]{:S(2)}) collective-permute-start(bf16[256,512]{1,0:T(8,128)(2,1)S(1)} %bitcast.147), channel_id=1, source_target_pairs={{0,4},{1,5},{2,6},{3,7},{4,0},{5,1},{6,2},{7,3},{8,12},{9,13},{10,... | collective-permute-start | bytes 786440 | tf_op jit(solution)/shard_map/ppermute | solution.py:128
  4.7 21.5 %collective-permute-start.5 = (bf16[256,512]{1,0:T(8,128)(2,1)S(1)}, bf16[256,512]{1,0:T(8,128)(2,1)S(1)}, u32[]{:S(2)}, u32[]{:S(2)}) collective-permute-start(bf16[256,512]{1,0:T(8,128)(2,1)S(1)} %bitcast.148), channel_id=1, source_target_pairs={{0,8},{1,9},{2,10},{3,11},{4,12},{5,13},{6,14},{7,15},{8,0},{9,1},... | collective-permute-start | bytes 786440 | tf_op jit(solution)/shard_map/ppermute | solution.py:128
  7.3 20.0 %collective-permute-start = (bf16[256,512]{1,0:T(8,128)(2,1)S(1)}, bf16[256,512]{1,0:T(8,128)(2,1)S(1)}, u32[]{:S(2)}, u32[]{:S(2)}) collective-permute-start(bf16[256,512]{1,0:T(8,128)(2,1)S(1)} %bitcast.149), channel_id=1, source_target_pairs={{0,12},{1,13},{2,14},{3,15},{4,8},{5,9},{6,10},{7,11},{8,4},{9,5},... | collective-permute-start | bytes 786440 | tf_op jit(solution)/shard_map/ppermute | solution.py:128
  8.4 20.5 %collective-permute-start.28 = (bf16[256,1024]{1,0:T(8,128)(2,1)S(1)}, bf16[256,1024]{1,0:T(8,128)(2,1)S(1)}, u32[]{:S(2)}, u32[]{:S(2)}) collective-permute-start(bf16[256,1024]{1,0:T(8,128)(2,1)S(1)} %slice.19), channel_id=1, source_target_pairs={{0,2},{1,3},{2,0},{3,1},{4,6},{5,7},{6,4},{7,5},{8,10},{9,11},{10,... | collective-permute-start | bytes 1572872 | tf_op jit(solution)/shard_map/ppermute | solution.py:128
  20.2 8.7 %collective-permute-start.17 = (bf16[256,1024]{1,0:T(8,128)(2,1)}, bf16[256,1024]{1,0:T(8,128)(2,1)S(1)}, u32[]{:S(2)}, u32[]{:S(2)}) collective-permute-start(bf16[256,1024]{1,0:T(8,128)(2,1)} %fusion.21), channel_id=1, source_target_pairs={{0,1},{1,0},{2,3},{3,2},{4,5},{5,4},{6,7},{7,6},{8,9},{9,8},{10,11... | collective-permute-start | bytes 1572872 | tf_op jit(solution)/shard_map/ppermute | solution.py:128
  22.1 7.4 %collective-permute-start.15 = (bf16[256,1024]{1,0:T(8,128)(2,1)S(1)}, bf16[256,1024]{1,0:T(8,128)(2,1)S(1)}, u32[]{:S(2)}, u32[]{:S(2)}) collective-permute-start(bf16[256,1024]{1,0:T(8,128)(2,1)S(1)} %fusion.20), channel_id=1, source_target_pairs={{0,1},{1,0},{2,3},{3,2},{4,5},{5,4},{6,7},{7,6},{8,9},{9,8},{10,11... | collective-permute-start | bytes 1572872 | tf_op jit(solution)/shard_map/ppermute | solution.py:128
  26.3 64.6 %copy-start.11 = (bf16[256,512]{1,0:T(8,128)(2,1)}, bf16[256,512]{1,0:T(8,128)(2,1)S(1)}, u32[]{:S(2)}) copy-start(bf16[256,512]{1,0:T(8,128)(2,1)S(1)} %collective-permute-done.5) | copy-start | bytes 786436
  26.3 3.5 %collective-permute-start.13 = (bf16[256,1024]{1,0:T(8,128)(2,1)S(1)}, bf16[256,1024]{1,0:T(8,128)(2,1)S(1)}, u32[]{:S(2)}, u32[]{:S(2)}) collective-permute-start(bf16[256,1024]{1,0:T(8,128)(2,1)S(1)} %fusion.19), channel_id=1, source_target_pairs={{0,1},{1,0},{2,3},{3,2},{4,5},{5,4},{6,7},{7,6},{8,9},{9,8},{10,11... | collective-permute-start | bytes 1572872 | tf_op jit(solution)/shard_map/ppermute | solution.py:128
  27.3 65.4 %copy-start.12 = (bf16[256,512]{1,0:T(8,128)(2,1)}, bf16[256,512]{1,0:T(8,128)(2,1)S(1)}, u32[]{:S(2)}) copy-start(bf16[256,512]{1,0:T(8,128)(2,1)S(1)} %collective-permute-done) | copy-start | bytes 786436
  27.3 3.3 %collective-permute-start.11 = (bf16[256,1024]{1,0:T(8,128)(2,1)S(1)}, bf16[256,1024]{1,0:T(8,128)(2,1)S(1)}, u32[]{:S(2)}, u32[]{:S(2)}) collective-permute-start(bf16[256,1024]{1,0:T(8,128)(2,1)S(1)} %fusion.18), channel_id=1, source_target_pairs={{0,1},{1,0},{2,3},{3,2},{4,5},{5,4},{6,7},{7,6},{8,9},{9,8},{10,11... | collective-permute-start | bytes 1572872 | tf_op jit(solution)/shard_map/ppermute | solution.py:128
  28.9 3.0 %collective-permute-start.7 = (bf16[256,1024]{1,0:T(8,128)(2,1)S(1)}, bf16[256,1024]{1,0:T(8,128)(2,1)S(1)}, u32[]{:S(2)}, u32[]{:S(2)}) collective-permute-start(bf16[256,1024]{1,0:T(8,128)(2,1)S(1)} %fusion.17), channel_id=1, source_target_pairs={{0,1},{1,0},{2,3},{3,2},{4,5},{5,4},{6,7},{7,6},{8,9},{9,8},{10,11... | collective-permute-start | bytes 1572872 | tf_op jit(solution)/shard_map/ppermute | solution.py:128
  29.0 7.0 %collective-permute-start.6 = (bf16[256,1024]{1,0:T(8,128)(2,1)S(1)}, bf16[256,1024]{1,0:T(8,128)(2,1)S(1)}, u32[]{:S(2)}, u32[]{:S(2)}) collective-permute-start(bf16[256,1024]{1,0:T(8,128)(2,1)S(1)} %fusion.16), channel_id=1, source_target_pairs={{0,1},{1,0},{2,3},{3,2},{4,5},{5,4},{6,7},{7,6},{8,9},{9,8},{10,11... | collective-permute-start | bytes 1572872 | tf_op jit(solution)/shard_map/ppermute | solution.py:128
  29.6 8.4 %collective-permute-start.2 = (bf16[256,1024]{1,0:T(8,128)(2,1)S(1)}, bf16[256,1024]{1,0:T(8,128)(2,1)S(1)}, u32[]{:S(2)}, u32[]{:S(2)}) collective-permute-start(bf16[256,1024]{1,0:T(8,128)(2,1)S(1)} %fusion.15), channel_id=1, source_target_pairs={{0,1},{1,0},{2,3},{3,2},{4,5},{5,4},{6,7},{7,6},{8,9},{9,8},{10,11... | collective-permute-start | bytes 1572872 | tf_op jit(solution)/shard_map/ppermute | solution.py:128
  29.7 9.5 %collective-permute-start.1 = (bf16[256,1024]{1,0:T(8,128)(2,1)S(1)}, bf16[256,1024]{1,0:T(8,128)(2,1)S(1)}, u32[]{:S(2)}, u32[]{:S(2)}) collective-permute-start(bf16[256,1024]{1,0:T(8,128)(2,1)S(1)} %fusion.14), channel_id=1, source_target_pairs={{0,1},{1,0},{2,3},{3,2},{4,5},{5,4},{6,7},{7,6},{8,9},{9,8},{10,11... | collective-permute-start | bytes 1572872 | tf_op jit(solution)/shard_map/ppermute | solution.py:128
  30.6 10.4 %collective-permute-start.29 = (bf16[256,1024]{1,0:T(8,128)(2,1)S(1)}, bf16[256,1024]{1,0:T(8,128)(2,1)S(1)}, u32[]{:S(2)}, u32[]{:S(2)}) collective-permute-start(bf16[256,1024]{1,0:T(8,128)(2,1)S(1)} %get-tuple-element.20), channel_id=1, source_target_pairs={{0,0},{1,4},{2,2},{3,6},{4,1},{5,5},{6,3},{7,7},{8,8},{9,12},{10,1... | collective-permute-start | bytes 1572872 | tf_op jit(solution)/shard_map/ppermute | solution.py:128
  31.8 27.2 %collective-permute-start.31 = (bf16[256,1024]{1,0:T(8,128)(2,1)S(1)}, bf16[256,1024]{1,0:T(8,128)(2,1)S(1)}, u32[]{:S(2)}, u32[]{:S(2)}) collective-permute-start(bf16[256,1024]{1,0:T(8,128)(2,1)S(1)} %get-tuple-element.19), channel_id=1, source_target_pairs={{0,8},{1,12},{2,10},{3,14},{4,9},{5,13},{6,11},{7,15},{8,0},{9,4},... | collective-permute-start | bytes 1572872 | tf_op jit(solution)/shard_map/ppermute | solution.py:128
  36.0 24.4 %collective-permute-start.19 = (bf16[256,1024]{1,0:T(8,128)(2,1)S(1)}, bf16[256,1024]{1,0:T(8,128)(2,1)S(1)}, u32[]{:S(2)}, u32[]{:S(2)}) collective-permute-start(bf16[256,1024]{1,0:T(8,128)(2,1)S(1)} %get-tuple-element.23), channel_id=1, source_target_pairs={{0,2},{1,3},{2,0},{3,1},{4,6},{5,7},{6,4},{7,5},{8,10},{9,11},{10,... | collective-permute-start | bytes 1572872 | tf_op jit(solution)/shard_map/ppermute | solution.py:128
  38.0 23.6 %collective-permute-start.18 = (bf16[256,1024]{1,0:T(8,128)(2,1)S(1)}, bf16[256,1024]{1,0:T(8,128)(2,1)S(1)}, u32[]{:S(2)}, u32[]{:S(2)}) collective-permute-start(bf16[256,1024]{1,0:T(8,128)(2,1)S(1)} %add_convert_fusion), channel_id=1, source_target_pairs={{16,2},{17,3},{18,0},{19,1},{20,6},{21,7},{22,4},{23,5},{24,10},{2... | collective-permute-start | bytes 1572872 | tf_op jit(solution)/shard_map/ppermute | solution.py:128
  39.3 25.0 %collective-permute-start.16 = (bf16[256,1024]{1,0:T(8,128)(2,1)S(1)}, bf16[256,1024]{1,0:T(8,128)(2,1)S(1)}, u32[]{:S(2)}, u32[]{:S(2)}) collective-permute-start(bf16[256,1024]{1,0:T(8,128)(2,1)S(1)} %add_convert_fusion.1), channel_id=1, source_target_pairs={{16,0},{17,1},{18,2},{19,3},{20,4},{21,5},{22,6},{23,7},{24,8},{25... | collective-permute-start | bytes 1572872 | tf_op jit(solution)/shard_map/ppermute | solution.py:128
  41.1 50.3 %copy-start.2 = (bf16[256,1024]{1,0:T(8,128)(2,1)}, bf16[256,1024]{1,0:T(8,128)(2,1)S(1)}, u32[]{:S(2)}) copy-start(bf16[256,1024]{1,0:T(8,128)(2,1)S(1)} %collective-permute-done.29.refs_0_) | copy-start | bytes 1572868
  41.1 35.5 %collective-permute-start.14 = (bf16[256,1024]{1,0:T(8,128)(2,1)S(1)}, bf16[256,1024]{1,0:T(8,128)(2,1)}, u32[]{:S(2)}, u32[]{:S(2)}) collective-permute-start(bf16[256,1024]{1,0:T(8,128)(2,1)S(1)} %fusion.8), channel_id=1, source_target_pairs={{16,2},{17,3},{18,0},{19,1},{20,6},{21,7},{22,4},{23,5},{24,10},{2... | collective-permute-start | bytes 1572872 | tf_op jit(solution)/shard_map/ppermute | solution.py:128
  59.0 34.2 %copy-start.4 = (bf16[256,1024]{1,0:T(8,128)(2,1)}, bf16[256,1024]{1,0:T(8,128)(2,1)S(1)}, u32[]{:S(2)}) copy-start(bf16[256,1024]{1,0:T(8,128)(2,1)S(1)} %collective-permute-done.31.refs_1_) | copy-start | bytes 1572868
  59.0 27.7 %collective-permute-start.12 = (bf16[256,1024]{1,0:T(8,128)(2,1)S(1)}, bf16[256,1024]{1,0:T(8,128)(2,1)S(1)}, u32[]{:S(2)}, u32[]{:S(2)}) collective-permute-start(bf16[256,1024]{1,0:T(8,128)(2,1)S(1)} %fusion.9), channel_id=1, source_target_pairs={{16,0},{17,1},{18,2},{19,3},{20,4},{21,5},{22,6},{23,7},{24,8},{25... | collective-permute-start | bytes 1572872 | tf_op jit(solution)/shard_map/ppermute | solution.py:128
  60.3 27.1 %collective-permute-start.8 = (bf16[256,1024]{1,0:T(8,128)(2,1)S(1)}, bf16[256,1024]{1,0:T(8,128)(2,1)S(1)}, u32[]{:S(2)}, u32[]{:S(2)}) collective-permute-start(bf16[256,1024]{1,0:T(8,128)(2,1)S(1)} %fusion.10), channel_id=1, source_target_pairs={{16,18},{17,19},{18,16},{19,17},{20,22},{21,23},{22,20},{23,21},{2... | collective-permute-start | bytes 1572872 | tf_op jit(solution)/shard_map/ppermute | solution.py:128
  61.5 78.7 %copy-start.14 = (bf16[1,256,2,256]{3,2,1,0:T(2,128)(2,1)S(1)}, bf16[1,256,2,256]{3,2,1,0:T(2,128)(2,1)}, u32[]{:S(2)}) copy-start(bf16[1,256,2,256]{3,2,1,0:T(2,128)(2,1)} %param.4) | copy-start | bytes 786436
  61.6 15.0 %copy-start.17 = (bf16[256,1024]{1,0:T(8,128)(2,1)}, bf16[256,1024]{1,0:T(8,128)(2,1)S(1)}, u32[]{:S(2)}) copy-start(bf16[256,1024]{1,0:T(8,128)(2,1)S(1)} %collective-permute-done.18.refs_1_) | copy-start | bytes 1572868
  61.6 27.3 %collective-permute-start.3 = (bf16[256,1024]{1,0:T(8,128)(2,1)S(1)}, bf16[256,1024]{1,0:T(8,128)(2,1)S(1)}, u32[]{:S(2)}, u32[]{:S(2)}) collective-permute-start(bf16[256,1024]{1,0:T(8,128)(2,1)S(1)} %fusion.12), channel_id=1, source_target_pairs={{16,18},{17,19},{18,16},{19,17},{20,22},{21,23},{22,20},{23,21},{2... | collective-permute-start | bytes 1572872 | tf_op jit(solution)/shard_map/ppermute | solution.py:128
  64.3 12.3 %copy-start.18 = (bf16[256,1024]{1,0:T(8,128)(2,1)}, bf16[256,1024]{1,0:T(8,128)(2,1)S(1)}, u32[]{:S(2)}) copy-start(bf16[256,1024]{1,0:T(8,128)(2,1)S(1)} %collective-permute-done.16.refs_0_) | copy-start | bytes 1572868
  64.3 26.1 %collective-permute-start.35 = (bf16[256,1024]{1,0:T(8,128)(2,1)S(1)}, bf16[256,1024]{1,0:T(8,128)(2,1)S(1)}, u32[]{:S(2)}, u32[]{:S(2)}) collective-permute-start(bf16[256,1024]{1,0:T(8,128)(2,1)S(1)} %collective-permute-done.29.refs_0_), channel_id=1, source_target_pairs={{0,1},{1,0},{2,3},{3,2},{4,5},{5,4},{6,7},{7,6},{8,9},{9,8},{10,11... | collective-permute-start | bytes 1572872 | tf_op jit(solution)/shard_map/ppermute | solution.py:128
  76.6 14.8 %collective-permute-start.36 = (bf16[256,1024]{1,0:T(8,128)(2,1)S(1)}, bf16[256,1024]{1,0:T(8,128)(2,1)S(1)}, u32[]{:S(2)}, u32[]{:S(2)}) collective-permute-start(bf16[256,1024]{1,0:T(8,128)(2,1)S(1)} %collective-permute-done.31.refs_1_), channel_id=1, source_target_pairs={{0,1},{1,0},{2,3},{3,2},{4,5},{5,4},{6,7},{7,6},{8,9},{9,8},{10,11... | collective-permute-start | bytes 1572872 | tf_op jit(solution)/shard_map/ppermute | solution.py:128
  86.8 28.2 %collective-permute-start.20 = (bf16[256,1024]{1,0:T(8,128)(2,1)S(1)}, bf16[256,1024]{1,0:T(8,128)(2,1)S(1)}, u32[]{:S(2)}, u32[]{:S(2)}) collective-permute-start(bf16[256,1024]{1,0:T(8,128)(2,1)S(1)} %get-tuple-element.22), channel_id=1, source_target_pairs={{0,0},{1,4},{2,2},{3,6},{4,1},{5,5},{6,3},{7,7},{8,8},{9,12},{10,1... | collective-permute-start | bytes 1572872 | tf_op jit(solution)/shard_map/ppermute | solution.py:128
  87.5 29.0 %collective-permute-start.22 = (bf16[256,1024]{1,0:T(8,128)(2,1)S(1)}, bf16[256,1024]{1,0:T(8,128)(2,1)S(1)}, u32[]{:S(2)}, u32[]{:S(2)}) collective-permute-start(bf16[256,1024]{1,0:T(8,128)(2,1)S(1)} %get-tuple-element.21), channel_id=1, source_target_pairs={{0,8},{1,12},{2,10},{3,14},{4,9},{5,13},{6,11},{7,15},{8,0},{9,4},... | collective-permute-start | bytes 1572872 | tf_op jit(solution)/shard_map/ppermute | solution.py:128
  88.8 13.1 %collective-permute-start.30 = (bf16[256,1024]{1,0:T(8,128)(2,1)S(1)}, bf16[256,1024]{1,0:T(8,128)(2,1)S(1)}, u32[]{:S(2)}, u32[]{:S(2)}) collective-permute-start(bf16[256,1024]{1,0:T(8,128)(2,1)S(1)} %collective-permute-done.29.refs_0_), channel_id=1, source_target_pairs={{0,2},{1,3},{2,0},{3,1},{4,6},{5,7},{6,4},{7,5},{8,10},{9,11},{10,... | collective-permute-start | bytes 1572872 | tf_op jit(solution)/shard_map/ppermute | solution.py:128
  90.4 49.8 %copy-start.6 = (bf16[256,1024]{1,0:T(8,128)(2,1)}, bf16[256,1024]{1,0:T(8,128)(2,1)S(1)}, u32[]{:S(2)}) copy-start(bf16[256,1024]{1,0:T(8,128)(2,1)S(1)} %collective-permute-done.35.refs_2_) | copy-start | bytes 1572868
  90.4 22.8 %collective-permute-start.32 = (bf16[256,1024]{1,0:T(8,128)(2,1)S(1)}, bf16[256,1024]{1,0:T(8,128)(2,1)S(1)}, u32[]{:S(2)}, u32[]{:S(2)}) collective-permute-start(bf16[256,1024]{1,0:T(8,128)(2,1)S(1)} %collective-permute-done.31.refs_1_), channel_id=1, source_target_pairs={{0,2},{1,3},{2,0},{3,1},{4,6},{5,7},{6,4},{7,5},{8,10},{9,11},{10,... | collective-permute-start | bytes 1572872 | tf_op jit(solution)/shard_map/ppermute | solution.py:128
  91.4 48.8 %copy-start.8 = (bf16[256,1024]{1,0:T(8,128)(2,1)}, bf16[256,1024]{1,0:T(8,128)(2,1)S(1)}, u32[]{:S(2)}) copy-start(bf16[256,1024]{1,0:T(8,128)(2,1)S(1)} %collective-permute-done.36.refs_3_) | copy-start | bytes 1572868
  91.4 25.6 %collective-permute-start.9 = (bf16[256,1024]{1,0:T(8,128)(2,1)S(1)}, bf16[256,1024]{1,0:T(8,128)(2,1)S(1)}, u32[]{:S(2)}, u32[]{:S(2)}) collective-permute-start(bf16[256,1024]{1,0:T(8,128)(2,1)S(1)} %fusion.11), channel_id=1, source_target_pairs={{16,0},{17,1},{18,2},{19,3},{20,4},{21,5},{22,6},{23,7},{24,8},{25... | collective-permute-start | bytes 1572872 | tf_op jit(solution)/shard_map/ppermute | solution.py:128
  102.0 15.5 %collective-permute-start.4 = (bf16[256,1024]{1,0:T(8,128)(2,1)S(1)}, bf16[256,1024]{1,0:T(8,128)(2,1)S(1)}, u32[]{:S(2)}, u32[]{:S(2)}) collective-permute-start(bf16[256,1024]{1,0:T(8,128)(2,1)S(1)} %fusion.13), channel_id=1, source_target_pairs={{16,0},{17,1},{18,2},{19,3},{20,4},{21,5},{22,6},{23,7},{24,8},{25... | collective-permute-start | bytes 1572872 | tf_op jit(solution)/shard_map/ppermute | solution.py:128
  113.2 6.4 %collective-permute-start.33 = (bf16[256,1024]{1,0:T(8,128)(2,1)S(1)}, bf16[256,1024]{1,0:T(8,128)(2,1)S(1)}, u32[]{:S(2)}, u32[]{:S(2)}) collective-permute-start(bf16[256,1024]{1,0:T(8,128)(2,1)S(1)} %collective-permute-done.30.refs_0_), channel_id=1, source_target_pairs={{0,1},{1,0},{2,3},{3,2},{4,5},{5,4},{6,7},{7,6},{8,9},{9,8},{10,11... | collective-permute-start | bytes 1572872 | tf_op jit(solution)/shard_map/ppermute | solution.py:128
  115.0 14.9 %collective-permute-start.21 = (bf16[256,1024]{1,0:T(8,128)(2,1)S(1)}, bf16[256,1024]{1,0:T(8,128)(2,1)}, u32[]{:S(2)}, u32[]{:S(2)}) collective-permute-start(bf16[256,1024]{1,0:T(8,128)(2,1)S(1)} %collective-permute-done.20.refs_0_), channel_id=1, source_target_pairs={{0,2},{1,3},{2,0},{3,1},{4,6},{5,7},{6,4},{7,5},{8,10},{9,11},{10,... | collective-permute-start | bytes 1572872 | tf_op jit(solution)/shard_map/ppermute | solution.py:128
  116.5 23.6 %collective-permute-start.23 = (bf16[256,1024]{1,0:T(8,128)(2,1)S(1)}, bf16[256,1024]{1,0:T(8,128)(2,1)}, u32[]{:S(2)}, u32[]{:S(2)}) collective-permute-start(bf16[256,1024]{1,0:T(8,128)(2,1)S(1)} %collective-permute-done.22.refs_1_), channel_id=1, source_target_pairs={{0,2},{1,3},{2,0},{3,1},{4,6},{5,7},{6,4},{7,5},{8,10},{9,11},{10,... | collective-permute-start | bytes 1572872 | tf_op jit(solution)/shard_map/ppermute | solution.py:128
  117.0 23.1 %copy-start.15 = (bf16[256,1024]{1,0:T(8,128)(2,1)}, bf16[256,1024]{1,0:T(8,128)(2,1)S(1)}, u32[]{:S(2)}) copy-start(bf16[256,1024]{1,0:T(8,128)(2,1)S(1)} %collective-permute-done.9.refs_0_) | copy-start | bytes 1572868
  117.0 42.3 %collective-permute-start.34 = (bf16[256,1024]{1,0:T(8,128)(2,1)S(1)}, bf16[256,1024]{1,0:T(8,128)(2,1)}, u32[]{:S(2)}, u32[]{:S(2)}) collective-permute-start(bf16[256,1024]{1,0:T(8,128)(2,1)S(1)} %collective-permute-done.32.refs_1_), channel_id=1, source_target_pairs={{0,1},{1,0},{2,3},{3,2},{4,5},{5,4},{6,7},{7,6},{8,9},{9,8},{10,11... | collective-permute-start | bytes 1572872 | tf_op jit(solution)/shard_map/ppermute | solution.py:128
  117.5 23.7 %copy-start.16 = (bf16[256,1024]{1,0:T(8,128)(2,1)}, bf16[256,1024]{1,0:T(8,128)(2,1)S(1)}, u32[]{:S(2)}) copy-start(bf16[256,1024]{1,0:T(8,128)(2,1)S(1)} %collective-permute-done.4.refs_0_) | copy-start | bytes 1572868
  117.5 48.2 %collective-permute-start.26 = (bf16[256,1024]{1,0:T(8,128)(2,1)S(1)}, bf16[256,1024]{1,0:T(8,128)(2,1)}, u32[]{:S(2)}, u32[]{:S(2)}) collective-permute-start(bf16[256,1024]{1,0:T(8,128)(2,1)S(1)} %collective-permute-done.20.refs_0_), channel_id=1, source_target_pairs={{0,1},{1,0},{2,3},{3,2},{4,5},{5,4},{6,7},{7,6},{8,9},{9,8},{10,11... | collective-permute-start | bytes 1572872 | tf_op jit(solution)/shard_map/ppermute | solution.py:128
  120.4 45.2 %collective-permute-start.27 = (bf16[256,1024]{1,0:T(8,128)(2,1)S(1)}, bf16[256,1024]{1,0:T(8,128)(2,1)}, u32[]{:S(2)}, u32[]{:S(2)}) collective-permute-start(bf16[256,1024]{1,0:T(8,128)(2,1)S(1)} %collective-permute-done.22.refs_1_), channel_id=1, source_target_pairs={{0,1},{1,0},{2,3},{3,2},{4,5},{5,4},{6,7},{7,6},{8,9},{9,8},{10,11... | collective-permute-start | bytes 1572872 | tf_op jit(solution)/shard_map/ppermute | solution.py:128
  129.9 41.1 %collective-permute-start.24 = (bf16[256,1024]{1,0:T(8,128)(2,1)}, bf16[256,1024]{1,0:T(8,128)(2,1)}, u32[]{:S(2)}, u32[]{:S(2)}) collective-permute-start(bf16[256,1024]{1,0:T(8,128)(2,1)} %collective-permute-done.21.refs_0_), channel_id=1, source_target_pairs={{0,1},{1,0},{2,3},{3,2},{4,5},{5,4},{6,7},{7,6},{8,9},{9,8},{10,11... | collective-permute-start | bytes 1572872 | tf_op jit(solution)/shard_map/ppermute | solution.py:128
  140.2 30.8 %collective-permute-start.25 = (bf16[256,1024]{1,0:T(8,128)(2,1)}, bf16[256,1024]{1,0:T(8,128)(2,1)}, u32[]{:S(2)}, u32[]{:S(2)}) collective-permute-start(bf16[256,1024]{1,0:T(8,128)(2,1)} %collective-permute-done.23.refs_1_), channel_id=1, source_target_pairs={{0,1},{1,0},{2,3},{3,2},{4,5},{5,4},{6,7},{7,6},{8,9},{9,8},{10,11... | collective-permute-start | bytes 1572872 | tf_op jit(solution)/shard_map/ppermute | solution.py:128
  (9 other events, 18.0 us)

commit v3 on v2

v3 whole, which is shorter than its diff:
```python
import jax
import jax.numpy as jnp
from jax import lax
from jax.experimental import pallas as pl
from jax.experimental.pallas import tpu as pltpu
from jax.sharding import PartitionSpec as P

BLOCK = 128
TILE = 256
RUNS = 2
MIB = 1024 * 1024
LIGHT = pl.CostEstimate(flops=0, bytes_accessed=0, transcendentals=0)


def turned_kernel(slots, *refs):
    for k in range(4):
        refs[-1][slots[k]] = refs[k // 2][k % 2].T


def turned(slots, grads):
    groups, tokens, columns = grads[0].shape
    return pl.pallas_call(
        turned_kernel,
        grid_spec=pltpu.PrefetchScalarGridSpec(
            num_scalar_prefetch=1,
            grid=(1,),
            in_specs=[pl.BlockSpec((groups, tokens, columns), lambda i, slots: (0, 0, 0)) for _ in grads],
            out_specs=pl.BlockSpec((2 * groups, columns, tokens), lambda i, slots: (0, 0, 0)),
        ),
        out_shape=jax.ShapeDtypeStruct((2 * groups, columns, tokens), jnp.bfloat16),
        cost_estimate=LIGHT,
    )(slots, *grads)


def stacked_kernel(a_ref, b_ref, out_ref):
    out_ref[0] = a_ref[...]
    out_ref[1] = b_ref[...]


def stacked(a, b):
    return pl.pallas_call(
        stacked_kernel, out_shape=jax.ShapeDtypeStruct((2, *a.shape), a.dtype), cost_estimate=LIGHT
    )(a, b)


def across_dot(a, b):
    return lax.dot_general(a, b, (((1,), (1,)), ((), ())), preferred_element_type=jnp.float32)


def input_grad_kernel(m, *refs):
    groups = (len(refs) - 6) // 2
    owns, others = refs[:groups], refs[groups : 2 * groups]
    own2_ref, own0_ref, other2_ref, other0_ref, a_ref, m_ref = refs[2 * groups :]
    for n in range(groups):
        own, other = owns[n][...], others[n][...]
        a = across_dot(own, own2_ref[...]) + across_dot(other, other2_ref[...])
        a_ref[n] = a.astype(a_ref.dtype)
        b = across_dot(own, own0_ref[...]) + across_dot(other, other0_ref[...])
        m_ref[n] = b.astype(m_ref.dtype)


def input_grad(m, owns, others, weights, other_weights, parts, kept):
    tokens, columns = owns[0].shape
    groups = len(owns)
    share = weights.shape[0] // parts
    tile = share // 2
    in_specs = [pl.BlockSpec((tokens, columns), lambda i, m: (0, 0)) for _ in range(2 * groups)]
    in_specs += [pl.BlockSpec((tile, columns), lambda i, m, k=k: ((m[0] ^ k) * 2 + i, 0)) for k in (2, 0, 2, 0)]
    out = pl.BlockSpec((groups, tokens, tile), lambda i, m: (0, 0, i))
    return pl.pallas_call(
        input_grad_kernel,
        grid_spec=pltpu.PrefetchScalarGridSpec(
            num_scalar_prefetch=1, grid=(share // tile,), in_specs=in_specs, out_specs=[out, out]
        ),
        out_shape=[jax.ShapeDtypeStruct((groups, tokens, share), t) for t in (jnp.bfloat16, kept)],
        compiler_params=pltpu.CompilerParams(vmem_limit_bytes=32 * MIB),
        cost_estimate=LIGHT,
    )(jnp.reshape(m, (1,)).astype(jnp.int32), *owns, *others, weights, weights, other_weights, other_weights)


def chosen_kernel(flag, here_ref, there_ref, a_ref, b_ref):
    @pl.when(flag[0] == 1)
    def _():
        a_ref[...] = here_ref[...]
        b_ref[...] = there_ref[...]

    @pl.when(flag[0] == 0)
    def _():
        a_ref[...] = there_ref[...]
        b_ref[...] = here_ref[...]


def chosen(flag, here, there, n, runs):
    tokens, width = there.shape
    run = width // runs
    block = (tokens // 2, run)
    return pl.pallas_call(
        chosen_kernel,
        grid_spec=pltpu.PrefetchScalarGridSpec(
            num_scalar_prefetch=1,
            grid=(2,),
            in_specs=[pl.BlockSpec(block, lambda i, flag: (i, n))] * 2,
            out_specs=[pl.BlockSpec(block, lambda i, flag: (i, 0))] * 2,
        ),
        out_shape=[jax.ShapeDtypeStruct((tokens, run), here.dtype)] * 2,
        cost_estimate=LIGHT,
    )(jnp.reshape(flag, (1,)).astype(jnp.int32), here, there)


def summed_kernel(a_ref, b_ref, out_ref):
    out_ref[...] = (a_ref[...].astype(jnp.float32) + b_ref[...].astype(jnp.float32)).astype(out_ref.dtype)


def summed(a, b):
    block = pl.BlockSpec((1, *a.shape[1:]), lambda i: (i, 0, 0))
    return pl.pallas_call(
        summed_kernel,
        grid=(a.shape[0],),
        in_specs=[block, block],
        out_specs=block,
        out_shape=jax.ShapeDtypeStruct(a.shape, jnp.bfloat16),
        cost_estimate=LIGHT,
    )(a, b)


def weight_grad_kernel(at, *refs):
    lefts, grads_ref = refs[:4], refs[4]
    mantissa_ref, scale_ref = refs[-2:]
    top = total = None
    for i, left in enumerate(lefts):
        part = jnp.dot(grads_ref[i], left[...], preferred_element_type=jnp.float32)
        total = part if total is None else total + part
        top = jnp.abs(part) if top is None else jnp.maximum(top, jnp.abs(part))
    columns, rows = top.shape
    blocks = columns // BLOCK
    scale = jnp.max(top.reshape(blocks, BLOCK, rows), axis=1) + 1e-6
    scale_ref[...] = scale
    inverse = 1.0 / scale
    scaled = [
        (total[b * BLOCK : (b + 1) * BLOCK] * inverse[b : b + 1]).astype(jnp.bfloat16) for b in range(blocks)
    ]
    half = blocks // 2
    mantissa_ref[:, 0, :] = jnp.concatenate(scaled[:half], axis=0).T
    mantissa_ref[:, 1, :] = jnp.concatenate(scaled[half:], axis=0).T


def weight_grad(at, lefts, grads, into, row_total):
    columns = grads.shape[1]
    tokens, rows = lefts[0].shape
    in_specs = [pl.BlockSpec((tokens, TILE), lambda i, at: (0, i)) for _ in lefts]
    in_specs.append(pl.BlockSpec(grads.shape, lambda i, at: (0, 0, 0)))
    operands = [*lefts, grads]
    aliases = {}
    for n, held in enumerate(into):
        in_specs.append(pl.BlockSpec(memory_space=pl.ANY))
        operands.append(held)
        aliases[len(operands)] = n
    return pl.pallas_call(
        weight_grad_kernel,
        grid_spec=pltpu.PrefetchScalarGridSpec(
            num_scalar_prefetch=1,
            grid=(rows // TILE,),
            in_specs=in_specs,
            out_specs=[
                pl.BlockSpec((TILE, 2, columns // 2), lambda i, at: (at[0] + i, 0, 0)),
                pl.BlockSpec((columns // BLOCK, TILE), lambda i, at: (0, at[0] + i)),
            ],
        ),
        out_shape=[
            jax.ShapeDtypeStruct((row_total, 2, columns // 2), jnp.bfloat16),
            jax.ShapeDtypeStruct((columns // BLOCK, row_total), jnp.float32),
        ],
        input_output_aliases=aliases,
        compiler_params=pltpu.CompilerParams(vmem_limit_bytes=32 * MIB),
        cost_estimate=LIGHT,
    )(at, *operands)


def placed_kernel(group, *refs):
    terms, out_ref = refs[:-1], refs[-1]
    if len(terms) == 1:
        out_ref[...] = terms[0][0]
    else:
        out_ref[...] = (terms[0][0].astype(jnp.float32) + terms[1][0].astype(jnp.float32)).astype(jnp.bfloat16)


def placed_again_kernel(group, *refs):
    placed_kernel(group, *refs[:-2], refs[-1])


def placed(group, first, by, terms, into, groups):
    some, tokens, width = terms[0].shape
    in_specs = [pl.BlockSpec((1, tokens, width), lambda i, group: (i, 0, 0)) for _ in terms]
    operands = list(terms)
    aliases = {}
    if into is not None:
        in_specs.append(pl.BlockSpec(memory_space=pl.ANY))
        operands.append(into)
        aliases[len(operands)] = 0
    return pl.pallas_call(
        placed_kernel if into is None else placed_again_kernel,
        grid_spec=pltpu.PrefetchScalarGridSpec(
            num_scalar_prefetch=1,
            grid=(some,),
            in_specs=in_specs,
            out_specs=pl.BlockSpec((tokens, width), lambda i, group: (group[0] ^ (first + by * i), 0)),
        ),
        out_shape=jax.ShapeDtypeStruct((groups * tokens, width), jnp.bfloat16),
        input_output_aliases=aliases,
        cost_estimate=LIGHT,
    )(jnp.reshape(group, (1,)).astype(jnp.int32), *operands)


def on_device(layer_input, kv_cotangent, kv_weight):
    n_pipe, n_dp, n_mp = (lax.axis_size(a) for a in ("pipe", "dp", "mp"))
    p, m = lax.axis_index("dp"), lax.axis_index("mp")
    features = layer_input[0]
    tokens, width = features.shape
    columns = 2 * kv_cotangent.shape[3]
    rows = kv_weight.shape[1]
    share = rows // n_mp

    def move(x, where):
        pairs = []
        for s in range(n_pipe):
            for i in range(n_dp):
                for j in range(n_mp):
                    to = where(s, i, j)
                    if to is not None:
                        pairs.append(((s * n_dp + i) * n_mp + j, (to[0] * n_dp + to[1]) * n_mp + to[2]))
        return lax.ppermute(x, ("pipe", "dp", "mp"), pairs)

    def across(x):
        return move(x, lambda s, i, j: (s, i, j ^ 2))

    def other_core(x):
        return move(x, lambda s, i, j: (s, i, j ^ 1))

    def near(x):
        return move(x, lambda s, i, j: (s, 2 * (i // 2) + j % 2, 2 * (j // 2) + i % 2))

    def far(x):
        return move(x, lambda s, i, j: (s, 2 * (1 - i // 2) + j % 2, 2 * (j // 2) + i % 2))

    def across(x):
        return move(x, lambda s, i, j: (s, i, j ^ 2))

    def behind(x):
        return move(x, lambda s, i, j: (s - 1, i, j) if s else None)

    def behind_across(x):
        return move(x, lambda s, i, j: (s - 1, i, j ^ 2) if s else None)

    def across_but_first(x):
        return move(x, lambda s, i, j: (s, i, j ^ 2) if s else None)

    last = []

    def step(x):
        x = lax.optimization_barrier((x, *last))[0] if last else x
        last[:] = [x]
        return x

    def now(x):
        return lax.optimization_barrier((x, *last))[0] if last else x

    same = (m ^ p) & 1
    slots = jnp.where(same == 0, jnp.array([0, 1, 2, 3], jnp.int32), jnp.array([2, 3, 0, 1], jnp.int32))
    own_side = (m // 2) == (p // 2)
    half = width // 2
    run = half // RUNS
    direct_at = (jnp.where(own_side, 0, half) // TILE).astype(jnp.int32)
    crossed_at = (jnp.where(own_side, half, 0) // TILE).astype(jnp.int32)

    def weighed(at, n, four, into):
        return weight_grad(jnp.reshape(at + n * run // TILE, (1,)), four, turned_grads, into, rows)

    there = across(features[:, half:])
    g0 = kv_cotangent[0].reshape(tokens, columns)
    g2 = move(g0, lambda s, i, j: (s, i ^ 2, j))
    g0_core = other_core(g0)
    other_weights = other_core(kv_weight)
    weights = kv_weight[0].reshape(rows, columns)
    other_weights = step(other_weights)[0].reshape(rows, columns)
    g2 = step(g2)
    g02 = stacked(g0, g2)
    last[:] = [g02]
    g13 = move(g02, lambda s, i, j: (s, i ^ 1, j))
    g2_core = other_core(now(g2))

    g0_core = step(g0_core)
    g2_core = step(g2_core)
    a_late, m_late = input_grad(m, (g0, g2), (g0_core, g2_core), weights, other_weights, n_mp, jnp.bfloat16)
    last[:] = [a_late]
    late_own = behind(m_late)
    there = step(there)
    a, b = chosen(own_side, features, there, 0, RUNS)
    last[:] = [a]
    far0 = far(b)
    near0 = near(a)
    a, b = chosen(own_side, features, now(there), 1, RUNS)
    last[:] = [a]
    g13 = step(g13)
    g1, g3 = g13[0], g13[1]
    g1_core, g3_core = other_core(g1), other_core(g3)
    turned_grads = turned(slots, (g02, g13))
    last[:] = [turned_grads]
    g1_core = step(g1_core)
    g3_core = step(g3_core)
    a_early, m_early = input_grad(m, (g1, g3), (g1_core, g3_core), weights, other_weights, n_mp, jnp.float32)
    last[:] = [a_early]
    a_across = across_but_first(a_early)
    near0 = step(near0)
    near0_across = across(near0)
    far0 = step(far0)
    far0_across = across(far0)
    far1 = far(now(b))
    near1 = near(now(a))
    near0_core, far0_core = other_core(now(near0)), other_core(now(far0))
    late_own = step(late_own)
    late_across = behind_across(now(a_late))
    near0_core, far0_core = step(near0_core), step(far0_core)
    out = weighed(direct_at, 0, (near0, far0, near0_core, far0_core), ())
    last[:] = [out[0]]
    a_across = step(a_across)
    early_sum = summed(m_early, a_across)
    last[:] = [early_sum]
    early = behind(early_sum)
    near1 = step(near1)
    near1_across = across(near1)
    far1 = step(far1)
    far1_across = across(far1)
    near1_core, far1_core = other_core(now(near1)), other_core(now(far1))
    near0_across = step(near0_across)
    far0_across = step(far0_across)
    near0_across_core, far0_across_core = other_core(now(near0_across)), other_core(now(far0_across))
    near1_core, far1_core = step(near1_core), step(far1_core)
    out = weighed(direct_at, 1, (near1, far1, near1_core, far1_core), out)
    last[:] = [out[0]]
    near0_across_core, far0_across_core = step(near0_across_core), step(far0_across_core)
    out = weighed(crossed_at, 0, (near0_across, far0_across, near0_across_core, far0_across_core), out)
    last[:] = [out[0]]
    late_across = step(late_across)
    total = placed(p, 0, 2, (late_own, late_across), None, n_dp)
    last[:] = [total]
    near1_across = step(near1_across)
    near1_across_core = other_core(now(near1_across))
    early = step(early)
    total = placed(p, 1, 2, (early,), total, n_dp)
    last[:] = [total]
    far1_across = step(far1_across)
    far1_across_core = other_core(far1_across)
    near1_across_core, far1_across_core = step(near1_across_core), step(far1_across_core)
    out = weighed(crossed_at, 1, (near1_across, far1_across, near1_across_core, far1_across_core), out)
    mantissa, scale = out
    scale = scale.T.reshape(rows, 2, columns // (2 * BLOCK))
    return (total[None], mantissa[None], scale[None])


def solution(mesh):
    in_specs = (P("pipe", "dp", "mp"), P("pipe", "dp", None, "mp"), P("pipe", "dp", None, "mp"))
    out_specs = (
        P("pipe", None, ("dp", "mp")),
        P("pipe", "dp", None, "mp"),
        P("pipe", "dp", None, "mp"),
    )
    return jax.shard_map(on_device, mesh=mesh, in_specs=in_specs, out_specs=out_specs, check_vma=False)
```

time: 178 us -> 160 us (0.90)
  waiting for transfers between devices: 72.7 us -> 58.3 us
  matrix products: 13.6 us -> 0 us
  Pallas kernels: 28.5 us -> 42 us
  starting transfers between devices: 42.1 us -> 29.2 us
  local copies, waits for them, and re-layouts: 17.7 us -> 28.1 us
    unnamed x41 -> x55, local copies, waits for them, and re-layouts: 7.19 us -> 26.1 us
    pallas_call x4 -> x9, Pallas kernels: 7.96 us -> 23.3 us  [the longest x2 6.75 us: input_grad(): pl.pallas_call(input_grad_kernel, grid_spec=pltpu.PrefetchScalarGridSpec(...]
    ppermute x37 -> x28, waiting for transfers between devices: 72.7 us -> 58.3 us  [move(): return lax.ppermute(x, ('pipe', 'dp', 'mp'), pairs)]
    dot_general x16 -> x0, matrix products: 13.6 us -> none  [times(): lax.dot_general(g, w[k], (((1,), (1,)), ((), ())), preferred_element_type...]
    ppermute x37 -> x28, starting transfers between devices: 42.1 us -> 29.2 us  [move(): return lax.ppermute(x, ('pipe', 'dp', 'mp'), pairs)]
    another operation x6 -> x0, local copies, waits for them, and re-layouts: 8.79 us -> none  [the longest x1 7.58 us: on_device(): quarters = kv_weight[0].reshape(n_mp, share, columns)]
  transfers between devices with their start and end apart: 37 -> 28, of which waited for: 9 -> 8; matrix products, arithmetic and copies ran while one was open for 14% -> 6% of each run, Pallas kernels for 13% -> 23%
where the time goes in v3:
time: 160 us; the launch traced here: 159 us
  waiting for transfers between devices  58.3 us (36%)
  Pallas kernels  42 us (26%)
  starting transfers between devices  29.2 us (18%)
  local copies, waits for them, and re-layouts  28.1 us (18%)
    ppermute x28, waiting for transfers between devices, move(): return lax.ppermute(x, ('pipe', 'dp', 'mp'), pairs)  58.3 us
    ppermute x28, starting transfers between devices, move(): return lax.ppermute(x, ('pipe', 'dp', 'mp'), pairs)  29.2 us
    unnamed x55, local copies, waits for them, and re-layouts  26.1 us
    pallas_call x4, Pallas kernels, weight_grad(): pl.pallas_call(weight_grad_kernel, grid_spec=pltpu.PrefetchScalarGridSpec...  18.7 us
    pallas_call x2, Pallas kernels, input_grad(): pl.pallas_call(input_grad_kernel, grid_spec=pltpu.PrefetchScalarGridSpec(...  6.75 us
    pallas_call x2, Pallas kernels, placed(): pl.pallas_call(placed_kernel if into is None else placed_again_kernel, gr...  4.47 us
    pallas_call x2, Pallas kernels, chosen(): pl.pallas_call(chosen_kernel, grid_spec=pltpu.PrefetchScalarGridSpec(num_...  4.14 us
    pallas_call x1, Pallas kernels, turned(): pl.pallas_call(turned_kernel, grid_spec=pltpu.PrefetchScalarGridSpec(num_...  3.26 us
  transfers between devices with their start and end apart: 28, of which 8 were waited for; matrix products, arithmetic and copies ran while one was open for 6% of the time, Pallas kernels for 23%

profile of v3, /device:TPU:0, one launch (start us, length us, event | category | flops | bytes accessed | tf_op | source)
XLA Modules:
  0.0 158.9 jit_solution(15427971524967101719)
XLA Ops:
  1.1 1.3 slice.12
  2.4 2.6 %collective-permute-start.3 = (bf16[256,2048]{1,0:T(8,128)(2,1)S(1)}, bf16[256,2048]{1,0:T(8,128)(2,1)S(1)}, u32[]{:S(2)}, u32[]{:S(2)}) collective-permute-start(bf16[256,2048]{1,0:T(8,128)(2,1)S(1)} %slice.12), channel_id=1, source_target_pairs={{0,2},{1,3},{2,0},{3,1},{4,6},{5,7},{6,4},{7,5},{8,10},{9,11},{10,... | collective-permute-start | bytes 3145736 | tf_op jit(solution)/shard_map/ppermute | solution.py:231
  5.0 1.0 copy.15
  6.0 2.7 %collective-permute-start = (bf16[256,512]{1,0:T(8,128)(2,1)S(1)}, bf16[256,512]{1,0:T(8,128)(2,1)S(1)}, u32[]{:S(2)}, u32[]{:S(2)}) collective-permute-start(bf16[256,512]{1,0:T(8,128)(2,1)S(1)} %bitcast.34), channel_id=1, source_target_pairs={{0,8},{1,9},{2,10},{3,11},{4,12},{5,13},{6,14},{7,15},{8,0},{9,1},... | collective-permute-start | bytes 786440 | tf_op jit(solution)/shard_map/ppermute | solution.py:231
  8.7 12.3 %collective-permute-done.b_ref.refs_1_ = bf16[256,512]{1,0:T(8,128)(2,1)S(1)} collective-permute-done((bf16[256,512]{1,0:T(8,128)(2,1)S(1)}, bf16[256,512]{1,0:T(8,128)(2,1)S(1)}, u32[]{:S(2)}, u32[]{:S(2)}) %collective-permute-start) | collective-permute-done | bytes 262176 | tf_op jit(solution)/shard_map/ppermute | solution.py:231
  21.8 1.9 %shard_map.76.refs_0_ = bf16[2,256,512]{2,1,0:T(8,128)(2,1)} custom-call(bf16[256,512]{1,0:T(8,128)(2,1)} %bitcast.35, bf16[256,512]{1,0:T(8,128)(2,1)} %copy-done.8), custom_call_target="tpu_custom_call" | custom-call | tf_op jit(solution)/shard_map/pallas_call | solution.py:41
  24.8 2.9 %copy.16 = bf16[512,8,2,256]{3,1,2,0:T(8,128)(2,1)S(1)} copy(bf16[512,8,2,256]{3,2,1,0:T(2,128)(2,1)} %bitcast.44) | data formatting | bytes 8388608
  27.8 4.4 %copy.17 = bf16[512,8,2,256]{3,1,2,0:T(8,128)(2,1)S(1)} copy(bf16[512,8,2,256]{3,2,1,0:T(2,128)(2,1)} %bitcast.20) | data formatting | bytes 8388608
  32.3 3.5 %shard_map.77 = (bf16[2,256,1024]{2,1,0:T(8,128)(2,1)S(1)}, bf16[2,256,1024]{2,1,0:T(8,128)(2,1)}) custom-call(s32[1]{0:T(128)} %bitcast.1.m, bf16[256,512]{1,0:T(8,128)(2,1)S(1)} %bitcast.37, bf16[256,512]{1,0:T(8,128)(2,1)S(1)} %copy-done.9, bf16[256,512]{1,0:T(8,128)(2,1)S(1)} %collective-permute-done.4.refs_2_, ...), custom_call_target="tpu_custom_call" | custom-call | tf_op jit(solution)/shard_map/pallas_call | solution.py:70
  35.8 1.0 copy-done.22
  36.8 1.0 copy-done.23
  37.8 2.0 %shard_map.78 = (bf16[256,1024]{1,0:T(8,128)(2,1)}, bf16[256,1024]{1,0:T(8,128)(2,1)}) custom-call(s32[1]{0:T(128)} %bitcast.2.flag, bf16[256,4096]{1,0:T(8,128)(2,1)} %bitcast.41, bf16[256,2048]{1,0:T(8,128)(2,1)} %copy-done.23), custom_call_target="tpu_custom_call" | custom-call | tf_op jit(solution)/shard_map/pallas_call | solution.py:97
  39.8 5.4 %collective-permute-start.9 = (bf16[256,1024]{1,0:T(8,128)(2,1)}, bf16[256,1024]{1,0:T(8,128)(2,1)}, u32[]{:S(2)}, u32[]{:S(2)}) collective-permute-start(bf16[256,1024]{1,0:T(8,128)(2,1)} %get-tuple-element.64), channel_id=1, source_target_pairs={{0,0},{1,4},{2,2},{3,6},{4,1},{5,5},{6,3},{7,7},{8,8},{9,12},{10,1... | collective-permute-start | bytes 1572872 | tf_op jit(solution)/shard_map/ppermute | solution.py:231
  45.2 3.4 %collective-permute-start.10 = (bf16[256,1024]{1,0:T(8,128)(2,1)}, bf16[256,1024]{1,0:T(8,128)(2,1)S(1)}, u32[]{:S(2)}, u32[]{:S(2)}) collective-permute-start(bf16[256,1024]{1,0:T(8,128)(2,1)} %get-tuple-element.73), channel_id=1, source_target_pairs={{0,8},{1,12},{2,10},{3,14},{4,9},{5,13},{6,11},{7,15},{8,0},{9,4},... | collective-permute-start | bytes 1572872 | tf_op jit(solution)/shard_map/ppermute | solution.py:231
  48.6 1.3 collective-permute-start.12
  49.9 2.1 %shard_map.79 = (bf16[256,1024]{1,0:T(8,128)(2,1)}, bf16[256,1024]{1,0:T(8,128)(2,1)}) custom-call(s32[1]{0:T(128)} %bitcast.2.flag, bf16[256,4096]{1,0:T(8,128)(2,1)} %bitcast.42, bf16[256,2048]{1,0:T(8,128)(2,1)} %copy-done.23), custom_call_target="tpu_custom_call" | custom-call | tf_op jit(solution)/shard_map/pallas_call | solution.py:97
  53.1 3.3 %shard_map.80.refs_4_ = bf16[4,512,256]{2,1,0:T(8,128)(2,1)} custom-call(s32[4]{0:T(128)} %broadcast_select_fusion.slots, bf16[2,256,512]{2,1,0:T(8,128)(2,1)} %shard_map.76.refs_0_, bf16[2,256,512]{2,1,0:T(8,128)(2,1)} %copy-done.24), custom_call_target="tpu_custom_call" | custom-call | tf_op jit(solution)/shard_map/pallas_call | solution.py:22
  56.4 2.2 %copy-done.1 = bf16[512,8,2,256]{3,1,2,0:T(8,128)(2,1)S(1)} copy-done((bf16[512,8,2,256]{3,1,2,0:T(8,128)(2,1)S(1)}, bf16[512,8,2,256]{3,1,2,0:T(8,128)(2,1)}, u32[]{:S(2)}) %copy-start.1) | copy-done | bytes 4194328
  58.6 2.2 %copy-done.3 = bf16[512,8,2,256]{3,1,2,0:T(8,128)(2,1)S(1)} copy-done((bf16[512,8,2,256]{3,1,2,0:T(8,128)(2,1)S(1)}, bf16[512,8,2,256]{3,1,2,0:T(8,128)(2,1)}, u32[]{:S(2)}) %copy-start.3) | copy-done | bytes 4194328
  60.8 3.2 %shard_map.81 = (bf16[2,256,1024]{2,1,0:T(8,128)(2,1)}, f32[2,256,1024]{2,1,0:T(8,128)S(1)}) custom-call(s32[1]{0:T(128)} %bitcast.1.m, bf16[256,512]{1,0:T(8,128)(2,1)S(1)} %get-tuple-element.114.refs_0_, bf16[256,512]{1,0:T(8,128)(2,1)S(1)} %get-tuple-element.113.refs_1_, bf16[256,512]{1,0:T(8,128)(2,1)S(1)} %collective-permute-done.6.refs_2_, ...), custom_call_target="tpu_custom_call" | custom-call | tf_op jit(solution)/shard_map/pallas_call | solution.py:70
  64.0 1.3 copy-done.7
  65.3 1.6 %collective-permute-start.8 = (bf16[2,256,1024]{2,1,0:T(8,128)(2,1)}, bf16[2,256,1024]{2,1,0:T(8,128)(2,1)}, u32[]{:S(2)}, u32[]{:S(2)}) collective-permute-start(bf16[2,256,1024]{2,1,0:T(8,128)(2,1)} %get-tuple-element.71), channel_id=1, source_target_pairs={{16,18},{17,19},{18,16},{19,17},{20,22},{21,23},{22,20},{23,21},{2... | collective-permute-start | bytes 3145736 | tf_op jit(solution)/shard_map/ppermute | solution.py:231
  67.0 1.8 %collective-permute-done.10.refs_1_ = bf16[256,1024]{1,0:T(8,128)(2,1)S(1)} collective-permute-done((bf16[256,1024]{1,0:T(8,128)(2,1)}, bf16[256,1024]{1,0:T(8,128)(2,1)S(1)}, u32[]{:S(2)}, u32[]{:S(2)}) %collective-permute-start.10) | collective-permute-done | bytes 524320 | tf_op jit(solution)/shard_map/ppermute | solution.py:231
  69.3 1.7 %collective-permute-start.15 = (bf16[256,1024]{1,0:T(8,128)(2,1)}, bf16[256,1024]{1,0:T(8,128)(2,1)S(1)}, u32[]{:S(2)}, u32[]{:S(2)}) collective-permute-start(bf16[256,1024]{1,0:T(8,128)(2,1)} %get-tuple-element.83), channel_id=1, source_target_pairs={{0,0},{1,4},{2,2},{3,6},{4,1},{5,5},{6,3},{7,7},{8,8},{9,12},{10,1... | collective-permute-start | bytes 1572872 | tf_op jit(solution)/shard_map/ppermute | solution.py:231
  72.5 0.8 copy-done.20
  73.8 1.5 collective-permute-start.20
  75.3 1.1 copy-done.17
  76.4 1.0 copy-done.19
  77.4 1.0 copy-done.21
  78.5 4.9 %shard_map.82 = (bf16[4096,2,256]{2,1,0:T(2,128)(2,1)}, f32[4,4096]{1,0:T(4,128)S(1)}) custom-call(s32[1]{0:T(128)} %bitcast.6.at, bf16[256,1024]{1,0:T(8,128)(2,1)} %collective-permute-done.9.refs_0_, bf16[256,1024]{1,0:T(8,128)(2,1)S(1)} %copy-done.17, bf16[256,1024]{1,0:T(8,128)(2,1)S(1)} %copy-done.19, bf16[256,1024]{1,0:T(8,128)(2,1)S(1)} %copy-done.21, ...), custom_call_target="tpu_custom_call" | custom-call | tf_op jit(solution)/shard_map/pallas_call | solution.py:158
  83.4 2.7 %shard_map.83 = bf16[2,256,1024]{2,1,0:T(8,128)(2,1)} custom-call(f32[2,256,1024]{2,1,0:T(8,128)} %copy-done.7, bf16[2,256,1024]{2,1,0:T(8,128)(2,1)} %collective-permute-done.8.b_ref), custom_call_target="tpu_custom_call" | custom-call | tf_op jit(solution)/shard_map/pallas_call | solution.py:116
  86.1 12.7 %collective-permute-done.19.refs_1_ = bf16[256,1024]{1,0:T(8,128)(2,1)S(1)} collective-permute-done((bf16[256,1024]{1,0:T(8,128)(2,1)}, bf16[256,1024]{1,0:T(8,128)(2,1)S(1)}, u32[]{:S(2)}, u32[]{:S(2)}) %collective-permute-start.19) | collective-permute-done | bytes 524320 | tf_op jit(solution)/shard_map/ppermute | solution.py:231
  98.8 1.3 collective-permute-start.17
  100.7 1.3 collective-permute-start.14
  102.1 0.8 copy-done.10
  103.4 0.9 copy-done.12
  105.5 1.5 collective-permute-start.25
  107.0 1.0 copy-done.11
  108.1 1.0 copy-done.13
  109.1 3.9 %shard_map.84 = (bf16[4096,2,256]{2,1,0:T(2,128)(2,1)}, f32[4,4096]{1,0:T(4,128)S(1)}) custom-call(s32[1]{0:T(128)} %bitcast.8.at, bf16[256,1024]{1,0:T(8,128)(2,1)S(1)} %collective-permute-done.15.refs_0_, bf16[256,1024]{1,0:T(8,128)(2,1)S(1)} %collective-permute-done.19.refs_1_, ...), custom_call_target="tpu_custom_call", output_to_operand_aliasing={{0}: (6, {}), {1}: (7, {})} | custom-call | tf_op jit(solution)/shard_map/pallas_call | solution.py:158
  113.1 4.9 %shard_map.85 = (bf16[4096,2,256]{2,1,0:T(2,128)(2,1)}, f32[4,4096]{1,0:T(4,128)S(1)}) custom-call(s32[1]{0:T(128)} %bitcast.7.at, bf16[256,1024]{1,0:T(8,128)(2,1)S(1)} %collective-permute-done.18.refs_0_, bf16[256,1024]{1,0:T(8,128)(2,1)S(1)} %collective-permute-done.20.refs_1_, ...), custom_call_target="tpu_custom_call", output_to_operand_aliasing={{0}: (6, {}), {1}: (7, {})} | custom-call | tf_op jit(solution)/shard_map/pallas_call | solution.py:158
  118.0 9.9 %collective-permute-done.17.refs_1_ = bf16[2,256,1024]{2,1,0:T(8,128)(2,1)} collective-permute-done((bf16[2,256,1024]{2,1,0:T(8,128)(2,1)}, bf16[2,256,1024]{2,1,0:T(8,128)(2,1)}, u32[]{:S(2)}, u32[]{:S(2)}) %collective-permute-start.17) | collective-permute-done | bytes 1048608 | tf_op jit(solution)/shard_map/ppermute | solution.py:231
  127.9 2.4 %shard_map.86.refs_1_ = bf16[1024,1024]{1,0:T(8,128)(2,1)} custom-call(s32[1]{0:T(128)} %bitcast.group, bf16[2,256,1024]{2,1,0:T(8,128)(2,1)} %collective-permute-done.12.refs_0_, bf16[2,256,1024]{2,1,0:T(8,128)(2,1)} %collective-permute-done.17.refs_1_), custom_call_target="tpu_custom_call" | custom-call | tf_op jit(solution)/shard_map/pallas_call | solution.py:200
  130.3 8.5 %collective-permute-done.16.refs_0_ = bf16[256,1024]{1,0:T(8,128)(2,1)} collective-permute-done((bf16[256,1024]{1,0:T(8,128)(2,1)S(1)}, bf16[256,1024]{1,0:T(8,128)(2,1)}, u32[]{:S(2)}, u32[]{:S(2)}) %collective-permute-start.16) | collective-permute-done | bytes 524320 | tf_op jit(solution)/shard_map/ppermute | solution.py:231
  138.8 10.2 %collective-permute-done.14.refs_0_ = bf16[2,256,1024]{2,1,0:T(8,128)(2,1)} collective-permute-done((bf16[2,256,1024]{2,1,0:T(8,128)(2,1)}, bf16[2,256,1024]{2,1,0:T(8,128)(2,1)}, u32[]{:S(2)}, u32[]{:S(2)}) %collective-permute-start.14) | collective-permute-done | bytes 1048608 | tf_op jit(solution)/shard_map/ppermute | solution.py:231
  149.0 2.0 %shard_map.87 = bf16[1024,1024]{1,0:T(8,128)(2,1)} custom-call(s32[1]{0:T(128)} %bitcast.group, bf16[2,256,1024]{2,1,0:T(8,128)(2,1)} %collective-permute-done.14.refs_0_, bf16[1024,1024]{1,0:T(8,128)(2,1)} %shard_map.86.refs_1_), custom_call_target="tpu_custom_call", output_to_operand_aliasing={{}: (2, {})} | custom-call | tf_op jit(solution)/shard_map/pallas_call | solution.py:200
  151.1 2.1 %collective-permute-done.27.refs_3_ = bf16[256,1024]{1,0:T(8,128)(2,1)S(1)} collective-permute-done((bf16[256,1024]{1,0:T(8,128)(2,1)}, bf16[256,1024]{1,0:T(8,128)(2,1)S(1)}, u32[]{:S(2)}, u32[]{:S(2)}) %collective-permute-start.27) | collective-permute-done | bytes 524320 | tf_op jit(solution)/shard_map/ppermute | solution.py:231
  153.2 5.0 %shard_map.88 = (bf16[4096,2,256]{2,1,0:T(2,128)(2,1)}, f32[4,4096]{1,0:T(4,128)S(1)}) custom-call(s32[1]{0:T(128)} %bitcast.10.at, bf16[256,1024]{1,0:T(8,128)(2,1)} %collective-permute-done.16.refs_0_, bf16[256,1024]{1,0:T(8,128)(2,1)} %collective-permute-done.25.refs_1_, ...), custom_call_target="tpu_custom_call", output_to_operand_aliasing={{0}: (6, {}), {1}: (7, {})} | custom-call | tf_op jit(solution)/shard_map/pallas_call | solution.py:158
  (80 shorter events, 9.3 us)
Async XLA Ops:
  0.6 20.4 %collective-permute-start.1 = (bf16[1,4096,2,256]{3,2,1,0:T(2,128)(2,1)}, bf16[1,4096,2,256]{3,2,1,0:T(2,128)(2,1)}, u32[]{:S(2)}, u32[]{:S(2)}) collective-permute-start(bf16[1,4096,2,256]{3,2,1,0:T(2,128)(2,1)} %param.7), channel_id=1, source_target_pairs={{0,1},{1,0},{2,3},{3,2},{4,5},{5,4},{6,7},{7,6},{8,9},{9,8},{10,11... | collective-permute-start | bytes 12582920 | tf_op jit(solution)/shard_map/ppermute | solution.py:231
  2.4 34.4 %collective-permute-start.3 = (bf16[256,2048]{1,0:T(8,128)(2,1)S(1)}, bf16[256,2048]{1,0:T(8,128)(2,1)S(1)}, u32[]{:S(2)}, u32[]{:S(2)}) collective-permute-start(bf16[256,2048]{1,0:T(8,128)(2,1)S(1)} %slice.12), channel_id=1, source_target_pairs={{0,2},{1,3},{2,0},{3,1},{4,6},{5,7},{6,4},{7,5},{8,10},{9,11},{10,... | collective-permute-start | bytes 3145736 | tf_op jit(solution)/shard_map/ppermute | solution.py:231
  6.0 15.0 %copy-start.5 = (bf16[32,8,2,256]{3,1,2,0:T(8,128)(2,1)}, bf16[32,8,2,256]{3,1,2,0:T(8,128)(2,1)S(1)}, u32[]{:S(2)}) copy-start(bf16[32,8,2,256]{3,1,2,0:T(8,128)(2,1)S(1)} %copy.15) | copy-start | bytes 786436
  6.0 15.0 %collective-permute-start = (bf16[256,512]{1,0:T(8,128)(2,1)S(1)}, bf16[256,512]{1,0:T(8,128)(2,1)S(1)}, u32[]{:S(2)}, u32[]{:S(2)}) collective-permute-start(bf16[256,512]{1,0:T(8,128)(2,1)S(1)} %bitcast.34), channel_id=1, source_target_pairs={{0,8},{1,9},{2,10},{3,11},{4,12},{5,13},{6,14},{7,15},{8,0},{9,1},... | collective-permute-start | bytes 786440 | tf_op jit(solution)/shard_map/ppermute | solution.py:231
  23.6 28.3 %collective-permute-start.2 = (bf16[2,256,512]{2,1,0:T(8,128)(2,1)}, bf16[2,256,512]{2,1,0:T(8,128)(2,1)S(1)}, u32[]{:S(2)}, u32[]{:S(2)}) collective-permute-start(bf16[2,256,512]{2,1,0:T(8,128)(2,1)} %shard_map.76.refs_0_), channel_id=1, source_target_pairs={{0,4},{1,5},{2,6},{3,7},{4,0},{5,1},{6,2},{7,3},{8,12},{9,13},{10,... | collective-permute-start | bytes 1572872 | tf_op jit(solution)/shard_map/ppermute | solution.py:231
  24.3 3.4 %collective-permute-start.4 = (bf16[256,512]{1,0:T(8,128)(2,1)}, bf16[256,512]{1,0:T(8,128)(2,1)S(1)}, u32[]{:S(2)}, u32[]{:S(2)}) collective-permute-start(bf16[256,512]{1,0:T(8,128)(2,1)} %bitcast.36), channel_id=1, source_target_pairs={{0,1},{1,0},{2,3},{3,2},{4,5},{5,4},{6,7},{7,6},{8,9},{9,8},{10,11... | collective-permute-start | bytes 786440 | tf_op jit(solution)/shard_map/ppermute | solution.py:231
  24.3 7.9 %collective-permute-start.5 = (bf16[256,512]{1,0:T(8,128)(2,1)}, bf16[256,512]{1,0:T(8,128)(2,1)S(1)}, u32[]{:S(2)}, u32[]{:S(2)}) collective-permute-start(bf16[256,512]{1,0:T(8,128)(2,1)} %copy-done.8), channel_id=1, source_target_pairs={{0,1},{1,0},{2,3},{3,2},{4,5},{5,4},{6,7},{7,6},{8,9},{9,8},{10,11... | collective-permute-start | bytes 786440 | tf_op jit(solution)/shard_map/ppermute | solution.py:231
  27.7 4.5 %copy-start = (bf16[512,8,2,256]{3,1,2,0:T(8,128)(2,1)}, bf16[512,8,2,256]{3,1,2,0:T(8,128)(2,1)S(1)}, u32[]{:S(2)}) copy-start(bf16[512,8,2,256]{3,1,2,0:T(8,128)(2,1)S(1)} %copy.16) | copy-start | bytes 12582916
  27.8 4.5 %copy-start.6 = (bf16[32,8,2,256]{3,1,2,0:T(8,128)(2,1)S(1)}, bf16[32,8,2,256]{3,1,2,0:T(8,128)(2,1)}, u32[]{:S(2)}) copy-start(bf16[32,8,2,256]{3,1,2,0:T(8,128)(2,1)} %copy-done.5) | copy-start | bytes 786436
  27.8 4.5 %copy-start.9 = (bf16[256,512]{1,0:T(8,128)(2,1)S(1)}, bf16[256,512]{1,0:T(8,128)(2,1)}, u32[]{:S(2)}) copy-start(bf16[256,512]{1,0:T(8,128)(2,1)} %copy-done.8) | copy-start | bytes 786436
  32.2 3.6 %copy-start.2 = (bf16[512,8,2,256]{3,1,2,0:T(8,128)(2,1)}, bf16[512,8,2,256]{3,1,2,0:T(8,128)(2,1)S(1)}, u32[]{:S(2)}) copy-start(bf16[512,8,2,256]{3,1,2,0:T(8,128)(2,1)S(1)} %copy.17) | copy-start | bytes 12582916
  35.8 1.0 copy-start.22
  36.8 15.8 %copy-start.25 = (s32[4]{0:T(128)S(1)}, s32[4]{0:T(128)}, u32[]{:S(2)}) copy-start(s32[4]{0:T(128)} %constant.62.clone) | copy-start | bytes 52
  36.8 1.0 copy-start.23
  39.8 27.2 %collective-permute-start.9 = (bf16[256,1024]{1,0:T(8,128)(2,1)}, bf16[256,1024]{1,0:T(8,128)(2,1)}, u32[]{:S(2)}, u32[]{:S(2)}) collective-permute-start(bf16[256,1024]{1,0:T(8,128)(2,1)} %get-tuple-element.64), channel_id=1, source_target_pairs={{0,0},{1,4},{2,2},{3,6},{4,1},{5,5},{6,3},{7,7},{8,8},{9,12},{10,1... | collective-permute-start | bytes 1572872 | tf_op jit(solution)/shard_map/ppermute | solution.py:231
  45.2 23.6 %collective-permute-start.10 = (bf16[256,1024]{1,0:T(8,128)(2,1)}, bf16[256,1024]{1,0:T(8,128)(2,1)S(1)}, u32[]{:S(2)}, u32[]{:S(2)}) collective-permute-start(bf16[256,1024]{1,0:T(8,128)(2,1)} %get-tuple-element.73), channel_id=1, source_target_pairs={{0,8},{1,12},{2,10},{3,14},{4,9},{5,13},{6,11},{7,15},{8,0},{9,4},... | collective-permute-start | bytes 1572872 | tf_op jit(solution)/shard_map/ppermute | solution.py:231
  48.6 25.2 %collective-permute-start.12 = (bf16[2,256,1024]{2,1,0:T(8,128)(2,1)}, bf16[2,256,1024]{2,1,0:T(8,128)(2,1)}, u32[]{:S(2)}, u32[]{:S(2)}) collective-permute-start(bf16[2,256,1024]{2,1,0:T(8,128)(2,1)} %get-tuple-element.76), channel_id=1, source_target_pairs={{16,0},{17,1},{18,2},{19,3},{20,4},{21,5},{22,6},{23,7},{24,8},{25... | collective-permute-start | bytes 3145736 | tf_op jit(solution)/shard_map/ppermute | solution.py:231
  52.0 1.2 copy-start.24
  52.0 4.4 %collective-permute-start.6 = (bf16[256,512]{1,0:T(8,128)(2,1)S(1)}, bf16[256,512]{1,0:T(8,128)(2,1)S(1)}, u32[]{:S(2)}, u32[]{:S(2)}) collective-permute-start(bf16[256,512]{1,0:T(8,128)(2,1)S(1)} %get-tuple-element.114.refs_0_), channel_id=1, source_target_pairs={{0,1},{1,0},{2,3},{3,2},{4,5},{5,4},{6,7},{7,6},{8,9},{9,8},{10,11... | collective-permute-start | bytes 786440 | tf_op jit(solution)/shard_map/ppermute | solution.py:231
  52.1 4.3 %collective-permute-start.7 = (bf16[256,512]{1,0:T(8,128)(2,1)S(1)}, bf16[256,512]{1,0:T(8,128)(2,1)S(1)}, u32[]{:S(2)}, u32[]{:S(2)}) collective-permute-start(bf16[256,512]{1,0:T(8,128)(2,1)S(1)} %get-tuple-element.113.refs_1_), channel_id=1, source_target_pairs={{0,1},{1,0},{2,3},{3,2},{4,5},{5,4},{6,7},{7,6},{8,9},{9,8},{10,11... | collective-permute-start | bytes 786440 | tf_op jit(solution)/shard_map/ppermute | solution.py:231
  56.4 2.2 %copy-start.1 = (bf16[512,8,2,256]{3,1,2,0:T(8,128)(2,1)S(1)}, bf16[512,8,2,256]{3,1,2,0:T(8,128)(2,1)}, u32[]{:S(2)}) copy-start(bf16[512,8,2,256]{3,1,2,0:T(8,128)(2,1)} %copy-done) | copy-start | bytes 12582916
  58.6 2.2 %copy-start.3 = (bf16[512,8,2,256]{3,1,2,0:T(8,128)(2,1)S(1)}, bf16[512,8,2,256]{3,1,2,0:T(8,128)(2,1)}, u32[]{:S(2)}) copy-start(bf16[512,8,2,256]{3,1,2,0:T(8,128)(2,1)} %copy-done.2) | copy-start | bytes 12582916
  60.8 14.5 %copy-start.4 = (bf16[4,512,256]{2,1,0:T(8,128)(2,1)S(1)}, bf16[4,512,256]{2,1,0:T(8,128)(2,1)}, u32[]{:S(2)}) copy-start(bf16[4,512,256]{2,1,0:T(8,128)(2,1)} %shard_map.80.refs_4_) | copy-start | bytes 3145732
  64.0 1.3 copy-start.7
  65.3 18.0 %collective-permute-start.8 = (bf16[2,256,1024]{2,1,0:T(8,128)(2,1)}, bf16[2,256,1024]{2,1,0:T(8,128)(2,1)}, u32[]{:S(2)}, u32[]{:S(2)}) collective-permute-start(bf16[2,256,1024]{2,1,0:T(8,128)(2,1)} %get-tuple-element.71), channel_id=1, source_target_pairs={{16,18},{17,19},{18,16},{19,17},{20,22},{21,23},{22,20},{23,21},{2... | collective-permute-start | bytes 3145736 | tf_op jit(solution)/shard_map/ppermute | solution.py:231
  68.8 3.6 %copy-start.16 = (bf16[256,1024]{1,0:T(8,128)(2,1)}, bf16[256,1024]{1,0:T(8,128)(2,1)S(1)}, u32[]{:S(2)}) copy-start(bf16[256,1024]{1,0:T(8,128)(2,1)S(1)} %collective-permute-done.10.refs_1_) | copy-start | bytes 1572868
  68.8 2.8 %collective-permute-start.11 = (bf16[256,1024]{1,0:T(8,128)(2,1)}, bf16[256,1024]{1,0:T(8,128)(2,1)S(1)}, u32[]{:S(2)}, u32[]{:S(2)}) collective-permute-start(bf16[256,1024]{1,0:T(8,128)(2,1)} %collective-permute-done.9.refs_0_), channel_id=1, source_target_pairs={{0,1},{1,0},{2,3},{3,2},{4,5},{5,4},{6,7},{7,6},{8,9},{9,8},{10,11... | collective-permute-start | bytes 1572872 | tf_op jit(solution)/shard_map/ppermute | solution.py:231
  68.8 3.6 %collective-permute-start.13 = (bf16[256,1024]{1,0:T(8,128)(2,1)S(1)}, bf16[256,1024]{1,0:T(8,128)(2,1)S(1)}, u32[]{:S(2)}, u32[]{:S(2)}) collective-permute-start(bf16[256,1024]{1,0:T(8,128)(2,1)S(1)} %collective-permute-done.10.refs_1_), channel_id=1, source_target_pairs={{0,1},{1,0},{2,3},{3,2},{4,5},{5,4},{6,7},{7,6},{8,9},{9,8},{10,11... | collective-permute-start | bytes 1572872 | tf_op jit(solution)/shard_map/ppermute | solution.py:231
  69.3 16.8 %collective-permute-start.15 = (bf16[256,1024]{1,0:T(8,128)(2,1)}, bf16[256,1024]{1,0:T(8,128)(2,1)S(1)}, u32[]{:S(2)}, u32[]{:S(2)}) collective-permute-start(bf16[256,1024]{1,0:T(8,128)(2,1)} %get-tuple-element.83), channel_id=1, source_target_pairs={{0,0},{1,4},{2,2},{3,6},{4,1},{5,5},{6,3},{7,7},{8,8},{9,12},{10,1... | collective-permute-start | bytes 1572872 | tf_op jit(solution)/shard_map/ppermute | solution.py:231
  72.5 26.3 %collective-permute-start.19 = (bf16[256,1024]{1,0:T(8,128)(2,1)}, bf16[256,1024]{1,0:T(8,128)(2,1)S(1)}, u32[]{:S(2)}, u32[]{:S(2)}) collective-permute-start(bf16[256,1024]{1,0:T(8,128)(2,1)} %get-tuple-element.87), channel_id=1, source_target_pairs={{0,8},{1,12},{2,10},{3,14},{4,9},{5,13},{6,11},{7,15},{8,0},{9,4},... | collective-permute-start | bytes 1572872 | tf_op jit(solution)/shard_map/ppermute | solution.py:231
  73.3 27.4 %collective-permute-start.18 = (bf16[256,1024]{1,0:T(8,128)(2,1)}, bf16[256,1024]{1,0:T(8,128)(2,1)S(1)}, u32[]{:S(2)}, u32[]{:S(2)}) collective-permute-start(bf16[256,1024]{1,0:T(8,128)(2,1)} %collective-permute-done.9.refs_0_), channel_id=1, source_target_pairs={{0,2},{1,3},{2,0},{3,1},{4,6},{5,7},{6,4},{7,5},{8,10},{9,11},{10,... | collective-permute-start | bytes 1572872 | tf_op jit(solution)/shard_map/ppermute | solution.py:231
  73.8 28.1 %collective-permute-start.20 = (bf16[256,1024]{1,0:T(8,128)(2,1)}, bf16[256,1024]{1,0:T(8,128)(2,1)S(1)}, u32[]{:S(2)}, u32[]{:S(2)}) collective-permute-start(bf16[256,1024]{1,0:T(8,128)(2,1)} %copy-done.16), channel_id=1, source_target_pairs={{0,2},{1,3},{2,0},{3,1},{4,6},{5,7},{6,4},{7,5},{8,10},{9,11},{10,... | collective-permute-start | bytes 1572872 | tf_op jit(solution)/shard_map/ppermute | solution.py:231
  75.3 1.1 copy-start.17
  76.4 1.0 copy-start.19
  77.4 1.0 copy-start.21
  98.8 3.3 %collective-permute-start.22 = (bf16[256,1024]{1,0:T(8,128)(2,1)S(1)}, bf16[256,1024]{1,0:T(8,128)(2,1)S(1)}, u32[]{:S(2)}, u32[]{:S(2)}) collective-permute-start(bf16[256,1024]{1,0:T(8,128)(2,1)S(1)} %collective-permute-done.15.refs_0_), channel_id=1, source_target_pairs={{0,1},{1,0},{2,3},{3,2},{4,5},{5,4},{6,7},{7,6},{8,9},{9,8},{10,11... | collective-permute-start | bytes 1572872 | tf_op jit(solution)/shard_map/ppermute | solution.py:231
  98.8 29.1 %collective-permute-start.17 = (bf16[2,256,1024]{2,1,0:T(8,128)(2,1)}, bf16[2,256,1024]{2,1,0:T(8,128)(2,1)}, u32[]{:S(2)}, u32[]{:S(2)}) collective-permute-start(bf16[2,256,1024]{2,1,0:T(8,128)(2,1)} %copy-done.22), channel_id=1, source_target_pairs={{16,2},{17,3},{18,0},{19,1},{20,6},{21,7},{22,4},{23,5},{24,10},{2... | collective-permute-start | bytes 3145736 | tf_op jit(solution)/shard_map/ppermute | solution.py:231
  100.1 3.3 %collective-permute-start.23 = (bf16[256,1024]{1,0:T(8,128)(2,1)S(1)}, bf16[256,1024]{1,0:T(8,128)(2,1)S(1)}, u32[]{:S(2)}, u32[]{:S(2)}) collective-permute-start(bf16[256,1024]{1,0:T(8,128)(2,1)S(1)} %collective-permute-done.19.refs_1_), channel_id=1, source_target_pairs={{0,1},{1,0},{2,3},{3,2},{4,5},{5,4},{6,7},{7,6},{8,9},{9,8},{10,11... | collective-permute-start | bytes 1572872 | tf_op jit(solution)/shard_map/ppermute | solution.py:231
  100.7 48.4 %collective-permute-start.14 = (bf16[2,256,1024]{2,1,0:T(8,128)(2,1)}, bf16[2,256,1024]{2,1,0:T(8,128)(2,1)}, u32[]{:S(2)}, u32[]{:S(2)}) collective-permute-start(bf16[2,256,1024]{2,1,0:T(8,128)(2,1)} %shard_map.83), channel_id=1, source_target_pairs={{16,0},{17,1},{18,2},{19,3},{20,4},{21,5},{22,6},{23,7},{24,8},{25... | collective-permute-start | bytes 3145736 | tf_op jit(solution)/shard_map/ppermute | solution.py:231
  102.0 2.8 %collective-permute-start.21 = (bf16[256,1024]{1,0:T(8,128)(2,1)S(1)}, bf16[256,1024]{1,0:T(8,128)(2,1)S(1)}, u32[]{:S(2)}, u32[]{:S(2)}) collective-permute-start(bf16[256,1024]{1,0:T(8,128)(2,1)S(1)} %collective-permute-done.18.refs_0_), channel_id=1, source_target_pairs={{0,1},{1,0},{2,3},{3,2},{4,5},{5,4},{6,7},{7,6},{8,9},{9,8},{10,11... | collective-permute-start | bytes 1572872 | tf_op jit(solution)/shard_map/ppermute | solution.py:231
  102.9 10.2 %collective-permute-start.24 = (bf16[256,1024]{1,0:T(8,128)(2,1)S(1)}, bf16[256,1024]{1,0:T(8,128)(2,1)}, u32[]{:S(2)}, u32[]{:S(2)}) collective-permute-start(bf16[256,1024]{1,0:T(8,128)(2,1)S(1)} %collective-permute-done.20.refs_1_), channel_id=1, source_target_pairs={{0,1},{1,0},{2,3},{3,2},{4,5},{5,4},{6,7},{7,6},{8,9},{9,8},{10,11... | collective-permute-start | bytes 1572872 | tf_op jit(solution)/shard_map/ppermute | solution.py:231
  104.2 34.6 %collective-permute-start.16 = (bf16[256,1024]{1,0:T(8,128)(2,1)S(1)}, bf16[256,1024]{1,0:T(8,128)(2,1)}, u32[]{:S(2)}, u32[]{:S(2)}) collective-permute-start(bf16[256,1024]{1,0:T(8,128)(2,1)S(1)} %collective-permute-done.15.refs_0_), channel_id=1, source_target_pairs={{0,2},{1,3},{2,0},{3,1},{4,6},{5,7},{6,4},{7,5},{8,10},{9,11},{10,... | collective-permute-start | bytes 1572872 | tf_op jit(solution)/shard_map/ppermute | solution.py:231
  105.5 45.6 %collective-permute-start.25 = (bf16[256,1024]{1,0:T(8,128)(2,1)S(1)}, bf16[256,1024]{1,0:T(8,128)(2,1)}, u32[]{:S(2)}, u32[]{:S(2)}) collective-permute-start(bf16[256,1024]{1,0:T(8,128)(2,1)S(1)} %collective-permute-done.19.refs_1_), channel_id=1, source_target_pairs={{0,2},{1,3},{2,0},{3,1},{4,6},{5,7},{6,4},{7,5},{8,10},{9,11},{10,... | collective-permute-start | bytes 1572872 | tf_op jit(solution)/shard_map/ppermute | solution.py:231
  107.0 1.0 copy-start.11
  108.1 1.0 copy-start.13
  109.1 3.9 %copy-start.15 = (bf16[256,1024]{1,0:T(8,128)(2,1)S(1)}, bf16[256,1024]{1,0:T(8,128)(2,1)}, u32[]{:S(2)}) copy-start(bf16[256,1024]{1,0:T(8,128)(2,1)} %copy-done.14) | copy-start | bytes 1572868
  138.8 12.3 %collective-permute-start.26 = (bf16[256,1024]{1,0:T(8,128)(2,1)}, bf16[256,1024]{1,0:T(8,128)(2,1)S(1)}, u32[]{:S(2)}, u32[]{:S(2)}) collective-permute-start(bf16[256,1024]{1,0:T(8,128)(2,1)} %collective-permute-done.16.refs_0_), channel_id=1, source_target_pairs={{0,1},{1,0},{2,3},{3,2},{4,5},{5,4},{6,7},{7,6},{8,9},{9,8},{10,11... | collective-permute-start | bytes 1572872 | tf_op jit(solution)/shard_map/ppermute | solution.py:231
  151.1 2.1 %collective-permute-start.27 = (bf16[256,1024]{1,0:T(8,128)(2,1)}, bf16[256,1024]{1,0:T(8,128)(2,1)S(1)}, u32[]{:S(2)}, u32[]{:S(2)}) collective-permute-start(bf16[256,1024]{1,0:T(8,128)(2,1)} %collective-permute-done.25.refs_1_), channel_id=1, source_target_pairs={{0,1},{1,0},{2,3},{3,2},{4,5},{5,4},{6,7},{7,6},{8,9},{9,8},{10,11... | collective-permute-start | bytes 1572872 | tf_op jit(solution)/shard_map/ppermute | solution.py:231
  (6 other events, 4.8 us)

commit v4 on v3

v4 whole, which is shorter than its diff:
```python
import jax
import jax.numpy as jnp
from jax import lax
from jax.experimental import pallas as pl
from jax.experimental.pallas import tpu as pltpu
from jax.sharding import PartitionSpec as P

BLOCK = 128
TILE = 512
MIB = 1024 * 1024
VMEM_MIB = 60
PARAMS = pltpu.CompilerParams(vmem_limit_bytes=VMEM_MIB * MIB)
LIGHT = pl.CostEstimate(flops=0, bytes_accessed=0, transcendentals=0)


def turned_kernel(slots, *refs):
    for k, ref in enumerate(refs[:-1]):
        refs[-1][slots[k]] = ref[...].T


def turned(slots, grads):
    tokens, columns = grads[0].shape
    return pl.pallas_call(
        turned_kernel,
        grid_spec=pltpu.PrefetchScalarGridSpec(
            num_scalar_prefetch=1,
            grid=(1,),
            in_specs=[pl.BlockSpec((tokens, columns), lambda i, slots: (0, 0)) for _ in grads],
            out_specs=pl.BlockSpec((4, columns, tokens), lambda i, slots: (0, 0, 0)),
        ),
        out_shape=jax.ShapeDtypeStruct((4, columns, tokens), jnp.bfloat16),
        compiler_params=PARAMS,
        cost_estimate=LIGHT,
    )(slots, *grads)


def across_dot(a, b):
    return lax.dot_general(a, b, (((1,), (1,)), ((), ())), preferred_element_type=jnp.float32)


def input_grad_kernel(m, *refs):
    groups = (len(refs) - 6) // 2
    owns, others = refs[:groups], refs[groups : 2 * groups]
    own2_ref, own0_ref, other2_ref, other0_ref, a_ref, m_ref = refs[2 * groups :]
    for n in range(groups):
        own, other = owns[n][...], others[n][...]
        a = across_dot(own, own2_ref[...]) + across_dot(other, other2_ref[...])
        a_ref[n] = a.astype(a_ref.dtype)
        b = across_dot(own, own0_ref[...]) + across_dot(other, other0_ref[...])
        m_ref[n] = b.astype(m_ref.dtype)


def input_grad(m, owns, others, weights, other_weights, parts, kept):
    tokens, columns = owns[0].shape
    groups = len(owns)
    share = weights.shape[0] // parts
    tile = share // 2
    in_specs = [pl.BlockSpec((tokens, columns), lambda i, m: (0, 0)) for _ in range(2 * groups)]
    in_specs += [pl.BlockSpec((tile, columns), lambda i, m, k=k: ((m[0] ^ k) * 2 + i, 0)) for k in (2, 0, 2, 0)]
    out = pl.BlockSpec((groups, tokens, tile), lambda i, m: (0, 0, i))
    return pl.pallas_call(
        input_grad_kernel,
        grid_spec=pltpu.PrefetchScalarGridSpec(
            num_scalar_prefetch=1, grid=(share // tile,), in_specs=in_specs, out_specs=[out, out]
        ),
        out_shape=[jax.ShapeDtypeStruct((groups, tokens, share), t) for t in (jnp.bfloat16, kept)],
        compiler_params=PARAMS,
        cost_estimate=LIGHT,
    )(jnp.reshape(m, (1,)).astype(jnp.int32), *owns, *others, weights, weights, other_weights, other_weights)


def chosen_kernel(flag, here_ref, there_ref, a_ref, b_ref):
    @pl.when(flag[0] == 1)
    def _():
        a_ref[...] = here_ref[...]
        b_ref[...] = there_ref[...]

    @pl.when(flag[0] == 0)
    def _():
        a_ref[...] = there_ref[...]
        b_ref[...] = here_ref[...]


def chosen(flag, run, here, there, runs):
    tokens, width = there.shape
    width = width // runs
    block = (tokens // 2, width)
    return pl.pallas_call(
        chosen_kernel,
        grid_spec=pltpu.PrefetchScalarGridSpec(
            num_scalar_prefetch=1,
            grid=(2,),
            in_specs=[pl.BlockSpec(block, lambda i, flag: (i, flag[1]))] * 2,
            out_specs=[pl.BlockSpec(block, lambda i, flag: (i, 0))] * 2,
        ),
        out_shape=[jax.ShapeDtypeStruct((tokens, width), here.dtype)] * 2,
        compiler_params=PARAMS,
        cost_estimate=LIGHT,
    )(jnp.stack([flag.astype(jnp.int32), run.astype(jnp.int32)]), here, there)


def summed_kernel(a_ref, b_ref, out_ref):
    out_ref[...] = (a_ref[...].astype(jnp.float32) + b_ref[...].astype(jnp.float32)).astype(out_ref.dtype)


def summed(a, b):
    block = pl.BlockSpec((1, *a.shape[1:]), lambda i: (i, 0, 0))
    return pl.pallas_call(
        summed_kernel,
        grid=(a.shape[0],),
        in_specs=[block, block],
        out_specs=block,
        out_shape=jax.ShapeDtypeStruct(a.shape, jnp.bfloat16),
        compiler_params=PARAMS,
        cost_estimate=LIGHT,
    )(a, b)


def weight_grad_kernel(at, *refs):
    lefts, grads_ref = refs[:4], refs[4]
    mantissa_ref, scale_ref = refs[-2:]
    top = total = None
    for i, left in enumerate(lefts):
        part = jnp.dot(grads_ref[i], left[...], preferred_element_type=jnp.float32)
        total = part if total is None else total + part
        top = jnp.abs(part) if top is None else jnp.maximum(top, jnp.abs(part))
    columns, rows = top.shape
    blocks = columns // BLOCK
    scale = jnp.max(top.reshape(blocks, BLOCK, rows), axis=1) + 1e-6
    for k in range(2):
        scale_ref[k] = scale[k * (blocks // 2) : (k + 1) * (blocks // 2)]
    inverse = 1.0 / scale
    scaled = [
        (total[b * BLOCK : (b + 1) * BLOCK] * inverse[b : b + 1]).astype(jnp.bfloat16) for b in range(blocks)
    ]
    half = blocks // 2
    mantissa_ref[:, 0, :] = jnp.concatenate(scaled[:half], axis=0).T
    mantissa_ref[:, 1, :] = jnp.concatenate(scaled[half:], axis=0).T


def weight_grad(at, lefts, grads, into, row_total):
    columns = grads.shape[1]
    tokens, rows = lefts[0].shape
    in_specs = [pl.BlockSpec((tokens, TILE), lambda i, at: (0, i)) for _ in lefts]
    in_specs.append(pl.BlockSpec(grads.shape, lambda i, at: (0, 0, 0)))
    operands = [*lefts, grads]
    aliases = {}
    for n, held in enumerate(into):
        in_specs.append(pl.BlockSpec(memory_space=pl.ANY))
        operands.append(held)
        aliases[len(operands)] = n
    return pl.pallas_call(
        weight_grad_kernel,
        grid_spec=pltpu.PrefetchScalarGridSpec(
            num_scalar_prefetch=1,
            grid=(rows // TILE,),
            in_specs=in_specs,
            out_specs=[
                pl.BlockSpec((TILE, 2, columns // 2), lambda i, at: (at[0] + i, 0, 0)),
                pl.BlockSpec((2, columns // BLOCK // 2, TILE), lambda i, at: (0, 0, at[0] + i)),
            ],
        ),
        out_shape=[
            jax.ShapeDtypeStruct((row_total, 2, columns // 2), jnp.bfloat16),
            jax.ShapeDtypeStruct((2, columns // BLOCK // 2, row_total), jnp.float32),
        ],
        input_output_aliases=aliases,
        compiler_params=PARAMS,
        cost_estimate=LIGHT,
    )(at, *operands)


def rows_placed_kernel(at, mantissa_ref, scale_ref, held_m, held_s, out_m_ref, out_s_ref):
    out_m_ref[...] = mantissa_ref[...]
    out_s_ref[...] = scale_ref[...]


def rows_placed(at, part, into):
    mantissa, scale = part
    rows, pair, columns = mantissa.shape
    tile = TILE
    blocks = scale.shape[1]
    return pl.pallas_call(
        rows_placed_kernel,
        grid_spec=pltpu.PrefetchScalarGridSpec(
            num_scalar_prefetch=1,
            grid=(rows // tile,),
            in_specs=[
                pl.BlockSpec((tile, pair, columns), lambda i, at: (i, 0, 0)),
                pl.BlockSpec((2, blocks, tile), lambda i, at: (0, 0, i)),
                pl.BlockSpec(memory_space=pl.ANY),
                pl.BlockSpec(memory_space=pl.ANY),
            ],
            out_specs=[
                pl.BlockSpec((tile, pair, columns), lambda i, at: (at[0] + i, 0, 0)),
                pl.BlockSpec((2, blocks, tile), lambda i, at: (0, 0, at[0] + i)),
            ],
        ),
        out_shape=[jax.ShapeDtypeStruct(held.shape, held.dtype) for held in into],
        input_output_aliases={3: 0, 4: 1},
        compiler_params=PARAMS,
        cost_estimate=LIGHT,
    )(at, mantissa, scale, *into)


def placed_kernel(group, *refs):
    terms, out_ref = refs[:-1], refs[-1]
    if len(terms) == 1:
        out_ref[...] = terms[0][0]
    else:
        out_ref[...] = (terms[0][0].astype(jnp.float32) + terms[1][0].astype(jnp.float32)).astype(jnp.bfloat16)


def placed_again_kernel(group, *refs):
    placed_kernel(group, *refs[:-2], refs[-1])


def placed(group, first, terms, into, groups):
    some, tokens, width = terms[0].shape
    in_specs = [pl.BlockSpec((1, tokens, width), lambda i, group: (i, 0, 0)) for _ in terms]
    operands = list(terms)
    aliases = {}
    if into is not None:
        in_specs.append(pl.BlockSpec(memory_space=pl.ANY))
        operands.append(into)
        aliases[len(operands)] = 0
    return pl.pallas_call(
        placed_kernel if into is None else placed_again_kernel,
        grid_spec=pltpu.PrefetchScalarGridSpec(
            num_scalar_prefetch=1,
            grid=(some,),
            in_specs=in_specs,
            out_specs=pl.BlockSpec((tokens, width), lambda i, group: (group[0] ^ (first + i), 0)),
        ),
        out_shape=jax.ShapeDtypeStruct((groups * tokens, width), jnp.bfloat16),
        input_output_aliases=aliases,
        compiler_params=PARAMS,
        cost_estimate=LIGHT,
    )(jnp.reshape(group, (1,)).astype(jnp.int32), *operands)


def on_device(layer_input, kv_cotangent, kv_weight):
    n_pipe, n_dp, n_mp = (lax.axis_size(a) for a in ("pipe", "dp", "mp"))
    p, m = lax.axis_index("dp"), lax.axis_index("mp")
    features = layer_input[0]
    tokens, width = features.shape
    columns = 2 * kv_cotangent.shape[3]
    rows = kv_weight.shape[1]
    share = rows // n_mp

    def move(x, where):
        pairs = []
        for s in range(n_pipe):
            for i in range(n_dp):
                for j in range(n_mp):
                    to = where(s, i, j)
                    if to is not None:
                        pairs.append(((s * n_dp + i) * n_mp + j, (to[0] * n_dp + to[1]) * n_mp + to[2]))
        return lax.ppermute(x, ("pipe", "dp", "mp"), pairs)

    def across(x):
        return move(x, lambda s, i, j: (s, i, j ^ 2))

    def other_core(x):
        return move(x, lambda s, i, j: (s, i, j ^ 1))

    def near(x, other):
        return move(x, lambda s, i, j: (s, 2 * (i // 2) + j % 2, 2 * (j // 2) + (i + other) % 2))

    def far(x, other):
        return move(x, lambda s, i, j: (s, 2 * (1 - i // 2) + j % 2, 2 * (j // 2) + (i + other) % 2))

    def across(x):
        return move(x, lambda s, i, j: (s, i, j ^ 2))

    def behind(x):
        return move(x, lambda s, i, j: (s - 1, i, j) if s else None)

    def behind_across(x):
        return move(x, lambda s, i, j: (s - 1, i, j ^ 2) if s else None)

    def across_but_first(x):
        return move(x, lambda s, i, j: (s, i, j ^ 2) if s else None)

    same = (m ^ p) & 1
    slots = jnp.where(same == 0, jnp.array([0, 1, 2, 3], jnp.int32), jnp.array([1, 0, 3, 2], jnp.int32))
    own_side = (m // 2) == (p // 2)
    half = width // 2
    run = half // 2
    core = m & 1
    direct_at = jnp.where(own_side, 0, half)
    crossed_at = jnp.where(own_side, half, 0)

    def tile_at(first):
        return jnp.reshape(first // TILE, (1,)).astype(jnp.int32)

    last = []

    def now(x):
        return lax.optimization_barrier((x, *last))[0] if last else x

    def ran(x):
        last[:] = [x]

    def step(x):
        x = now(x)
        ran(x)
        return x

    def group(k, x):
        return move(x, lambda s, i, j: (s, i ^ k, j))

    g0 = kv_cotangent[0].reshape(tokens, columns)
    own_w = step(kv_weight[0].reshape(rows, columns))
    other_raw = step(other_core(kv_weight))
    g0_core = step(other_core(g0))
    other_w = step(other_raw[0].reshape(rows, columns))
    g1 = step(group(1, g0))
    g2 = step(group(2, g0))
    g1_core = step(other_core(g1))
    a_early, m_early = input_grad(
        m, (now(g0), g1), (g0_core, g1_core), own_w, other_w, n_mp, jnp.float32
    )
    ran(a_early)
    there = step(across(features[:, half:]))
    near0_sent, far0_sent = chosen(own_side, p & 1, features, now(there), 2)
    ran(near0_sent)
    g3 = step(group(3, g0))
    near1_sent, far1_sent = chosen(own_side, (p + 1) & 1, features, now(there), 2)
    ran(near1_sent)
    g2_core = step(other_core(g2))
    near1_begun = near(now(near1_sent), 1)
    g3_core = step(other_core(g3))
    a_late, m_late = input_grad(
        m, (now(g2), g3), (g2_core, g3_core), own_w, other_w, n_mp, jnp.bfloat16
    )
    ran(a_late)
    far1_begun = far(now(far1_sent), 1)
    near0 = step(near(near0_sent, 0))
    near1 = step(near1_begun)
    near1_x_begun = across(now(near1))
    a_across = step(across_but_first(a_early))
    early_sum = step(summed(now(m_early), a_across))
    far0 = step(far(far0_sent, 0))
    other_turned = step(turned(slots, (now(g0_core), g1_core, g2_core, g3_core)))
    late_across_begun = behind_across(now(a_late))
    late_own = step(behind(m_late))
    own_turned = step(turned(slots, (now(g0), g1, g2, g3)))
    near0_x = step(across(near0))
    near1_x = step(near1_x_begun)
    far1 = step(far1_begun)
    far1_x_begun = across(now(far1))
    direct_m_sent, direct_s_sent = weight_grad(tile_at(0), (now(near0), near1, far0, far1), other_turned, (), run)
    ran(direct_m_sent)
    early_begun = behind(now(early_sum))
    out = weight_grad(tile_at(direct_at + core * run), (now(near0), near1, far0, far1), own_turned, (), rows)
    ran(out[0])
    far0_x = step(across(far0))
    late_across = step(late_across_begun)
    total = step(placed(p, 2, (now(late_own), late_across), None, n_dp))
    far1_x = step(far1_x_begun)
    crossed_m_sent, crossed_s_sent = weight_grad(tile_at(0), (now(near0_x), near1_x, far0_x, far1_x), other_turned, (), run)
    ran(crossed_m_sent)
    out = weight_grad(tile_at(crossed_at + core * run), (now(near0_x), near1_x, far0_x, far1_x), own_turned, out, rows)
    ran(out[0])
    direct_m = step(other_core(direct_m_sent))
    direct_s = step(other_core(direct_s_sent))
    out = rows_placed(tile_at(direct_at + (1 - core) * run), (now(direct_m), direct_s), out)
    ran(out[0])
    early = step(early_begun)
    total = step(placed(p, 0, (now(early),), total, n_dp))
    crossed_m = step(other_core(crossed_m_sent))
    crossed_s = step(other_core(crossed_s_sent))
    out = rows_placed(tile_at(crossed_at + (1 - core) * run), (now(crossed_m), crossed_s), out)
    ran(out[0])
    mantissa, scale = out
    scale = scale.transpose(2, 0, 1)
    return (total[None], mantissa[None], scale[None])


def solution(mesh):
    in_specs = (P("pipe", "dp", "mp"), P("pipe", "dp", None, "mp"), P("pipe", "dp", None, "mp"))
    out_specs = (
        P("pipe", None, ("dp", "mp")),
        P("pipe", "dp", None, "mp"),
        P("pipe", "dp", None, "mp"),
    )
    return jax.shard_map(on_device, mesh=mesh, in_specs=in_specs, out_specs=out_specs, check_vma=False)
```

time: 160 us -> 144 us (0.900)
  waiting for transfers between devices: 58.3 us -> 36.6 us
  Pallas kernels: 42 us -> 54.6 us
  local copies, waits for them, and re-layouts: 28.1 us -> 17 us
  starting transfers between devices: 29.2 us -> 33.2 us
    ppermute x28 -> x25, waiting for transfers between devices: 58.3 us -> 36.6 us  [move(): return lax.ppermute(x, ('pipe', 'dp', 'mp'), pairs)]
    unnamed x55 -> x45, local copies, waits for them, and re-layouts: 26.1 us -> 14.7 us
    pallas_call x2, Pallas kernels: 6.75 us -> 11.1 us  [input_grad(): pl.pallas_call(input_grad_kernel, grid_spec=pltpu.PrefetchScalarGridSpec(...]
    ppermute x28 -> x25, starting transfers between devices: 29.2 us -> 33.2 us  [move(): return lax.ppermute(x, ('pipe', 'dp', 'mp'), pairs)]
    pallas_call x1 -> x2, Pallas kernels: 3.26 us -> 6.32 us  [turned(): pl.pallas_call(turned_kernel, grid_spec=pltpu.PrefetchScalarGridSpec(num_...]
    pallas_call x1 -> x2, Pallas kernels: 1.88 us -> 4.11 us  [rows_placed(): pl.pallas_call(rows_placed_kernel, grid_spec=pltpu.PrefetchScalarGridSpec...]
  transfers between devices with their start and end apart: 28 -> 25, of which waited for: 8 -> 7; matrix products, arithmetic and copies ran while one was open for 6% -> 9% of each run, Pallas kernels for 23% -> 37%
where the time goes in v4:
time: 144 us; the launch traced here: 143 us
  Pallas kernels  54.6 us (38%)
  waiting for transfers between devices  36.6 us (25%)
  starting transfers between devices  33.2 us (23%)
  local copies, waits for them, and re-layouts  17 us (12%)
    ppermute x25, waiting for transfers between devices, move(): return lax.ppermute(x, ('pipe', 'dp', 'mp'), pairs)  36.6 us
    ppermute x25, starting transfers between devices, move(): return lax.ppermute(x, ('pipe', 'dp', 'mp'), pairs)  33.2 us
    pallas_call x4, Pallas kernels, weight_grad(): pl.pallas_call(weight_grad_kernel, grid_spec=pltpu.PrefetchScalarGridSpec...  20.2 us
    unnamed x45, local copies, waits for them, and re-layouts  14.7 us
    pallas_call x2, Pallas kernels, input_grad(): pl.pallas_call(input_grad_kernel, grid_spec=pltpu.PrefetchScalarGridSpec(...  11.1 us
    pallas_call x2, Pallas kernels, turned(): pl.pallas_call(turned_kernel, grid_spec=pltpu.PrefetchScalarGridSpec(num_...  6.32 us
    pallas_call x2, Pallas kernels, chosen(): pl.pallas_call(chosen_kernel, grid_spec=pltpu.PrefetchScalarGridSpec(num_...  5.53 us
    pallas_call x2, Pallas kernels, placed(): pl.pallas_call(placed_kernel if into is None else placed_again_kernel, gr...  4.67 us
  transfers between devices with their start and end apart: 25, of which 7 were waited for; matrix products, arithmetic and copies ran while one was open for 9% of the time, Pallas kernels for 37%

profile of v4, /device:TPU:0, one launch (start us, length us, event | category | flops | bytes accessed | tf_op | source)
XLA Modules:
  0.0 143.5 jit_solution(8725382103530279278)
XLA Ops:
  1.1 2.3 %slice.4 = bf16[256,2048]{1,0:T(8,128)(2,1)} slice(bf16[256,4096]{1,0:T(8,128)(2,1)} %bitcast.33), slice={[0:256], [2048:4096]} | slice | bytes 2097152 | tf_op jit(solution)/shard_map/slice | solution.py:325
  3.5 2.5 %collective-permute-start.6 = (bf16[256,2048]{1,0:T(8,128)(2,1)}, bf16[256,2048]{1,0:T(8,128)(2,1)S(1)}, u32[]{:S(2)}, u32[]{:S(2)}) collective-permute-start(bf16[256,2048]{1,0:T(8,128)(2,1)} %slice.4), channel_id=1, source_target_pairs={{0,2},{1,3},{2,0},{3,1},{4,6},{5,7},{6,4},{7,5},{8,10},{9,11},{10,... | collective-permute-start | bytes 3145736 | tf_op jit(solution)/shard_map/ppermute | solution.py:259
  6.0 1.0 copy.15
  7.3 1.6 %collective-permute-start = (bf16[256,512]{1,0:T(8,128)(2,1)S(1)}, bf16[256,512]{1,0:T(8,128)(2,1)S(1)}, u32[]{:S(2)}, u32[]{:S(2)}) collective-permute-start(bf16[256,512]{1,0:T(8,128)(2,1)S(1)} %bitcast.40), channel_id=1, source_target_pairs={{0,4},{1,5},{2,6},{3,7},{4,0},{5,1},{6,2},{7,3},{8,12},{9,13},{10,... | collective-permute-start | bytes 786440 | tf_op jit(solution)/shard_map/ppermute | solution.py:259
  8.9 2.6 %collective-permute-start.4 = (bf16[256,512]{1,0:T(8,128)(2,1)S(1)}, bf16[256,512]{1,0:T(8,128)(2,1)S(1)}, u32[]{:S(2)}, u32[]{:S(2)}) collective-permute-start(bf16[256,512]{1,0:T(8,128)(2,1)S(1)} %bitcast.41), channel_id=1, source_target_pairs={{0,8},{1,9},{2,10},{3,11},{4,12},{5,13},{6,14},{7,15},{8,0},{9,1},... | collective-permute-start | bytes 786440 | tf_op jit(solution)/shard_map/ppermute | solution.py:259
  11.4 4.9 %copy.16 = bf16[512,8,2,256]{3,1,2,0:T(8,128)(2,1)} copy(bf16[512,8,2,256]{3,2,1,0:T(2,128)(2,1)} %bitcast.37) | data formatting | bytes 8388608
  16.4 2.9 %copy.17 = bf16[512,8,2,256]{3,1,2,0:T(8,128)(2,1)} copy(bf16[512,8,2,256]{3,2,1,0:T(2,128)(2,1)S(1)} %bitcast.38) | data formatting | bytes 8388608
  19.3 2.0 %collective-permute-done.refs_1_ = bf16[256,512]{1,0:T(8,128)(2,1)S(1)} collective-permute-done((bf16[256,512]{1,0:T(8,128)(2,1)S(1)}, bf16[256,512]{1,0:T(8,128)(2,1)S(1)}, u32[]{:S(2)}, u32[]{:S(2)}) %collective-permute-start) | collective-permute-done | bytes 262176 | tf_op jit(solution)/shard_map/ppermute | solution.py:259
  21.3 2.5 %collective-permute-start.7 = (bf16[256,512]{1,0:T(8,128)(2,1)S(1)}, bf16[256,512]{1,0:T(8,128)(2,1)S(1)}, u32[]{:S(2)}, u32[]{:S(2)}) collective-permute-start(bf16[256,512]{1,0:T(8,128)(2,1)S(1)} %bitcast.42), channel_id=1, source_target_pairs={{0,12},{1,13},{2,14},{3,15},{4,8},{5,9},{6,10},{7,11},{8,4},{9,5},... | collective-permute-start | bytes 786440 | tf_op jit(solution)/shard_map/ppermute | solution.py:259
  23.9 0.7 copy-done.12
  24.6 5.6 %shard_map.76 = (bf16[2,256,1024]{2,1,0:T(8,128)(2,1)}, f32[2,256,1024]{2,1,0:T(8,128)}) custom-call(s32[1]{0:T(128)} %bitcast.1.m, bf16[256,512]{1,0:T(8,128)(2,1)} %bitcast.43, bf16[256,512]{1,0:T(8,128)(2,1)} %copy-done.8, bf16[256,512]{1,0:T(8,128)(2,1)} %copy-done.10, bf16[256,512]{1,0:T(8,128)(2,1)} %copy-done.12, bf16[4096,512]{1,0:T(8,128)(2,1)} %bitcast.24, ...), custom_call_target="tpu_custom_call" | custom-call | tf_op jit(solution)/shard_map/pallas_call | solution.py:61
  30.2 1.6 %collective-permute-start.5 = (bf16[2,256,1024]{2,1,0:T(8,128)(2,1)}, bf16[2,256,1024]{2,1,0:T(8,128)(2,1)}, u32[]{:S(2)}, u32[]{:S(2)}) collective-permute-start(bf16[2,256,1024]{2,1,0:T(8,128)(2,1)} %get-tuple-element.83), channel_id=1, source_target_pairs={{16,18},{17,19},{18,16},{19,17},{20,22},{21,23},{22,20},{23,21},{2... | collective-permute-start | bytes 3145736 | tf_op jit(solution)/shard_map/ppermute | solution.py:259
  32.0 0.6 pad_add_fusion
  32.6 1.0 copy-done
  33.6 2.8 %shard_map.77 = (bf16[256,1024]{1,0:T(8,128)(2,1)}, bf16[256,1024]{1,0:T(8,128)(2,1)}) custom-call(s32[2]{0:T(128)} %get-tuple-element.148.flag, bf16[256,4096]{1,0:T(8,128)(2,1)} %bitcast.34, bf16[256,2048]{1,0:T(8,128)(2,1)} %copy-done), custom_call_target="tpu_custom_call" | custom-call | tf_op jit(solution)/shard_map/pallas_call | solution.py:88
  36.8 1.7 %collective-permute-start.10 = (bf16[256,1024]{1,0:T(8,128)(2,1)}, bf16[256,1024]{1,0:T(8,128)(2,1)S(1)}, u32[]{:S(2)}, u32[]{:S(2)}) collective-permute-start(bf16[256,1024]{1,0:T(8,128)(2,1)} %get-tuple-element.86), channel_id=1, source_target_pairs={{0,0},{1,4},{2,2},{3,6},{4,1},{5,5},{6,3},{7,7},{8,8},{9,12},{10,1... | collective-permute-start | bytes 1572872 | tf_op jit(solution)/shard_map/ppermute | solution.py:259
  38.5 2.7 %shard_map.78 = (bf16[256,1024]{1,0:T(8,128)(2,1)}, bf16[256,1024]{1,0:T(8,128)(2,1)}) custom-call(s32[2]{0:T(128)} %get-tuple-element.147.flag, bf16[256,4096]{1,0:T(8,128)(2,1)} %bitcast.35, bf16[256,2048]{1,0:T(8,128)(2,1)} %copy-done), custom_call_target="tpu_custom_call" | custom-call | tf_op jit(solution)/shard_map/pallas_call | solution.py:88
  41.3 0.6 collective-permute-start.9
  41.9 2.8 %collective-permute-start.16 = (bf16[256,1024]{1,0:T(8,128)(2,1)}, bf16[256,1024]{1,0:T(8,128)(2,1)}, u32[]{:S(2)}, u32[]{:S(2)}) collective-permute-start(bf16[256,1024]{1,0:T(8,128)(2,1)} %get-tuple-element.104), channel_id=1, source_target_pairs={{0,8},{1,12},{2,10},{3,14},{4,9},{5,13},{6,11},{7,15},{8,0},{9,4},... | collective-permute-start | bytes 1572872 | tf_op jit(solution)/shard_map/ppermute | solution.py:259
  44.7 0.7 copy-done.14
  45.4 5.5 %shard_map.79 = (bf16[2,256,1024]{2,1,0:T(8,128)(2,1)}, bf16[2,256,1024]{2,1,0:T(8,128)(2,1)}) custom-call(s32[1]{0:T(128)} %bitcast.1.m, bf16[256,512]{1,0:T(8,128)(2,1)} %copy-done.9, bf16[256,512]{1,0:T(8,128)(2,1)} %copy-done.11, bf16[256,512]{1,0:T(8,128)(2,1)} %copy-done.13, bf16[256,512]{1,0:T(8,128)(2,1)} %copy-done.14, bf16[4096,512]{1,0:T(8,128)(2,1)} %bitcast.26, ...), custom_call_target="tpu_custom_call" | custom-call | tf_op jit(solution)/shard_map/pallas_call | solution.py:61
  50.9 1.3 collective-permute-start.15
  53.2 2.7 %collective-permute-done.9.refs_1_ = bf16[256,1024]{1,0:T(8,128)(2,1)S(1)} collective-permute-done((bf16[256,1024]{1,0:T(8,128)(2,1)}, bf16[256,1024]{1,0:T(8,128)(2,1)S(1)}, u32[]{:S(2)}, u32[]{:S(2)}) %collective-permute-start.9) | collective-permute-done | bytes 524320 | tf_op jit(solution)/shard_map/ppermute | solution.py:259
  56.5 2.7 %shard_map.80 = bf16[2,256,1024]{2,1,0:T(8,128)(2,1)} custom-call(f32[2,256,1024]{2,1,0:T(8,128)} %get-tuple-element.98.a_ref, bf16[2,256,1024]{2,1,0:T(8,128)(2,1)} %collective-permute-done.5.b_ref), custom_call_target="tpu_custom_call" | custom-call | tf_op jit(solution)/shard_map/pallas_call | solution.py:108
  59.2 9.4 %collective-permute-done.16.refs_2_ = bf16[256,1024]{1,0:T(8,128)(2,1)} collective-permute-done((bf16[256,1024]{1,0:T(8,128)(2,1)}, bf16[256,1024]{1,0:T(8,128)(2,1)}, u32[]{:S(2)}, u32[]{:S(2)}) %collective-permute-start.16) | collective-permute-done | bytes 524320 | tf_op jit(solution)/shard_map/ppermute | solution.py:259
  68.6 3.2 %shard_map.81.refs_4_ = bf16[4,512,256]{2,1,0:T(8,128)(2,1)} custom-call(s32[4]{0:T(128)} %broadcast_select_fusion.slots, bf16[256,512]{1,0:T(8,128)(2,1)} %copy-done.10, bf16[256,512]{1,0:T(8,128)(2,1)} %copy-done.12, bf16[256,512]{1,0:T(8,128)(2,1)} %copy-done.13, bf16[256,512]{1,0:T(8,128)(2,1)} %copy-done.14), custom_call_target="tpu_custom_call" | custom-call | tf_op jit(solution)/shard_map/pallas_call | solution.py:23
  71.8 1.3 collective-permute-start.20
  73.1 1.1 collective-permute-start.12
  74.1 5.1 %collective-permute-done.15.refs_0_ = bf16[2,256,1024]{2,1,0:T(8,128)(2,1)} collective-permute-done((bf16[2,256,1024]{2,1,0:T(8,128)(2,1)}, bf16[2,256,1024]{2,1,0:T(8,128)(2,1)}, u32[]{:S(2)}, u32[]{:S(2)}) %collective-permute-start.15) | collective-permute-done | bytes 1048608 | tf_op jit(solution)/shard_map/ppermute | solution.py:259
  79.2 1.2 collective-permute-start.21
  80.4 3.2 %shard_map.82.refs_4_ = bf16[4,512,256]{2,1,0:T(8,128)(2,1)} custom-call(s32[4]{0:T(128)} %broadcast_select_fusion.slots, bf16[256,512]{1,0:T(8,128)(2,1)} %bitcast.44, bf16[256,512]{1,0:T(8,128)(2,1)} %copy-done.8, bf16[256,512]{1,0:T(8,128)(2,1)} %copy-done.9, bf16[256,512]{1,0:T(8,128)(2,1)} %copy-done.11), custom_call_target="tpu_custom_call" | custom-call | tf_op jit(solution)/shard_map/pallas_call | solution.py:23
  83.6 4.6 %collective-permute-done.12.refs_3_ = bf16[256,1024]{1,0:T(8,128)(2,1)} collective-permute-done((bf16[256,1024]{1,0:T(8,128)(2,1)}, bf16[256,1024]{1,0:T(8,128)(2,1)}, u32[]{:S(2)}, u32[]{:S(2)}) %collective-permute-start.12) | collective-permute-done | bytes 524320 | tf_op jit(solution)/shard_map/ppermute | solution.py:259
  88.7 5.0 %shard_map.83 = (bf16[1024,2,256]{2,1,0:T(2,128)(2,1)}, f32[2,2,1024]{2,1,0:T(2,128)}) custom-call(s32[1]{0:T(128)} %constant.67.clone.1.at, bf16[256,1024]{1,0:T(8,128)(2,1)} %copy-done.6, bf16[256,1024]{1,0:T(8,128)(2,1)} %copy-done.7, bf16[256,1024]{1,0:T(8,128)(2,1)} %collective-permute-done.16.refs_2_, ...), custom_call_target="tpu_custom_call" | custom-call | tf_op jit(solution)/shard_map/pallas_call | solution.py:152
  93.7 7.5 %collective-permute-start.18 = (bf16[1024,2,256]{2,1,0:T(2,128)(2,1)}, bf16[1024,2,256]{2,1,0:T(2,128)(2,1)}, u32[]{:S(2)}, u32[]{:S(2)}) collective-permute-start(bf16[1024,2,256]{2,1,0:T(2,128)(2,1)} %get-tuple-element.115), channel_id=1, source_target_pairs={{0,1},{1,0},{2,3},{3,2},{4,5},{5,4},{6,7},{7,6},{8,9},{9,8},{10,11... | collective-permute-start | bytes 3145736 | tf_op jit(solution)/shard_map/ppermute | solution.py:259
  101.2 1.5 %collective-permute-start.17 = (bf16[2,256,1024]{2,1,0:T(8,128)(2,1)}, bf16[2,256,1024]{2,1,0:T(8,128)(2,1)S(1)}, u32[]{:S(2)}, u32[]{:S(2)}) collective-permute-start(bf16[2,256,1024]{2,1,0:T(8,128)(2,1)} %shard_map.80), channel_id=1, source_target_pairs={{16,0},{17,1},{18,2},{19,3},{20,4},{21,5},{22,6},{23,7},{24,8},{25... | collective-permute-start | bytes 3145736 | tf_op jit(solution)/shard_map/ppermute | solution.py:259
  102.6 5.1 %shard_map.84 = (bf16[4096,2,256]{2,1,0:T(2,128)(2,1)}, f32[2,2,4096]{2,1,0:T(2,128)}) custom-call(s32[1]{0:T(128)} %bitcast.8.at, bf16[256,1024]{1,0:T(8,128)(2,1)} %copy-done.6, bf16[256,1024]{1,0:T(8,128)(2,1)} %copy-done.7, bf16[256,1024]{1,0:T(8,128)(2,1)} %collective-permute-done.16.refs_2_, bf16[256,1024]{1,0:T(8,128)(2,1)} %collective-permute-done.12.refs_3_, ...), custom_call_target="tpu_custom_call" | custom-call | tf_op jit(solution)/shard_map/pallas_call | solution.py:152
  107.7 4.7 %collective-permute-done.21.refs_2_ = bf16[256,1024]{1,0:T(8,128)(2,1)S(1)} collective-permute-done((bf16[256,1024]{1,0:T(8,128)(2,1)}, bf16[256,1024]{1,0:T(8,128)(2,1)S(1)}, u32[]{:S(2)}, u32[]{:S(2)}) %collective-permute-start.21) | collective-permute-done | bytes 524320 | tf_op jit(solution)/shard_map/ppermute | solution.py:259
  112.4 2.6 %shard_map.85.refs_1_ = bf16[1024,1024]{1,0:T(8,128)(2,1)} custom-call(s32[1]{0:T(128)} %bitcast.group, bf16[2,256,1024]{2,1,0:T(8,128)(2,1)} %collective-permute-done.15.refs_0_, bf16[2,256,1024]{2,1,0:T(8,128)(2,1)} %collective-permute-done.20.refs_1_), custom_call_target="tpu_custom_call" | custom-call | tf_op jit(solution)/shard_map/pallas_call | solution.py:227
  115.0 8.1 %collective-permute-done.19.refs_3_ = bf16[256,1024]{1,0:T(8,128)(2,1)S(1)} collective-permute-done((bf16[256,1024]{1,0:T(8,128)(2,1)}, bf16[256,1024]{1,0:T(8,128)(2,1)S(1)}, u32[]{:S(2)}, u32[]{:S(2)}) %collective-permute-start.19) | collective-permute-done | bytes 524320 | tf_op jit(solution)/shard_map/ppermute | solution.py:259
  123.2 0.8 copy-done.5
  124.0 5.0 %shard_map.86 = (bf16[1024,2,256]{2,1,0:T(2,128)(2,1)}, f32[2,2,1024]{2,1,0:T(2,128)}) custom-call(s32[1]{0:T(128)} %constant.67.clone.1.at, bf16[256,1024]{1,0:T(8,128)(2,1)} %copy-done.2, bf16[256,1024]{1,0:T(8,128)(2,1)} %copy-done.3, bf16[256,1024]{1,0:T(8,128)(2,1)} %copy-done.4, bf16[256,1024]{1,0:T(8,128)(2,1)} %copy-done.5, ...), custom_call_target="tpu_custom_call" | custom-call | tf_op jit(solution)/shard_map/pallas_call | solution.py:152
  129.6 5.0 %shard_map.87 = (bf16[4096,2,256]{2,1,0:T(2,128)(2,1)}, f32[2,2,4096]{2,1,0:T(2,128)}) custom-call(s32[1]{0:T(128)} %bitcast.7.at, bf16[256,1024]{1,0:T(8,128)(2,1)} %copy-done.2, bf16[256,1024]{1,0:T(8,128)(2,1)} %copy-done.3, bf16[256,1024]{1,0:T(8,128)(2,1)} %copy-done.4, ...), custom_call_target="tpu_custom_call", output_to_operand_aliasing={{0}: (6, {}), {1}: (7, {})} | custom-call | tf_op jit(solution)/shard_map/pallas_call | solution.py:152
  134.7 0.6 copy-done.18
  135.3 2.1 %shard_map.88 = (bf16[4096,2,256]{2,1,0:T(2,128)(2,1)}, f32[2,2,4096]{2,1,0:T(2,128)}) custom-call(s32[1]{0:T(128)} %bitcast.6.at, bf16[1024,2,256]{2,1,0:T(2,128)(2,1)} %collective-permute-done.18.mantissa_ref, f32[2,2,1024]{2,1,0:T(2,128)} %copy-done.18, ...), custom_call_target="tpu_custom_call", output_to_operand_aliasing={{0}: (3, {}), {1}: (4, {})} | custom-call | tf_op jit(solution)/shard_map/pallas_call | solution.py:183
  137.3 1.0 copy-done.15
  138.3 2.0 %shard_map.89 = bf16[1024,1024]{1,0:T(8,128)(2,1)} custom-call(s32[1]{0:T(128)} %bitcast.group, bf16[2,256,1024]{2,1,0:T(8,128)(2,1)} %copy-done.15, bf16[1024,1024]{1,0:T(8,128)(2,1)} %shard_map.85.refs_1_), custom_call_target="tpu_custom_call", output_to_operand_aliasing={{}: (2, {})} | custom-call | tf_op jit(solution)/shard_map/pallas_call | solution.py:227
  140.4 1.0 copy-done.16
  141.4 2.1 %shard_map.90 = (bf16[4096,2,256]{2,1,0:T(2,128)(2,1)}, f32[2,2,4096]{2,1,0:T(2,128)}) custom-call(s32[1]{0:T(128)} %bitcast.10.at, bf16[1024,2,256]{2,1,0:T(2,128)(2,1)} %copy-done.16, f32[2,2,1024]{2,1,0:T(2,128)} %copy-done.17, bf16[4096,2,256]{2,1,0:T(2,128)(2,1)} %get-tuple-element.136.held_m, ...), custom_call_target="tpu_custom_call", output_to_operand_aliasing={{0}: (3, {}), {1}: (4, {})} | custom-call | tf_op jit(solution)/shard_map/pallas_call | solution.py:183
  (65 shorter events, 4.1 us)
Async XLA Ops:
  0.6 15.8 %collective-permute-start.1 = (bf16[1,4096,2,256]{3,2,1,0:T(2,128)(2,1)}, bf16[1,4096,2,256]{3,2,1,0:T(2,128)(2,1)S(1)}, u32[]{:S(2)}, u32[]{:S(2)}) collective-permute-start(bf16[1,4096,2,256]{3,2,1,0:T(2,128)(2,1)} %param.7), channel_id=1, source_target_pairs={{0,1},{1,0},{2,3},{3,2},{4,5},{5,4},{6,7},{7,6},{8,9},{9,8},{10,11... | collective-permute-start | bytes 12582920 | tf_op jit(solution)/shard_map/ppermute | solution.py:259
  3.5 29.1 %collective-permute-start.6 = (bf16[256,2048]{1,0:T(8,128)(2,1)}, bf16[256,2048]{1,0:T(8,128)(2,1)S(1)}, u32[]{:S(2)}, u32[]{:S(2)}) collective-permute-start(bf16[256,2048]{1,0:T(8,128)(2,1)} %slice.4), channel_id=1, source_target_pairs={{0,2},{1,3},{2,0},{3,1},{4,6},{5,7},{6,4},{7,5},{8,10},{9,11},{10,... | collective-permute-start | bytes 3145736 | tf_op jit(solution)/shard_map/ppermute | solution.py:259
  7.0 14.3 %copy-start.1 = (bf16[32,8,2,256]{3,1,2,0:T(8,128)(2,1)}, bf16[32,8,2,256]{3,1,2,0:T(8,128)(2,1)S(1)}, u32[]{:S(2)}) copy-start(bf16[32,8,2,256]{3,1,2,0:T(8,128)(2,1)S(1)} %copy.15) | copy-start | bytes 786436
  7.0 12.3 %collective-permute-start.2 = (bf16[256,512]{1,0:T(8,128)(2,1)S(1)}, bf16[256,512]{1,0:T(8,128)(2,1)S(1)}, u32[]{:S(2)}, u32[]{:S(2)}) collective-permute-start(bf16[256,512]{1,0:T(8,128)(2,1)S(1)} %bitcast.39), channel_id=1, source_target_pairs={{0,1},{1,0},{2,3},{3,2},{4,5},{5,4},{6,7},{7,6},{8,9},{9,8},{10,11... | collective-permute-start | bytes 786440 | tf_op jit(solution)/shard_map/ppermute | solution.py:259
  7.3 14.0 %collective-permute-start = (bf16[256,512]{1,0:T(8,128)(2,1)S(1)}, bf16[256,512]{1,0:T(8,128)(2,1)S(1)}, u32[]{:S(2)}, u32[]{:S(2)}) collective-permute-start(bf16[256,512]{1,0:T(8,128)(2,1)S(1)} %bitcast.40), channel_id=1, source_target_pairs={{0,4},{1,5},{2,6},{3,7},{4,0},{5,1},{6,2},{7,3},{8,12},{9,13},{10,... | collective-permute-start | bytes 786440 | tf_op jit(solution)/shard_map/ppermute | solution.py:259
  8.9 15.0 %collective-permute-start.4 = (bf16[256,512]{1,0:T(8,128)(2,1)S(1)}, bf16[256,512]{1,0:T(8,128)(2,1)S(1)}, u32[]{:S(2)}, u32[]{:S(2)}) collective-permute-start(bf16[256,512]{1,0:T(8,128)(2,1)S(1)} %bitcast.41), channel_id=1, source_target_pairs={{0,8},{1,9},{2,10},{3,11},{4,12},{5,13},{6,14},{7,15},{8,0},{9,1},... | collective-permute-start | bytes 786440 | tf_op jit(solution)/shard_map/ppermute | solution.py:259
  19.3 4.5 %copy-start.10 = (bf16[256,512]{1,0:T(8,128)(2,1)}, bf16[256,512]{1,0:T(8,128)(2,1)S(1)}, u32[]{:S(2)}) copy-start(bf16[256,512]{1,0:T(8,128)(2,1)S(1)} %collective-permute-done.2.refs_2_.refs_0_) | copy-start | bytes 786436
  21.3 2.6 %copy-start.8 = (bf16[256,512]{1,0:T(8,128)(2,1)}, bf16[256,512]{1,0:T(8,128)(2,1)S(1)}, u32[]{:S(2)}) copy-start(bf16[256,512]{1,0:T(8,128)(2,1)S(1)} %collective-permute-done.refs_1_) | copy-start | bytes 786436
  21.3 2.6 %collective-permute-start.3 = (bf16[256,512]{1,0:T(8,128)(2,1)S(1)}, bf16[256,512]{1,0:T(8,128)(2,1)S(1)}, u32[]{:S(2)}, u32[]{:S(2)}) collective-permute-start(bf16[256,512]{1,0:T(8,128)(2,1)S(1)} %collective-permute-done.refs_1_), channel_id=1, source_target_pairs={{0,1},{1,0},{2,3},{3,2},{4,5},{5,4},{6,7},{7,6},{8,9},{9,8},{10,11... | collective-permute-start | bytes 786440 | tf_op jit(solution)/shard_map/ppermute | solution.py:259
  21.3 15.1 %collective-permute-start.7 = (bf16[256,512]{1,0:T(8,128)(2,1)S(1)}, bf16[256,512]{1,0:T(8,128)(2,1)S(1)}, u32[]{:S(2)}, u32[]{:S(2)}) collective-permute-start(bf16[256,512]{1,0:T(8,128)(2,1)S(1)} %bitcast.42), channel_id=1, source_target_pairs={{0,12},{1,13},{2,14},{3,15},{4,8},{5,9},{6,10},{7,11},{8,4},{9,5},... | collective-permute-start | bytes 786440 | tf_op jit(solution)/shard_map/ppermute | solution.py:259
  23.9 8.0 %copy-start.9 = (bf16[256,512]{1,0:T(8,128)(2,1)}, bf16[256,512]{1,0:T(8,128)(2,1)S(1)}, u32[]{:S(2)}) copy-start(bf16[256,512]{1,0:T(8,128)(2,1)S(1)} %collective-permute-done.4.refs_0_.refs_2_) | copy-start | bytes 786436
  23.9 0.7 copy-start.12
  30.2 26.3 %collective-permute-start.5 = (bf16[2,256,1024]{2,1,0:T(8,128)(2,1)}, bf16[2,256,1024]{2,1,0:T(8,128)(2,1)}, u32[]{:S(2)}, u32[]{:S(2)}) collective-permute-start(bf16[2,256,1024]{2,1,0:T(8,128)(2,1)} %get-tuple-element.83), channel_id=1, source_target_pairs={{16,18},{17,19},{18,16},{19,17},{20,22},{21,23},{22,20},{23,21},{2... | collective-permute-start | bytes 3145736 | tf_op jit(solution)/shard_map/ppermute | solution.py:259
  31.8 9.4 %collective-permute-start.8 = (bf16[256,512]{1,0:T(8,128)(2,1)S(1)}, bf16[256,512]{1,0:T(8,128)(2,1)S(1)}, u32[]{:S(2)}, u32[]{:S(2)}) collective-permute-start(bf16[256,512]{1,0:T(8,128)(2,1)S(1)} %collective-permute-done.4.refs_0_.refs_2_), channel_id=1, source_target_pairs={{0,1},{1,0},{2,3},{3,2},{4,5},{5,4},{6,7},{7,6},{8,9},{9,8},{10,11... | collective-permute-start | bytes 786440 | tf_op jit(solution)/shard_map/ppermute | solution.py:259
  32.6 1.0 copy-start
  36.4 8.3 %copy-start.11 = (bf16[256,512]{1,0:T(8,128)(2,1)}, bf16[256,512]{1,0:T(8,128)(2,1)S(1)}, u32[]{:S(2)}) copy-start(bf16[256,512]{1,0:T(8,128)(2,1)S(1)} %collective-permute-done.7.refs_1_.refs_3_) | copy-start | bytes 786436
  36.4 8.3 %collective-permute-start.11 = (bf16[256,512]{1,0:T(8,128)(2,1)S(1)}, bf16[256,512]{1,0:T(8,128)(2,1)S(1)}, u32[]{:S(2)}, u32[]{:S(2)}) collective-permute-start(bf16[256,512]{1,0:T(8,128)(2,1)S(1)} %collective-permute-done.7.refs_1_.refs_3_), channel_id=1, source_target_pairs={{0,1},{1,0},{2,3},{3,2},{4,5},{5,4},{6,7},{7,6},{8,9},{9,8},{10,11... | collective-permute-start | bytes 786440 | tf_op jit(solution)/shard_map/ppermute | solution.py:259
  36.8 15.9 %collective-permute-start.10 = (bf16[256,1024]{1,0:T(8,128)(2,1)}, bf16[256,1024]{1,0:T(8,128)(2,1)S(1)}, u32[]{:S(2)}, u32[]{:S(2)}) collective-permute-start(bf16[256,1024]{1,0:T(8,128)(2,1)} %get-tuple-element.86), channel_id=1, source_target_pairs={{0,0},{1,4},{2,2},{3,6},{4,1},{5,5},{6,3},{7,7},{8,8},{9,12},{10,1... | collective-permute-start | bytes 1572872 | tf_op jit(solution)/shard_map/ppermute | solution.py:259
  41.3 3.4 %copy-start.13 = (bf16[256,512]{1,0:T(8,128)(2,1)}, bf16[256,512]{1,0:T(8,128)(2,1)S(1)}, u32[]{:S(2)}) copy-start(bf16[256,512]{1,0:T(8,128)(2,1)S(1)} %collective-permute-done.8.refs_2_) | copy-start | bytes 786436
  41.3 14.7 %collective-permute-start.9 = (bf16[256,1024]{1,0:T(8,128)(2,1)}, bf16[256,1024]{1,0:T(8,128)(2,1)S(1)}, u32[]{:S(2)}, u32[]{:S(2)}) collective-permute-start(bf16[256,1024]{1,0:T(8,128)(2,1)} %get-tuple-element.91), channel_id=1, source_target_pairs={{0,1},{1,5},{2,3},{3,7},{4,0},{5,4},{6,2},{7,6},{8,9},{9,13},{10,1... | collective-permute-start | bytes 1572872 | tf_op jit(solution)/shard_map/ppermute | solution.py:259
  41.9 10.3 %copy-start.20 = (s32[4]{0:T(128)S(1)}, s32[4]{0:T(128)}, u32[]{:S(2)}) copy-start(s32[4]{0:T(128)} %constant.72.clone) | copy-start | bytes 52
  41.9 26.7 %collective-permute-start.16 = (bf16[256,1024]{1,0:T(8,128)(2,1)}, bf16[256,1024]{1,0:T(8,128)(2,1)}, u32[]{:S(2)}, u32[]{:S(2)}) collective-permute-start(bf16[256,1024]{1,0:T(8,128)(2,1)} %get-tuple-element.104), channel_id=1, source_target_pairs={{0,8},{1,12},{2,10},{3,14},{4,9},{5,13},{6,11},{7,15},{8,0},{9,4},... | collective-permute-start | bytes 1572872 | tf_op jit(solution)/shard_map/ppermute | solution.py:259
  44.7 0.7 copy-start.14
  50.9 28.3 %collective-permute-start.15 = (bf16[2,256,1024]{2,1,0:T(8,128)(2,1)}, bf16[2,256,1024]{2,1,0:T(8,128)(2,1)}, u32[]{:S(2)}, u32[]{:S(2)}) collective-permute-start(bf16[2,256,1024]{2,1,0:T(8,128)(2,1)} %get-tuple-element.103), channel_id=1, source_target_pairs={{16,0},{17,1},{18,2},{19,3},{20,4},{21,5},{22,6},{23,7},{24,8},{25... | collective-permute-start | bytes 3145736 | tf_op jit(solution)/shard_map/ppermute | solution.py:259
  52.7 30.8 %copy-start.6 = (bf16[256,1024]{1,0:T(8,128)(2,1)}, bf16[256,1024]{1,0:T(8,128)(2,1)S(1)}, u32[]{:S(2)}) copy-start(bf16[256,1024]{1,0:T(8,128)(2,1)S(1)} %collective-permute-done.10.refs_0_) | copy-start | bytes 1572868
  52.7 30.8 %collective-permute-start.14 = (bf16[256,1024]{1,0:T(8,128)(2,1)S(1)}, bf16[256,1024]{1,0:T(8,128)(2,1)S(1)}, u32[]{:S(2)}, u32[]{:S(2)}) collective-permute-start(bf16[256,1024]{1,0:T(8,128)(2,1)S(1)} %collective-permute-done.10.refs_0_), channel_id=1, source_target_pairs={{0,2},{1,3},{2,0},{3,1},{4,6},{5,7},{6,4},{7,5},{8,10},{9,11},{10,... | collective-permute-start | bytes 1572872 | tf_op jit(solution)/shard_map/ppermute | solution.py:259
  56.0 27.6 %copy-start.7 = (bf16[256,1024]{1,0:T(8,128)(2,1)}, bf16[256,1024]{1,0:T(8,128)(2,1)S(1)}, u32[]{:S(2)}) copy-start(bf16[256,1024]{1,0:T(8,128)(2,1)S(1)} %collective-permute-done.9.refs_1_) | copy-start | bytes 1572868
  56.0 27.6 %collective-permute-start.13 = (bf16[256,1024]{1,0:T(8,128)(2,1)S(1)}, bf16[256,1024]{1,0:T(8,128)(2,1)S(1)}, u32[]{:S(2)}, u32[]{:S(2)}) collective-permute-start(bf16[256,1024]{1,0:T(8,128)(2,1)S(1)} %collective-permute-done.9.refs_1_), channel_id=1, source_target_pairs={{0,2},{1,3},{2,0},{3,1},{4,6},{5,7},{6,4},{7,5},{8,10},{9,11},{10,... | collective-permute-start | bytes 1572872 | tf_op jit(solution)/shard_map/ppermute | solution.py:259
  71.8 40.6 %collective-permute-start.20 = (bf16[2,256,1024]{2,1,0:T(8,128)(2,1)}, bf16[2,256,1024]{2,1,0:T(8,128)(2,1)}, u32[]{:S(2)}, u32[]{:S(2)}) collective-permute-start(bf16[2,256,1024]{2,1,0:T(8,128)(2,1)} %get-tuple-element.118), channel_id=1, source_target_pairs={{16,2},{17,3},{18,0},{19,1},{20,6},{21,7},{22,4},{23,5},{24,10},{2... | collective-permute-start | bytes 3145736 | tf_op jit(solution)/shard_map/ppermute | solution.py:259
  73.1 15.1 %collective-permute-start.12 = (bf16[256,1024]{1,0:T(8,128)(2,1)}, bf16[256,1024]{1,0:T(8,128)(2,1)}, u32[]{:S(2)}, u32[]{:S(2)}) collective-permute-start(bf16[256,1024]{1,0:T(8,128)(2,1)} %get-tuple-element.101), channel_id=1, source_target_pairs={{0,9},{1,13},{2,11},{3,15},{4,8},{5,12},{6,10},{7,14},{8,1},{9,5},... | collective-permute-start | bytes 1572872 | tf_op jit(solution)/shard_map/ppermute | solution.py:259
  79.2 33.2 %collective-permute-start.21 = (bf16[256,1024]{1,0:T(8,128)(2,1)}, bf16[256,1024]{1,0:T(8,128)(2,1)S(1)}, u32[]{:S(2)}, u32[]{:S(2)}) collective-permute-start(bf16[256,1024]{1,0:T(8,128)(2,1)} %collective-permute-done.16.refs_2_), channel_id=1, source_target_pairs={{0,2},{1,3},{2,0},{3,1},{4,6},{5,7},{6,4},{7,5},{8,10},{9,11},{10,... | collective-permute-start | bytes 1572872 | tf_op jit(solution)/shard_map/ppermute | solution.py:259
  83.6 31.5 %copy-start.2 = (bf16[256,1024]{1,0:T(8,128)(2,1)}, bf16[256,1024]{1,0:T(8,128)(2,1)S(1)}, u32[]{:S(2)}) copy-start(bf16[256,1024]{1,0:T(8,128)(2,1)S(1)} %collective-permute-done.14.refs_0_) | copy-start | bytes 1572868
  83.6 31.4 %copy-start.3 = (bf16[256,1024]{1,0:T(8,128)(2,1)}, bf16[256,1024]{1,0:T(8,128)(2,1)S(1)}, u32[]{:S(2)}) copy-start(bf16[256,1024]{1,0:T(8,128)(2,1)S(1)} %collective-permute-done.13.refs_1_) | copy-start | bytes 1572868
  88.2 35.0 %collective-permute-start.19 = (bf16[256,1024]{1,0:T(8,128)(2,1)}, bf16[256,1024]{1,0:T(8,128)(2,1)S(1)}, u32[]{:S(2)}, u32[]{:S(2)}) collective-permute-start(bf16[256,1024]{1,0:T(8,128)(2,1)} %collective-permute-done.12.refs_3_), channel_id=1, source_target_pairs={{0,2},{1,3},{2,0},{3,1},{4,6},{5,7},{6,4},{7,5},{8,10},{9,11},{10,... | collective-permute-start | bytes 1572872 | tf_op jit(solution)/shard_map/ppermute | solution.py:259
  93.7 41.0 %collective-permute-start.18 = (bf16[1024,2,256]{2,1,0:T(2,128)(2,1)}, bf16[1024,2,256]{2,1,0:T(2,128)(2,1)}, u32[]{:S(2)}, u32[]{:S(2)}) collective-permute-start(bf16[1024,2,256]{2,1,0:T(2,128)(2,1)} %get-tuple-element.115), channel_id=1, source_target_pairs={{0,1},{1,0},{2,3},{3,2},{4,5},{5,4},{6,7},{7,6},{8,9},{9,8},{10,11... | collective-permute-start | bytes 3145736 | tf_op jit(solution)/shard_map/ppermute | solution.py:259
  101.2 36.2 %collective-permute-start.17 = (bf16[2,256,1024]{2,1,0:T(8,128)(2,1)}, bf16[2,256,1024]{2,1,0:T(8,128)(2,1)S(1)}, u32[]{:S(2)}, u32[]{:S(2)}) collective-permute-start(bf16[2,256,1024]{2,1,0:T(8,128)(2,1)} %shard_map.80), channel_id=1, source_target_pairs={{16,0},{17,1},{18,2},{19,3},{20,4},{21,5},{22,6},{23,7},{24,8},{25... | collective-permute-start | bytes 3145736 | tf_op jit(solution)/shard_map/ppermute | solution.py:259
  107.7 21.4 %copy-start.19 = (f32[2,2,1024]{2,1,0:T(2,128)S(1)}, f32[2,2,1024]{2,1,0:T(2,128)}, u32[]{:S(2)}) copy-start(f32[2,2,1024]{2,1,0:T(2,128)} %get-tuple-element.132) | copy-start | bytes 49156
  112.4 10.8 %copy-start.4 = (bf16[256,1024]{1,0:T(8,128)(2,1)}, bf16[256,1024]{1,0:T(8,128)(2,1)S(1)}, u32[]{:S(2)}) copy-start(bf16[256,1024]{1,0:T(8,128)(2,1)S(1)} %collective-permute-done.21.refs_2_) | copy-start | bytes 1572868
  123.2 0.8 copy-start.5
  129.0 11.4 %collective-permute-start.23 = (bf16[1024,2,256]{2,1,0:T(2,128)(2,1)}, bf16[1024,2,256]{2,1,0:T(2,128)(2,1)S(1)}, u32[]{:S(2)}, u32[]{:S(2)}) collective-permute-start(bf16[1024,2,256]{2,1,0:T(2,128)(2,1)} %get-tuple-element.127), channel_id=1, source_target_pairs={{0,1},{1,0},{2,3},{3,2},{4,5},{5,4},{6,7},{7,6},{8,9},{9,8},{10,11... | collective-permute-start | bytes 3145736 | tf_op jit(solution)/shard_map/ppermute | solution.py:259
  129.1 5.6 %collective-permute-start.22 = (f32[2,2,1024]{2,1,0:T(2,128)S(1)}, f32[2,2,1024]{2,1,0:T(2,128)S(1)}, u32[]{:S(2)}, u32[]{:S(2)}) collective-permute-start(f32[2,2,1024]{2,1,0:T(2,128)S(1)} %copy-done.19), channel_id=1, source_target_pairs={{0,1},{1,0},{2,3},{3,2},{4,5},{5,4},{6,7},{7,6},{8,9},{9,8},{10,11... | collective-permute-start | bytes 49160 | tf_op jit(solution)/shard_map/ppermute | solution.py:259
  129.6 10.8 %collective-permute-start.24 = (f32[2,2,1024]{2,1,0:T(2,128)}, f32[2,2,1024]{2,1,0:T(2,128)S(1)}, u32[]{:S(2)}, u32[]{:S(2)}) collective-permute-start(f32[2,2,1024]{2,1,0:T(2,128)} %get-tuple-element.141), channel_id=1, source_target_pairs={{0,1},{1,0},{2,3},{3,2},{4,5},{5,4},{6,7},{7,6},{8,9},{9,8},{10,11... | collective-permute-start | bytes 49160 | tf_op jit(solution)/shard_map/ppermute | solution.py:259
  134.7 0.6 copy-start.18
  137.3 1.0 copy-start.15
  140.4 1.0 copy-start.16
  140.4 1.0 copy-start.17

commit v5 on v4

--- a/solution.py
+++ b/solution.py
@@ -355,9 +355,9 @@
     early_begun = behind(now(early_sum))
     out = weight_grad(tile_at(direct_at + core * run), (now(near0), near1, far0, far1), own_turned, (), rows)
     ran(out[0])
-    far0_x = step(across(far0))
     late_across = step(late_across_begun)
     total = step(placed(p, 2, (now(late_own), late_across), None, n_dp))
+    far0_x = step(across(far0))
     far1_x = step(far1_x_begun)
     crossed_m_sent, crossed_s_sent = weight_grad(tile_at(0), (now(near0_x), near1_x, far0_x, far1_x), other_turned, (), run)
     ran(crossed_m_sent)

time: 144 us -> 155 us (1.076)
  waiting for transfers between devices: 36.6 us -> 57.7 us
  starting transfers between devices: 33.2 us -> 25.4 us
  local copies, waits for them, and re-layouts: 17 us -> 15.1 us
    ppermute x25, waiting for transfers between devices: 36.6 us -> 57.7 us  [move(): return lax.ppermute(x, ('pipe', 'dp', 'mp'), pairs)]
    ppermute x25, starting transfers between devices: 33.2 us -> 25.4 us  [move(): return lax.ppermute(x, ('pipe', 'dp', 'mp'), pairs)]
    unnamed x45 -> x47, local copies, waits for them, and re-layouts: 14.7 us -> 13.8 us
  transfers between devices with their start and end apart: 25 -> 25, of which waited for: 7 -> 9; matrix products, arithmetic and copies ran while one was open for 9% -> 7% of each run, Pallas kernels for 37% -> 34%
where the time goes in v5:
time: 155 us
  waiting for transfers between devices  57.7 us (37%)
  Pallas kernels  54.7 us (35%)
  starting transfers between devices  25.4 us (16%)
  local copies, waits for them, and re-layouts  15.1 us (10%)
    ppermute x25, waiting for transfers between devices, move(): return lax.ppermute(x, ('pipe', 'dp', 'mp'), pairs)  57.7 us
    ppermute x25, starting transfers between devices, move(): return lax.ppermute(x, ('pipe', 'dp', 'mp'), pairs)  25.4 us
    pallas_call x4, Pallas kernels, weight_grad(): pl.pallas_call(weight_grad_kernel, grid_spec=pltpu.PrefetchScalarGridSpec...  20.3 us
    unnamed x47, local copies, waits for them, and re-layouts  13.8 us
    pallas_call x2, Pallas kernels, input_grad(): pl.pallas_call(input_grad_kernel, grid_spec=pltpu.PrefetchScalarGridSpec(...  11.1 us
    pallas_call x2, Pallas kernels, turned(): pl.pallas_call(turned_kernel, grid_spec=pltpu.PrefetchScalarGridSpec(num_...  6.32 us
    pallas_call x2, Pallas kernels, chosen(): pl.pallas_call(chosen_kernel, grid_spec=pltpu.PrefetchScalarGridSpec(num_...  5.43 us
    pallas_call x2, Pallas kernels, placed(): pl.pallas_call(placed_kernel if into is None else placed_again_kernel, gr...  4.5 us
  transfers between devices with their start and end apart: 25, of which 9 were waited for; matrix products, arithmetic and copies ran while one was open for 7% of the time, Pallas kernels for 34%

profile of v5, /device:TPU:0, one launch (start us, length us, event | category | flops | bytes accessed | tf_op | source)
XLA Modules:
  0.0 154.7 jit_solution(8671967449931869263)
XLA Ops:
  0.6 0.5 collective-permute-start.1
  1.1 1.3 slice.4
  2.4 2.6 %collective-permute-start.6 = (bf16[256,2048]{1,0:T(8,128)(2,1)S(1)}, bf16[256,2048]{1,0:T(8,128)(2,1)S(1)}, u32[]{:S(2)}, u32[]{:S(2)}) collective-permute-start(bf16[256,2048]{1,0:T(8,128)(2,1)S(1)} %slice.4), channel_id=1, source_target_pairs={{0,2},{1,3},{2,0},{3,1},{4,6},{5,7},{6,4},{7,5},{8,10},{9,11},{10,... | collective-permute-start | bytes 3145736 | tf_op jit(solution)/shard_map/ppermute | solution.py:259
  5.0 1.0 copy.15
  6.3 1.6 %collective-permute-start = (bf16[256,512]{1,0:T(8,128)(2,1)S(1)}, bf16[256,512]{1,0:T(8,128)(2,1)S(1)}, u32[]{:S(2)}, u32[]{:S(2)}) collective-permute-start(bf16[256,512]{1,0:T(8,128)(2,1)S(1)} %bitcast.40), channel_id=1, source_target_pairs={{0,4},{1,5},{2,6},{3,7},{4,0},{5,1},{6,2},{7,3},{8,12},{9,13},{10,... | collective-permute-start | bytes 786440 | tf_op jit(solution)/shard_map/ppermute | solution.py:259
  7.9 2.6 %collective-permute-start.4 = (bf16[256,512]{1,0:T(8,128)(2,1)S(1)}, bf16[256,512]{1,0:T(8,128)(2,1)S(1)}, u32[]{:S(2)}, u32[]{:S(2)}) collective-permute-start(bf16[256,512]{1,0:T(8,128)(2,1)S(1)} %bitcast.41), channel_id=1, source_target_pairs={{0,8},{1,9},{2,10},{3,11},{4,12},{5,13},{6,14},{7,15},{8,0},{9,1},... | collective-permute-start | bytes 786440 | tf_op jit(solution)/shard_map/ppermute | solution.py:259
  10.5 4.9 %copy.16 = bf16[512,8,2,256]{3,1,2,0:T(8,128)(2,1)} copy(bf16[512,8,2,256]{3,2,1,0:T(2,128)(2,1)} %bitcast.37) | data formatting | bytes 8388608
  15.4 2.9 %copy.17 = bf16[512,8,2,256]{3,1,2,0:T(8,128)(2,1)} copy(bf16[512,8,2,256]{3,2,1,0:T(2,128)(2,1)S(1)} %bitcast.38) | data formatting | bytes 8388608
  18.4 1.9 %collective-permute-done.refs_1_ = bf16[256,512]{1,0:T(8,128)(2,1)S(1)} collective-permute-done((bf16[256,512]{1,0:T(8,128)(2,1)S(1)}, bf16[256,512]{1,0:T(8,128)(2,1)S(1)}, u32[]{:S(2)}, u32[]{:S(2)}) %collective-permute-start) | collective-permute-done | bytes 262176 | tf_op jit(solution)/shard_map/ppermute | solution.py:259
  20.3 2.4 %collective-permute-done.4.refs_0_.refs_2_ = bf16[256,512]{1,0:T(8,128)(2,1)S(1)} collective-permute-done((bf16[256,512]{1,0:T(8,128)(2,1)S(1)}, bf16[256,512]{1,0:T(8,128)(2,1)S(1)}, u32[]{:S(2)}, u32[]{:S(2)}) %collective-permute-start.4) | collective-permute-done | bytes 262176 | tf_op jit(solution)/shard_map/ppermute | solution.py:259
  22.7 0.7 copy-done.14
  23.4 5.6 %shard_map.76 = (bf16[2,256,1024]{2,1,0:T(8,128)(2,1)}, f32[2,256,1024]{2,1,0:T(8,128)}) custom-call(s32[1]{0:T(128)} %bitcast.1.m, bf16[256,512]{1,0:T(8,128)(2,1)} %bitcast.42, bf16[256,512]{1,0:T(8,128)(2,1)} %copy-done.10, bf16[256,512]{1,0:T(8,128)(2,1)} %copy-done.12, bf16[256,512]{1,0:T(8,128)(2,1)} %copy-done.14, bf16[4096,512]{1,0:T(8,128)(2,1)} %bitcast.24, ...), custom_call_target="tpu_custom_call" | custom-call | tf_op jit(solution)/shard_map/pallas_call | solution.py:61
  29.1 1.6 %collective-permute-start.5 = (bf16[2,256,1024]{2,1,0:T(8,128)(2,1)}, bf16[2,256,1024]{2,1,0:T(8,128)(2,1)}, u32[]{:S(2)}, u32[]{:S(2)}) collective-permute-start(bf16[2,256,1024]{2,1,0:T(8,128)(2,1)} %get-tuple-element.83), channel_id=1, source_target_pairs={{16,18},{17,19},{18,16},{19,17},{20,22},{21,23},{22,20},{23,21},{2... | collective-permute-start | bytes 3145736 | tf_op jit(solution)/shard_map/ppermute | solution.py:259
  30.7 2.5 %collective-permute-start.7 = (bf16[256,512]{1,0:T(8,128)(2,1)S(1)}, bf16[256,512]{1,0:T(8,128)(2,1)S(1)}, u32[]{:S(2)}, u32[]{:S(2)}) collective-permute-start(bf16[256,512]{1,0:T(8,128)(2,1)S(1)} %bitcast.44), channel_id=1, source_target_pairs={{0,12},{1,13},{2,14},{3,15},{4,8},{5,9},{6,10},{7,11},{8,4},{9,5},... | collective-permute-start | bytes 786440 | tf_op jit(solution)/shard_map/ppermute | solution.py:259
  33.2 0.6 pad_add_fusion
  33.9 1.0 copy-done
  34.8 2.7 %shard_map.77 = (bf16[256,1024]{1,0:T(8,128)(2,1)}, bf16[256,1024]{1,0:T(8,128)(2,1)}) custom-call(s32[2]{0:T(128)} %get-tuple-element.148.flag, bf16[256,4096]{1,0:T(8,128)(2,1)} %bitcast.34, bf16[256,2048]{1,0:T(8,128)(2,1)} %copy-done), custom_call_target="tpu_custom_call" | custom-call | tf_op jit(solution)/shard_map/pallas_call | solution.py:88
  37.6 2.6 %collective-permute-done.7.refs_1_.refs_3_ = bf16[256,512]{1,0:T(8,128)(2,1)S(1)} collective-permute-done((bf16[256,512]{1,0:T(8,128)(2,1)S(1)}, bf16[256,512]{1,0:T(8,128)(2,1)S(1)}, u32[]{:S(2)}, u32[]{:S(2)}) %collective-permute-start.7) | collective-permute-done | bytes 262176 | tf_op jit(solution)/shard_map/ppermute | solution.py:259
  40.1 1.7 %collective-permute-start.10 = (bf16[256,1024]{1,0:T(8,128)(2,1)}, bf16[256,1024]{1,0:T(8,128)(2,1)S(1)}, u32[]{:S(2)}, u32[]{:S(2)}) collective-permute-start(bf16[256,1024]{1,0:T(8,128)(2,1)} %get-tuple-element.86), channel_id=1, source_target_pairs={{0,0},{1,4},{2,2},{3,6},{4,1},{5,5},{6,3},{7,7},{8,8},{9,12},{10,1... | collective-permute-start | bytes 1572872 | tf_op jit(solution)/shard_map/ppermute | solution.py:259
  41.8 2.7 %shard_map.78 = (bf16[256,1024]{1,0:T(8,128)(2,1)}, bf16[256,1024]{1,0:T(8,128)(2,1)}) custom-call(s32[2]{0:T(128)} %get-tuple-element.147.flag, bf16[256,4096]{1,0:T(8,128)(2,1)} %bitcast.35, bf16[256,2048]{1,0:T(8,128)(2,1)} %copy-done), custom_call_target="tpu_custom_call" | custom-call | tf_op jit(solution)/shard_map/pallas_call | solution.py:88
  44.5 4.7 %collective-permute-start.9 = (bf16[256,1024]{1,0:T(8,128)(2,1)}, bf16[256,1024]{1,0:T(8,128)(2,1)S(1)}, u32[]{:S(2)}, u32[]{:S(2)}) collective-permute-start(bf16[256,1024]{1,0:T(8,128)(2,1)} %get-tuple-element.91), channel_id=1, source_target_pairs={{0,1},{1,5},{2,3},{3,7},{4,0},{5,4},{6,2},{7,6},{8,9},{9,13},{10,1... | collective-permute-start | bytes 1572872 | tf_op jit(solution)/shard_map/ppermute | solution.py:259
  49.6 0.7 copy-done.16
  50.3 5.5 %shard_map.79 = (bf16[2,256,1024]{2,1,0:T(8,128)(2,1)}, bf16[2,256,1024]{2,1,0:T(8,128)(2,1)}) custom-call(s32[1]{0:T(128)} %bitcast.1.m, bf16[256,512]{1,0:T(8,128)(2,1)} %copy-done.11, bf16[256,512]{1,0:T(8,128)(2,1)} %copy-done.13, bf16[256,512]{1,0:T(8,128)(2,1)} %copy-done.15, bf16[256,512]{1,0:T(8,128)(2,1)} %copy-done.16, bf16[4096,512]{1,0:T(8,128)(2,1)} %bitcast.26, ...), custom_call_target="tpu_custom_call" | custom-call | tf_op jit(solution)/shard_map/pallas_call | solution.py:61
  55.8 1.3 collective-permute-start.15
  57.6 0.5 collective-permute-start.14
  58.2 2.9 %collective-permute-done.9.refs_1_ = bf16[256,1024]{1,0:T(8,128)(2,1)S(1)} collective-permute-done((bf16[256,1024]{1,0:T(8,128)(2,1)}, bf16[256,1024]{1,0:T(8,128)(2,1)S(1)}, u32[]{:S(2)}, u32[]{:S(2)}) %collective-permute-start.9) | collective-permute-done | bytes 524320 | tf_op jit(solution)/shard_map/ppermute | solution.py:259
  61.1 2.9 %shard_map.80 = bf16[2,256,1024]{2,1,0:T(8,128)(2,1)} custom-call(f32[2,256,1024]{2,1,0:T(8,128)} %get-tuple-element.98.a_ref, bf16[2,256,1024]{2,1,0:T(8,128)(2,1)} %collective-permute-done.5.b_ref), custom_call_target="tpu_custom_call" | custom-call | tf_op jit(solution)/shard_map/pallas_call | solution.py:108
  64.0 10.3 %collective-permute-done.16.refs_2_ = bf16[256,1024]{1,0:T(8,128)(2,1)S(1)} collective-permute-done((bf16[256,1024]{1,0:T(8,128)(2,1)}, bf16[256,1024]{1,0:T(8,128)(2,1)S(1)}, u32[]{:S(2)}, u32[]{:S(2)}) %collective-permute-start.16) | collective-permute-done | bytes 524320 | tf_op jit(solution)/shard_map/ppermute | solution.py:259
  74.4 3.2 %shard_map.81.refs_4_ = bf16[4,512,256]{2,1,0:T(8,128)(2,1)} custom-call(s32[4]{0:T(128)} %broadcast_select_fusion.slots, bf16[256,512]{1,0:T(8,128)(2,1)} %copy-done.12, bf16[256,512]{1,0:T(8,128)(2,1)} %copy-done.14, bf16[256,512]{1,0:T(8,128)(2,1)} %copy-done.15, bf16[256,512]{1,0:T(8,128)(2,1)} %copy-done.16), custom_call_target="tpu_custom_call" | custom-call | tf_op jit(solution)/shard_map/pallas_call | solution.py:23
  77.5 1.3 collective-permute-start.21
  78.8 0.6 collective-permute-start.13
  79.4 4.4 %collective-permute-done.15.refs_0_ = bf16[2,256,1024]{2,1,0:T(8,128)(2,1)} collective-permute-done((bf16[2,256,1024]{2,1,0:T(8,128)(2,1)}, bf16[2,256,1024]{2,1,0:T(8,128)(2,1)}, u32[]{:S(2)}, u32[]{:S(2)}) %collective-permute-start.15) | collective-permute-done | bytes 1048608 | tf_op jit(solution)/shard_map/ppermute | solution.py:259
  83.8 0.7 collective-permute-start.20
  84.5 3.2 %shard_map.82.refs_4_ = bf16[4,512,256]{2,1,0:T(8,128)(2,1)} custom-call(s32[4]{0:T(128)} %broadcast_select_fusion.slots, bf16[256,512]{1,0:T(8,128)(2,1)} %bitcast.43, bf16[256,512]{1,0:T(8,128)(2,1)} %copy-done.10, bf16[256,512]{1,0:T(8,128)(2,1)} %copy-done.11, bf16[256,512]{1,0:T(8,128)(2,1)} %copy-done.13), custom_call_target="tpu_custom_call" | custom-call | tf_op jit(solution)/shard_map/pallas_call | solution.py:23
  87.7 28.5 %collective-permute-done.13.refs_1_ = bf16[256,1024]{1,0:T(8,128)(2,1)S(1)} collective-permute-done((bf16[256,1024]{1,0:T(8,128)(2,1)S(1)}, bf16[256,1024]{1,0:T(8,128)(2,1)S(1)}, u32[]{:S(2)}, u32[]{:S(2)}) %collective-permute-start.13) | collective-permute-done | bytes 524320 | tf_op jit(solution)/shard_map/ppermute | solution.py:259
  116.7 5.1 %shard_map.83 = (bf16[1024,2,256]{2,1,0:T(2,128)(2,1)}, f32[2,2,1024]{2,1,0:T(2,128)}) custom-call(s32[1]{0:T(128)} %constant.67.clone.1.at, bf16[256,1024]{1,0:T(8,128)(2,1)} %copy-done.7, bf16[256,1024]{1,0:T(8,128)(2,1)} %copy-done.9, bf16[256,1024]{1,0:T(8,128)(2,1)} %copy-done.8, bf16[256,1024]{1,0:T(8,128)(2,1)} %collective-permute-done.12.refs_3_, ...), custom_call_target="tpu_custom_call" | custom-call | tf_op jit(solution)/shard_map/pallas_call | solution.py:152
  121.8 1.5 collective-permute-start.17
  123.3 5.1 %shard_map.84 = (bf16[4096,2,256]{2,1,0:T(2,128)(2,1)}, f32[2,2,4096]{2,1,0:T(2,128)}) custom-call(s32[1]{0:T(128)} %bitcast.8.at, bf16[256,1024]{1,0:T(8,128)(2,1)} %copy-done.7, bf16[256,1024]{1,0:T(8,128)(2,1)} %copy-done.9, bf16[256,1024]{1,0:T(8,128)(2,1)} %copy-done.8, bf16[256,1024]{1,0:T(8,128)(2,1)} %collective-permute-done.12.refs_3_, ...), custom_call_target="tpu_custom_call" | custom-call | tf_op jit(solution)/shard_map/pallas_call | solution.py:152
  128.4 2.5 %shard_map.85.refs_1_ = bf16[1024,1024]{1,0:T(8,128)(2,1)} custom-call(s32[1]{0:T(128)} %bitcast.group, bf16[2,256,1024]{2,1,0:T(8,128)(2,1)} %collective-permute-done.15.refs_0_, bf16[2,256,1024]{2,1,0:T(8,128)(2,1)} %collective-permute-done.21.refs_1_), custom_call_target="tpu_custom_call" | custom-call | tf_op jit(solution)/shard_map/pallas_call | solution.py:227
  130.9 4.4 %collective-permute-done.19.refs_3_ = bf16[256,1024]{1,0:T(8,128)(2,1)S(1)} collective-permute-done((bf16[256,1024]{1,0:T(8,128)(2,1)}, bf16[256,1024]{1,0:T(8,128)(2,1)S(1)}, u32[]{:S(2)}, u32[]{:S(2)}) %collective-permute-start.19) | collective-permute-done | bytes 524320 | tf_op jit(solution)/shard_map/ppermute | solution.py:259
  135.3 0.8 copy-done.6
  136.1 5.0 %shard_map.86 = (bf16[1024,2,256]{2,1,0:T(2,128)(2,1)}, f32[2,2,1024]{2,1,0:T(2,128)}) custom-call(s32[1]{0:T(128)} %constant.67.clone.1.at, bf16[256,1024]{1,0:T(8,128)(2,1)} %copy-done.3, bf16[256,1024]{1,0:T(8,128)(2,1)} %copy-done.4, bf16[256,1024]{1,0:T(8,128)(2,1)} %copy-done.5, bf16[256,1024]{1,0:T(8,128)(2,1)} %copy-done.6, ...), custom_call_target="tpu_custom_call" | custom-call | tf_op jit(solution)/shard_map/pallas_call | solution.py:152
  141.7 5.0 %shard_map.87 = (bf16[4096,2,256]{2,1,0:T(2,128)(2,1)}, f32[2,2,4096]{2,1,0:T(2,128)}) custom-call(s32[1]{0:T(128)} %bitcast.7.at, bf16[256,1024]{1,0:T(8,128)(2,1)} %copy-done.3, bf16[256,1024]{1,0:T(8,128)(2,1)} %copy-done.4, bf16[256,1024]{1,0:T(8,128)(2,1)} %copy-done.5, ...), custom_call_target="tpu_custom_call", output_to_operand_aliasing={{0}: (6, {}), {1}: (7, {})} | custom-call | tf_op jit(solution)/shard_map/pallas_call | solution.py:152
  146.8 0.6 copy-done.19
  147.4 2.1 %shard_map.88 = (bf16[4096,2,256]{2,1,0:T(2,128)(2,1)}, f32[2,2,4096]{2,1,0:T(2,128)}) custom-call(s32[1]{0:T(128)} %bitcast.6.at, bf16[1024,2,256]{2,1,0:T(2,128)(2,1)} %collective-permute-done.18.mantissa_ref, f32[2,2,1024]{2,1,0:T(2,128)} %copy-done.19, ...), custom_call_target="tpu_custom_call", output_to_operand_aliasing={{0}: (3, {}), {1}: (4, {})} | custom-call | tf_op jit(solution)/shard_map/pallas_call | solution.py:183
  149.6 2.0 %shard_map.89 = bf16[1024,1024]{1,0:T(8,128)(2,1)} custom-call(s32[1]{0:T(128)} %bitcast.group, bf16[2,256,1024]{2,1,0:T(8,128)(2,1)} %collective-permute-done.17.refs_0_, bf16[1024,1024]{1,0:T(8,128)(2,1)} %shard_map.85.refs_1_), custom_call_target="tpu_custom_call", output_to_operand_aliasing={{}: (2, {})} | custom-call | tf_op jit(solution)/shard_map/pallas_call | solution.py:227
  151.7 1.0 copy-done.17
  152.7 2.1 %shard_map.90 = (bf16[4096,2,256]{2,1,0:T(2,128)(2,1)}, f32[2,2,4096]{2,1,0:T(2,128)}) custom-call(s32[1]{0:T(128)} %bitcast.10.at, bf16[1024,2,256]{2,1,0:T(2,128)(2,1)} %copy-done.17, f32[2,2,1024]{2,1,0:T(2,128)} %copy-done.18, bf16[4096,2,256]{2,1,0:T(2,128)(2,1)} %get-tuple-element.136.held_m, ...), custom_call_target="tpu_custom_call", output_to_operand_aliasing={{0}: (3, {}), {1}: (4, {})} | custom-call | tf_op jit(solution)/shard_map/pallas_call | solution.py:183
  (67 shorter events, 2.5 us)
Async XLA Ops:
  0.6 14.8 %collective-permute-start.1 = (bf16[1,4096,2,256]{3,2,1,0:T(2,128)(2,1)}, bf16[1,4096,2,256]{3,2,1,0:T(2,128)(2,1)S(1)}, u32[]{:S(2)}, u32[]{:S(2)}) collective-permute-start(bf16[1,4096,2,256]{3,2,1,0:T(2,128)(2,1)} %param.7), channel_id=1, source_target_pairs={{0,1},{1,0},{2,3},{3,2},{4,5},{5,4},{6,7},{7,6},{8,9},{9,8},{10,11... | collective-permute-start | bytes 12582920 | tf_op jit(solution)/shard_map/ppermute | solution.py:259
  2.4 31.4 %collective-permute-start.6 = (bf16[256,2048]{1,0:T(8,128)(2,1)S(1)}, bf16[256,2048]{1,0:T(8,128)(2,1)S(1)}, u32[]{:S(2)}, u32[]{:S(2)}) collective-permute-start(bf16[256,2048]{1,0:T(8,128)(2,1)S(1)} %slice.4), channel_id=1, source_target_pairs={{0,2},{1,3},{2,0},{3,1},{4,6},{5,7},{6,4},{7,5},{8,10},{9,11},{10,... | collective-permute-start | bytes 3145736 | tf_op jit(solution)/shard_map/ppermute | solution.py:259
  6.0 9.4 %copy-start.1 = (bf16[32,8,2,256]{3,1,2,0:T(8,128)(2,1)}, bf16[32,8,2,256]{3,1,2,0:T(8,128)(2,1)S(1)}, u32[]{:S(2)}) copy-start(bf16[32,8,2,256]{3,1,2,0:T(8,128)(2,1)S(1)} %copy.15) | copy-start | bytes 786436
  6.0 12.3 %collective-permute-start.2 = (bf16[256,512]{1,0:T(8,128)(2,1)S(1)}, bf16[256,512]{1,0:T(8,128)(2,1)S(1)}, u32[]{:S(2)}, u32[]{:S(2)}) collective-permute-start(bf16[256,512]{1,0:T(8,128)(2,1)S(1)} %bitcast.39), channel_id=1, source_target_pairs={{0,1},{1,0},{2,3},{3,2},{4,5},{5,4},{6,7},{7,6},{8,9},{9,8},{10,11... | collective-permute-start | bytes 786440 | tf_op jit(solution)/shard_map/ppermute | solution.py:259
  6.3 14.0 %collective-permute-start = (bf16[256,512]{1,0:T(8,128)(2,1)S(1)}, bf16[256,512]{1,0:T(8,128)(2,1)S(1)}, u32[]{:S(2)}, u32[]{:S(2)}) collective-permute-start(bf16[256,512]{1,0:T(8,128)(2,1)S(1)} %bitcast.40), channel_id=1, source_target_pairs={{0,4},{1,5},{2,6},{3,7},{4,0},{5,1},{6,2},{7,3},{8,12},{9,13},{10,... | collective-permute-start | bytes 786440 | tf_op jit(solution)/shard_map/ppermute | solution.py:259
  7.9 14.8 %collective-permute-start.4 = (bf16[256,512]{1,0:T(8,128)(2,1)S(1)}, bf16[256,512]{1,0:T(8,128)(2,1)S(1)}, u32[]{:S(2)}, u32[]{:S(2)}) collective-permute-start(bf16[256,512]{1,0:T(8,128)(2,1)S(1)} %bitcast.41), channel_id=1, source_target_pairs={{0,8},{1,9},{2,10},{3,11},{4,12},{5,13},{6,14},{7,15},{8,0},{9,1},... | collective-permute-start | bytes 786440 | tf_op jit(solution)/shard_map/ppermute | solution.py:259
  18.4 4.3 %copy-start.12 = (bf16[256,512]{1,0:T(8,128)(2,1)}, bf16[256,512]{1,0:T(8,128)(2,1)S(1)}, u32[]{:S(2)}) copy-start(bf16[256,512]{1,0:T(8,128)(2,1)S(1)} %collective-permute-done.2.refs_2_.refs_0_) | copy-start | bytes 786436
  20.3 2.4 %copy-start.10 = (bf16[256,512]{1,0:T(8,128)(2,1)}, bf16[256,512]{1,0:T(8,128)(2,1)S(1)}, u32[]{:S(2)}) copy-start(bf16[256,512]{1,0:T(8,128)(2,1)S(1)} %collective-permute-done.refs_1_) | copy-start | bytes 786436
  20.3 2.4 %collective-permute-start.3 = (bf16[256,512]{1,0:T(8,128)(2,1)S(1)}, bf16[256,512]{1,0:T(8,128)(2,1)S(1)}, u32[]{:S(2)}, u32[]{:S(2)}) collective-permute-start(bf16[256,512]{1,0:T(8,128)(2,1)S(1)} %collective-permute-done.refs_1_), channel_id=1, source_target_pairs={{0,1},{1,0},{2,3},{3,2},{4,5},{5,4},{6,7},{7,6},{8,9},{9,8},{10,11... | collective-permute-start | bytes 786440 | tf_op jit(solution)/shard_map/ppermute | solution.py:259
  22.7 10.5 %copy-start.11 = (bf16[256,512]{1,0:T(8,128)(2,1)}, bf16[256,512]{1,0:T(8,128)(2,1)S(1)}, u32[]{:S(2)}) copy-start(bf16[256,512]{1,0:T(8,128)(2,1)S(1)} %collective-permute-done.4.refs_0_.refs_2_) | copy-start | bytes 786436
  22.7 0.8 copy-start.14
  23.4 7.3 %copy-start.2 = (bf16[32,8,2,256]{3,1,2,0:T(8,128)(2,1)S(1)}, bf16[32,8,2,256]{3,1,2,0:T(8,128)(2,1)}, u32[]{:S(2)}) copy-start(bf16[32,8,2,256]{3,1,2,0:T(8,128)(2,1)} %copy-done.1) | copy-start | bytes 786436
  29.1 32.0 %collective-permute-start.5 = (bf16[2,256,1024]{2,1,0:T(8,128)(2,1)}, bf16[2,256,1024]{2,1,0:T(8,128)(2,1)}, u32[]{:S(2)}, u32[]{:S(2)}) collective-permute-start(bf16[2,256,1024]{2,1,0:T(8,128)(2,1)} %get-tuple-element.83), channel_id=1, source_target_pairs={{16,18},{17,19},{18,16},{19,17},{20,22},{21,23},{22,20},{23,21},{2... | collective-permute-start | bytes 3145736 | tf_op jit(solution)/shard_map/ppermute | solution.py:259
  30.7 9.4 %collective-permute-start.7 = (bf16[256,512]{1,0:T(8,128)(2,1)S(1)}, bf16[256,512]{1,0:T(8,128)(2,1)S(1)}, u32[]{:S(2)}, u32[]{:S(2)}) collective-permute-start(bf16[256,512]{1,0:T(8,128)(2,1)S(1)} %bitcast.44), channel_id=1, source_target_pairs={{0,12},{1,13},{2,14},{3,15},{4,8},{5,9},{6,10},{7,11},{8,4},{9,5},... | collective-permute-start | bytes 786440 | tf_op jit(solution)/shard_map/ppermute | solution.py:259
  33.2 11.3 %collective-permute-start.8 = (bf16[256,512]{1,0:T(8,128)(2,1)S(1)}, bf16[256,512]{1,0:T(8,128)(2,1)S(1)}, u32[]{:S(2)}, u32[]{:S(2)}) collective-permute-start(bf16[256,512]{1,0:T(8,128)(2,1)S(1)} %collective-permute-done.4.refs_0_.refs_2_), channel_id=1, source_target_pairs={{0,1},{1,0},{2,3},{3,2},{4,5},{5,4},{6,7},{7,6},{8,9},{9,8},{10,11... | collective-permute-start | bytes 786440 | tf_op jit(solution)/shard_map/ppermute | solution.py:259
  33.8 1.0 copy-start
  40.1 9.5 %copy-start.13 = (bf16[256,512]{1,0:T(8,128)(2,1)}, bf16[256,512]{1,0:T(8,128)(2,1)S(1)}, u32[]{:S(2)}) copy-start(bf16[256,512]{1,0:T(8,128)(2,1)S(1)} %collective-permute-done.7.refs_1_.refs_3_) | copy-start | bytes 786436
  40.1 9.5 %collective-permute-start.11 = (bf16[256,512]{1,0:T(8,128)(2,1)S(1)}, bf16[256,512]{1,0:T(8,128)(2,1)S(1)}, u32[]{:S(2)}, u32[]{:S(2)}) collective-permute-start(bf16[256,512]{1,0:T(8,128)(2,1)S(1)} %collective-permute-done.7.refs_1_.refs_3_), channel_id=1, source_target_pairs={{0,1},{1,0},{2,3},{3,2},{4,5},{5,4},{6,7},{7,6},{8,9},{9,8},{10,11... | collective-permute-start | bytes 786440 | tf_op jit(solution)/shard_map/ppermute | solution.py:259
  40.1 17.5 %collective-permute-start.10 = (bf16[256,1024]{1,0:T(8,128)(2,1)}, bf16[256,1024]{1,0:T(8,128)(2,1)S(1)}, u32[]{:S(2)}, u32[]{:S(2)}) collective-permute-start(bf16[256,1024]{1,0:T(8,128)(2,1)} %get-tuple-element.86), channel_id=1, source_target_pairs={{0,0},{1,4},{2,2},{3,6},{4,1},{5,5},{6,3},{7,7},{8,8},{9,12},{10,1... | collective-permute-start | bytes 1572872 | tf_op jit(solution)/shard_map/ppermute | solution.py:259
  44.5 5.1 %copy-start.15 = (bf16[256,512]{1,0:T(8,128)(2,1)}, bf16[256,512]{1,0:T(8,128)(2,1)S(1)}, u32[]{:S(2)}) copy-start(bf16[256,512]{1,0:T(8,128)(2,1)S(1)} %collective-permute-done.8.refs_2_) | copy-start | bytes 786436
  44.5 16.5 %collective-permute-start.9 = (bf16[256,1024]{1,0:T(8,128)(2,1)}, bf16[256,1024]{1,0:T(8,128)(2,1)S(1)}, u32[]{:S(2)}, u32[]{:S(2)}) collective-permute-start(bf16[256,1024]{1,0:T(8,128)(2,1)} %get-tuple-element.91), channel_id=1, source_target_pairs={{0,1},{1,5},{2,3},{3,7},{4,0},{5,4},{6,2},{7,6},{8,9},{9,13},{10,1... | collective-permute-start | bytes 1572872 | tf_op jit(solution)/shard_map/ppermute | solution.py:259
  49.3 7.8 %copy-start.21 = (s32[4]{0:T(128)S(1)}, s32[4]{0:T(128)}, u32[]{:S(2)}) copy-start(s32[4]{0:T(128)} %constant.72.clone) | copy-start | bytes 52
  49.3 25.1 %collective-permute-start.16 = (bf16[256,1024]{1,0:T(8,128)(2,1)}, bf16[256,1024]{1,0:T(8,128)(2,1)S(1)}, u32[]{:S(2)}, u32[]{:S(2)}) collective-permute-start(bf16[256,1024]{1,0:T(8,128)(2,1)} %get-tuple-element.104), channel_id=1, source_target_pairs={{0,8},{1,12},{2,10},{3,14},{4,9},{5,13},{6,11},{7,15},{8,0},{9,4},... | collective-permute-start | bytes 1572872 | tf_op jit(solution)/shard_map/ppermute | solution.py:259
  49.6 0.7 copy-start.16
  55.8 27.9 %collective-permute-start.15 = (bf16[2,256,1024]{2,1,0:T(8,128)(2,1)}, bf16[2,256,1024]{2,1,0:T(8,128)(2,1)}, u32[]{:S(2)}, u32[]{:S(2)}) collective-permute-start(bf16[2,256,1024]{2,1,0:T(8,128)(2,1)} %get-tuple-element.103), channel_id=1, source_target_pairs={{16,0},{17,1},{18,2},{19,3},{20,4},{21,5},{22,6},{23,7},{24,8},{25... | collective-permute-start | bytes 3145736 | tf_op jit(solution)/shard_map/ppermute | solution.py:259
  57.6 30.0 %copy-start.7 = (bf16[256,1024]{1,0:T(8,128)(2,1)}, bf16[256,1024]{1,0:T(8,128)(2,1)S(1)}, u32[]{:S(2)}) copy-start(bf16[256,1024]{1,0:T(8,128)(2,1)S(1)} %collective-permute-done.10.refs_0_) | copy-start | bytes 1572868
  57.6 30.0 %collective-permute-start.14 = (bf16[256,1024]{1,0:T(8,128)(2,1)S(1)}, bf16[256,1024]{1,0:T(8,128)(2,1)S(1)}, u32[]{:S(2)}, u32[]{:S(2)}) collective-permute-start(bf16[256,1024]{1,0:T(8,128)(2,1)S(1)} %collective-permute-done.10.refs_0_), channel_id=1, source_target_pairs={{0,2},{1,3},{2,0},{3,1},{4,6},{5,7},{6,4},{7,5},{8,10},{9,11},{10,... | collective-permute-start | bytes 1572872 | tf_op jit(solution)/shard_map/ppermute | solution.py:259
  61.1 26.6 %copy-start.9 = (bf16[256,1024]{1,0:T(8,128)(2,1)}, bf16[256,1024]{1,0:T(8,128)(2,1)S(1)}, u32[]{:S(2)}) copy-start(bf16[256,1024]{1,0:T(8,128)(2,1)S(1)} %collective-permute-done.9.refs_1_) | copy-start | bytes 1572868
  74.4 42.4 %copy-start.8 = (bf16[256,1024]{1,0:T(8,128)(2,1)}, bf16[256,1024]{1,0:T(8,128)(2,1)S(1)}, u32[]{:S(2)}) copy-start(bf16[256,1024]{1,0:T(8,128)(2,1)S(1)} %collective-permute-done.16.refs_2_) | copy-start | bytes 1572868
  77.5 50.9 %collective-permute-start.21 = (bf16[2,256,1024]{2,1,0:T(8,128)(2,1)}, bf16[2,256,1024]{2,1,0:T(8,128)(2,1)}, u32[]{:S(2)}, u32[]{:S(2)}) collective-permute-start(bf16[2,256,1024]{2,1,0:T(8,128)(2,1)} %get-tuple-element.118), channel_id=1, source_target_pairs={{16,2},{17,3},{18,0},{19,1},{20,6},{21,7},{22,4},{23,5},{24,10},{2... | collective-permute-start | bytes 3145736 | tf_op jit(solution)/shard_map/ppermute | solution.py:259
  78.8 37.4 %collective-permute-start.13 = (bf16[256,1024]{1,0:T(8,128)(2,1)S(1)}, bf16[256,1024]{1,0:T(8,128)(2,1)S(1)}, u32[]{:S(2)}, u32[]{:S(2)}) collective-permute-start(bf16[256,1024]{1,0:T(8,128)(2,1)S(1)} %collective-permute-done.9.refs_1_), channel_id=1, source_target_pairs={{0,2},{1,3},{2,0},{3,1},{4,6},{5,7},{6,4},{7,5},{8,10},{9,11},{10,... | collective-permute-start | bytes 1572872 | tf_op jit(solution)/shard_map/ppermute | solution.py:259
  79.4 36.8 %collective-permute-start.12 = (bf16[256,1024]{1,0:T(8,128)(2,1)}, bf16[256,1024]{1,0:T(8,128)(2,1)}, u32[]{:S(2)}, u32[]{:S(2)}) collective-permute-start(bf16[256,1024]{1,0:T(8,128)(2,1)} %get-tuple-element.101), channel_id=1, source_target_pairs={{0,9},{1,13},{2,11},{3,15},{4,8},{5,12},{6,10},{7,14},{8,1},{9,5},... | collective-permute-start | bytes 1572872 | tf_op jit(solution)/shard_map/ppermute | solution.py:259
  83.8 47.1 %collective-permute-start.20 = (bf16[256,1024]{1,0:T(8,128)(2,1)S(1)}, bf16[256,1024]{1,0:T(8,128)(2,1)S(1)}, u32[]{:S(2)}, u32[]{:S(2)}) collective-permute-start(bf16[256,1024]{1,0:T(8,128)(2,1)S(1)} %collective-permute-done.16.refs_2_), channel_id=1, source_target_pairs={{0,2},{1,3},{2,0},{3,1},{4,6},{5,7},{6,4},{7,5},{8,10},{9,11},{10,... | collective-permute-start | bytes 1572872 | tf_op jit(solution)/shard_map/ppermute | solution.py:259
  87.7 43.2 %copy-start.3 = (bf16[256,1024]{1,0:T(8,128)(2,1)}, bf16[256,1024]{1,0:T(8,128)(2,1)S(1)}, u32[]{:S(2)}) copy-start(bf16[256,1024]{1,0:T(8,128)(2,1)S(1)} %collective-permute-done.14.refs_0_) | copy-start | bytes 1572868
  116.2 14.6 %copy-start.4 = (bf16[256,1024]{1,0:T(8,128)(2,1)}, bf16[256,1024]{1,0:T(8,128)(2,1)S(1)}, u32[]{:S(2)}) copy-start(bf16[256,1024]{1,0:T(8,128)(2,1)S(1)} %collective-permute-done.13.refs_1_) | copy-start | bytes 1572868
  116.2 19.1 %collective-permute-start.19 = (bf16[256,1024]{1,0:T(8,128)(2,1)}, bf16[256,1024]{1,0:T(8,128)(2,1)S(1)}, u32[]{:S(2)}, u32[]{:S(2)}) collective-permute-start(bf16[256,1024]{1,0:T(8,128)(2,1)} %collective-permute-done.12.refs_3_), channel_id=1, source_target_pairs={{0,2},{1,3},{2,0},{3,1},{4,6},{5,7},{6,4},{7,5},{8,10},{9,11},{10,... | collective-permute-start | bytes 1572872 | tf_op jit(solution)/shard_map/ppermute | solution.py:259
  121.8 24.9 %collective-permute-start.18 = (bf16[1024,2,256]{2,1,0:T(2,128)(2,1)}, bf16[1024,2,256]{2,1,0:T(2,128)(2,1)}, u32[]{:S(2)}, u32[]{:S(2)}) collective-permute-start(bf16[1024,2,256]{2,1,0:T(2,128)(2,1)} %get-tuple-element.115), channel_id=1, source_target_pairs={{0,1},{1,0},{2,3},{3,2},{4,5},{5,4},{6,7},{7,6},{8,9},{9,8},{10,11... | collective-permute-start | bytes 3145736 | tf_op jit(solution)/shard_map/ppermute | solution.py:259
  121.8 27.8 %collective-permute-start.17 = (bf16[2,256,1024]{2,1,0:T(8,128)(2,1)}, bf16[2,256,1024]{2,1,0:T(8,128)(2,1)}, u32[]{:S(2)}, u32[]{:S(2)}) collective-permute-start(bf16[2,256,1024]{2,1,0:T(8,128)(2,1)} %shard_map.80), channel_id=1, source_target_pairs={{16,0},{17,1},{18,2},{19,3},{20,4},{21,5},{22,6},{23,7},{24,8},{25... | collective-permute-start | bytes 3145736 | tf_op jit(solution)/shard_map/ppermute | solution.py:259
  128.4 12.8 %copy-start.20 = (f32[2,2,1024]{2,1,0:T(2,128)S(1)}, f32[2,2,1024]{2,1,0:T(2,128)}, u32[]{:S(2)}) copy-start(f32[2,2,1024]{2,1,0:T(2,128)} %get-tuple-element.132) | copy-start | bytes 49156
  130.9 4.4 %copy-start.5 = (bf16[256,1024]{1,0:T(8,128)(2,1)}, bf16[256,1024]{1,0:T(8,128)(2,1)S(1)}, u32[]{:S(2)}) copy-start(bf16[256,1024]{1,0:T(8,128)(2,1)S(1)} %collective-permute-done.20.refs_2_) | copy-start | bytes 1572868
  135.3 0.8 copy-start.6
  141.1 10.5 %collective-permute-start.23 = (bf16[1024,2,256]{2,1,0:T(2,128)(2,1)}, bf16[1024,2,256]{2,1,0:T(2,128)(2,1)S(1)}, u32[]{:S(2)}, u32[]{:S(2)}) collective-permute-start(bf16[1024,2,256]{2,1,0:T(2,128)(2,1)} %get-tuple-element.127), channel_id=1, source_target_pairs={{0,1},{1,0},{2,3},{3,2},{4,5},{5,4},{6,7},{7,6},{8,9},{9,8},{10,11... | collective-permute-start | bytes 3145736 | tf_op jit(solution)/shard_map/ppermute | solution.py:259
  141.2 5.6 %collective-permute-start.22 = (f32[2,2,1024]{2,1,0:T(2,128)S(1)}, f32[2,2,1024]{2,1,0:T(2,128)S(1)}, u32[]{:S(2)}, u32[]{:S(2)}) collective-permute-start(f32[2,2,1024]{2,1,0:T(2,128)S(1)} %copy-done.20), channel_id=1, source_target_pairs={{0,1},{1,0},{2,3},{3,2},{4,5},{5,4},{6,7},{7,6},{8,9},{9,8},{10,11... | collective-permute-start | bytes 49160 | tf_op jit(solution)/shard_map/ppermute | solution.py:259
  141.7 10.0 %collective-permute-start.24 = (f32[2,2,1024]{2,1,0:T(2,128)}, f32[2,2,1024]{2,1,0:T(2,128)S(1)}, u32[]{:S(2)}, u32[]{:S(2)}) collective-permute-start(f32[2,2,1024]{2,1,0:T(2,128)} %get-tuple-element.141), channel_id=1, source_target_pairs={{0,1},{1,0},{2,3},{3,2},{4,5},{5,4},{6,7},{7,6},{8,9},{9,8},{10,11... | collective-permute-start | bytes 49160 | tf_op jit(solution)/shard_map/ppermute | solution.py:259
  146.8 0.6 copy-start.19
  151.7 1.0 copy-start.17
  151.7 1.0 copy-start.18

commit v6 on v4

--- a/solution.py
+++ b/solution.py
@@ -342,9 +342,9 @@
     a_across = step(across_but_first(a_early))
     early_sum = step(summed(now(m_early), a_across))
     far0 = step(far(far0_sent, 0))
-    other_turned = step(turned(slots, (now(g0_core), g1_core, g2_core, g3_core)))
     late_across_begun = behind_across(now(a_late))
     late_own = step(behind(m_late))
+    other_turned = step(turned(slots, (now(g0_core), g1_core, g2_core, g3_core)))
     own_turned = step(turned(slots, (now(g0), g1, g2, g3)))
     near0_x = step(across(near0))
     near1_x = step(near1_x_begun)

time: 144 us -> 145 us (level); the launches traced: 143 us -> 143 us
  starting transfers between devices: 33.2 us -> 25.1 us
  waiting for transfers between devices: 36.6 us -> 43.8 us
    ppermute x25, starting transfers between devices: 33.2 us -> 25.1 us  [move(): return lax.ppermute(x, ('pipe', 'dp', 'mp'), pairs)]
    ppermute x25, waiting for transfers between devices: 36.6 us -> 43.8 us  [move(): return lax.ppermute(x, ('pipe', 'dp', 'mp'), pairs)]
    unnamed x45 -> x47, local copies, waits for them, and re-layouts: 14.7 us -> 14.8 us
  transfers between devices with their start and end apart: 25 -> 25, of which waited for: 7 -> 5; matrix products, arithmetic and copies ran while one was open for 9% -> 9% of each run, Pallas kernels for 37% -> 37%
where the time goes in v6:
time: 145 us; the launch traced here: 143 us
  Pallas kernels  54.6 us (38%)
  waiting for transfers between devices  43.8 us (30%)
  starting transfers between devices  25.1 us (17%)
  local copies, waits for them, and re-layouts  17.1 us (12%)
    ppermute x25, waiting for transfers between devices, move(): return lax.ppermute(x, ('pipe', 'dp', 'mp'), pairs)  43.8 us
    ppermute x25, starting transfers between devices, move(): return lax.ppermute(x, ('pipe', 'dp', 'mp'), pairs)  25.1 us
    pallas_call x4, Pallas kernels, weight_grad(): pl.pallas_call(weight_grad_kernel, grid_spec=pltpu.PrefetchScalarGridSpec...  20.2 us
    unnamed x47, local copies, waits for them, and re-layouts  14.8 us
    pallas_call x2, Pallas kernels, input_grad(): pl.pallas_call(input_grad_kernel, grid_spec=pltpu.PrefetchScalarGridSpec(...  11.1 us
    pallas_call x2, Pallas kernels, turned(): pl.pallas_call(turned_kernel, grid_spec=pltpu.PrefetchScalarGridSpec(num_...  6.3 us
    pallas_call x2, Pallas kernels, chosen(): pl.pallas_call(chosen_kernel, grid_spec=pltpu.PrefetchScalarGridSpec(num_...  5.46 us
    pallas_call x2, Pallas kernels, placed(): pl.pallas_call(placed_kernel if into is None else placed_again_kernel, gr...  4.66 us
  transfers between devices with their start and end apart: 25, of which 5 were waited for; matrix products, arithmetic and copies ran while one was open for 9% of the time, Pallas kernels for 37%

profile of v6, /device:TPU:0, one launch (start us, length us, event | category | flops | bytes accessed | tf_op | source)
XLA Modules:
  0.0 142.6 jit_solution(16943694414187708838)
XLA Ops:
  0.6 0.5 collective-permute-start.1
  1.1 2.3 %slice.4 = bf16[256,2048]{1,0:T(8,128)(2,1)} slice(bf16[256,4096]{1,0:T(8,128)(2,1)} %bitcast.33), slice={[0:256], [2048:4096]} | slice | bytes 2097152 | tf_op jit(solution)/shard_map/slice | solution.py:325
  3.5 2.5 %collective-permute-start.6 = (bf16[256,2048]{1,0:T(8,128)(2,1)}, bf16[256,2048]{1,0:T(8,128)(2,1)S(1)}, u32[]{:S(2)}, u32[]{:S(2)}) collective-permute-start(bf16[256,2048]{1,0:T(8,128)(2,1)} %slice.4), channel_id=1, source_target_pairs={{0,2},{1,3},{2,0},{3,1},{4,6},{5,7},{6,4},{7,5},{8,10},{9,11},{10,... | collective-permute-start | bytes 3145736 | tf_op jit(solution)/shard_map/ppermute | solution.py:259
  6.0 1.0 copy.15
  7.3 1.6 %collective-permute-start = (bf16[256,512]{1,0:T(8,128)(2,1)S(1)}, bf16[256,512]{1,0:T(8,128)(2,1)S(1)}, u32[]{:S(2)}, u32[]{:S(2)}) collective-permute-start(bf16[256,512]{1,0:T(8,128)(2,1)S(1)} %bitcast.40), channel_id=1, source_target_pairs={{0,4},{1,5},{2,6},{3,7},{4,0},{5,1},{6,2},{7,3},{8,12},{9,13},{10,... | collective-permute-start | bytes 786440 | tf_op jit(solution)/shard_map/ppermute | solution.py:259
  8.9 2.6 %collective-permute-start.4 = (bf16[256,512]{1,0:T(8,128)(2,1)S(1)}, bf16[256,512]{1,0:T(8,128)(2,1)S(1)}, u32[]{:S(2)}, u32[]{:S(2)}) collective-permute-start(bf16[256,512]{1,0:T(8,128)(2,1)S(1)} %bitcast.41), channel_id=1, source_target_pairs={{0,8},{1,9},{2,10},{3,11},{4,12},{5,13},{6,14},{7,15},{8,0},{9,1},... | collective-permute-start | bytes 786440 | tf_op jit(solution)/shard_map/ppermute | solution.py:259
  11.4 4.9 %copy.16 = bf16[512,8,2,256]{3,1,2,0:T(8,128)(2,1)} copy(bf16[512,8,2,256]{3,2,1,0:T(2,128)(2,1)} %bitcast.37) | data formatting | bytes 8388608
  16.4 2.9 %copy.17 = bf16[512,8,2,256]{3,1,2,0:T(8,128)(2,1)} copy(bf16[512,8,2,256]{3,2,1,0:T(2,128)(2,1)S(1)} %bitcast.38) | data formatting | bytes 8388608
  19.3 1.9 %collective-permute-done.refs_1_ = bf16[256,512]{1,0:T(8,128)(2,1)S(1)} collective-permute-done((bf16[256,512]{1,0:T(8,128)(2,1)S(1)}, bf16[256,512]{1,0:T(8,128)(2,1)S(1)}, u32[]{:S(2)}, u32[]{:S(2)}) %collective-permute-start) | collective-permute-done | bytes 262176 | tf_op jit(solution)/shard_map/ppermute | solution.py:259
  21.3 2.5 %collective-permute-start.7 = (bf16[256,512]{1,0:T(8,128)(2,1)S(1)}, bf16[256,512]{1,0:T(8,128)(2,1)S(1)}, u32[]{:S(2)}, u32[]{:S(2)}) collective-permute-start(bf16[256,512]{1,0:T(8,128)(2,1)S(1)} %bitcast.42), channel_id=1, source_target_pairs={{0,12},{1,13},{2,14},{3,15},{4,8},{5,9},{6,10},{7,11},{8,4},{9,5},... | collective-permute-start | bytes 786440 | tf_op jit(solution)/shard_map/ppermute | solution.py:259
  23.9 0.7 copy-done.12
  24.6 5.6 %shard_map.76 = (bf16[2,256,1024]{2,1,0:T(8,128)(2,1)}, f32[2,256,1024]{2,1,0:T(8,128)}) custom-call(s32[1]{0:T(128)} %bitcast.1.m, bf16[256,512]{1,0:T(8,128)(2,1)} %bitcast.43, bf16[256,512]{1,0:T(8,128)(2,1)} %copy-done.8, bf16[256,512]{1,0:T(8,128)(2,1)} %copy-done.9, bf16[256,512]{1,0:T(8,128)(2,1)} %copy-done.12, bf16[4096,512]{1,0:T(8,128)(2,1)} %bitcast.24, ...), custom_call_target="tpu_custom_call" | custom-call | tf_op jit(solution)/shard_map/pallas_call | solution.py:61
  30.2 1.6 %collective-permute-start.5 = (bf16[2,256,1024]{2,1,0:T(8,128)(2,1)}, bf16[2,256,1024]{2,1,0:T(8,128)(2,1)}, u32[]{:S(2)}, u32[]{:S(2)}) collective-permute-start(bf16[2,256,1024]{2,1,0:T(8,128)(2,1)} %get-tuple-element.83), channel_id=1, source_target_pairs={{16,18},{17,19},{18,16},{19,17},{20,22},{21,23},{22,20},{23,21},{2... | collective-permute-start | bytes 3145736 | tf_op jit(solution)/shard_map/ppermute | solution.py:259
  31.9 0.7 pad_add_fusion
  32.7 1.0 copy-done
  33.7 2.7 %shard_map.77 = (bf16[256,1024]{1,0:T(8,128)(2,1)}, bf16[256,1024]{1,0:T(8,128)(2,1)}) custom-call(s32[2]{0:T(128)} %get-tuple-element.148.flag, bf16[256,4096]{1,0:T(8,128)(2,1)} %bitcast.34, bf16[256,2048]{1,0:T(8,128)(2,1)} %copy-done), custom_call_target="tpu_custom_call" | custom-call | tf_op jit(solution)/shard_map/pallas_call | solution.py:88
  36.8 1.7 %collective-permute-start.10 = (bf16[256,1024]{1,0:T(8,128)(2,1)}, bf16[256,1024]{1,0:T(8,128)(2,1)S(1)}, u32[]{:S(2)}, u32[]{:S(2)}) collective-permute-start(bf16[256,1024]{1,0:T(8,128)(2,1)} %get-tuple-element.86), channel_id=1, source_target_pairs={{0,0},{1,4},{2,2},{3,6},{4,1},{5,5},{6,3},{7,7},{8,8},{9,12},{10,1... | collective-permute-start | bytes 1572872 | tf_op jit(solution)/shard_map/ppermute | solution.py:259
  38.5 2.7 %shard_map.78 = (bf16[256,1024]{1,0:T(8,128)(2,1)}, bf16[256,1024]{1,0:T(8,128)(2,1)}) custom-call(s32[2]{0:T(128)} %get-tuple-element.147.flag, bf16[256,4096]{1,0:T(8,128)(2,1)} %bitcast.35, bf16[256,2048]{1,0:T(8,128)(2,1)} %copy-done), custom_call_target="tpu_custom_call" | custom-call | tf_op jit(solution)/shard_map/pallas_call | solution.py:88
  41.3 0.7 collective-permute-start.9
  42.0 0.7 copy-done.14
  42.7 5.5 %shard_map.79 = (bf16[2,256,1024]{2,1,0:T(8,128)(2,1)}, bf16[2,256,1024]{2,1,0:T(8,128)(2,1)}) custom-call(s32[1]{0:T(128)} %bitcast.1.m, bf16[256,512]{1,0:T(8,128)(2,1)} %copy-done.10, bf16[256,512]{1,0:T(8,128)(2,1)} %copy-done.11, bf16[256,512]{1,0:T(8,128)(2,1)} %copy-done.13, bf16[256,512]{1,0:T(8,128)(2,1)} %copy-done.14, bf16[4096,512]{1,0:T(8,128)(2,1)} %bitcast.26, ...), custom_call_target="tpu_custom_call" | custom-call | tf_op jit(solution)/shard_map/pallas_call | solution.py:61
  48.2 1.3 collective-permute-start.15
  49.5 2.8 %collective-permute-start.16 = (bf16[256,1024]{1,0:T(8,128)(2,1)S(1)}, bf16[256,1024]{1,0:T(8,128)(2,1)}, u32[]{:S(2)}, u32[]{:S(2)}) collective-permute-start(bf16[256,1024]{1,0:T(8,128)(2,1)S(1)} %copy-done.19), channel_id=1, source_target_pairs={{0,8},{1,12},{2,10},{3,14},{4,9},{5,13},{6,11},{7,15},{8,0},{9,4},... | collective-permute-start | bytes 1572872 | tf_op jit(solution)/shard_map/ppermute | solution.py:259
  52.3 0.5 collective-permute-start.14
  52.8 0.7 collective-permute-done.9.refs_1_
  53.5 0.8 collective-permute-start.13
  54.3 2.7 %shard_map.80 = bf16[2,256,1024]{2,1,0:T(8,128)(2,1)} custom-call(f32[2,256,1024]{2,1,0:T(8,128)} %get-tuple-element.98.a_ref, bf16[2,256,1024]{2,1,0:T(8,128)(2,1)} %collective-permute-done.5.b_ref), custom_call_target="tpu_custom_call" | custom-call | tf_op jit(solution)/shard_map/pallas_call | solution.py:108
  57.0 19.5 %collective-permute-done.16.refs_2_ = bf16[256,1024]{1,0:T(8,128)(2,1)} collective-permute-done((bf16[256,1024]{1,0:T(8,128)(2,1)S(1)}, bf16[256,1024]{1,0:T(8,128)(2,1)}, u32[]{:S(2)}, u32[]{:S(2)}) %collective-permute-start.16) | collective-permute-done | bytes 524320 | tf_op jit(solution)/shard_map/ppermute | solution.py:259
  76.5 1.3 collective-permute-start.20
  77.8 0.5 collective-permute-start.12
  78.9 0.5 collective-permute-start.21
  79.4 3.2 %shard_map.81.refs_4_ = bf16[4,512,256]{2,1,0:T(8,128)(2,1)} custom-call(s32[4]{0:T(128)} %broadcast_select_fusion.slots, bf16[256,512]{1,0:T(8,128)(2,1)} %copy-done.9, bf16[256,512]{1,0:T(8,128)(2,1)} %copy-done.12, bf16[256,512]{1,0:T(8,128)(2,1)} %copy-done.13, bf16[256,512]{1,0:T(8,128)(2,1)} %copy-done.14), custom_call_target="tpu_custom_call" | custom-call | tf_op jit(solution)/shard_map/pallas_call | solution.py:23
  82.6 3.1 %shard_map.82.refs_4_ = bf16[4,512,256]{2,1,0:T(8,128)(2,1)} custom-call(s32[4]{0:T(128)} %broadcast_select_fusion.slots, bf16[256,512]{1,0:T(8,128)(2,1)} %bitcast.44, bf16[256,512]{1,0:T(8,128)(2,1)} %copy-done.8, bf16[256,512]{1,0:T(8,128)(2,1)} %copy-done.10, bf16[256,512]{1,0:T(8,128)(2,1)} %copy-done.11), custom_call_target="tpu_custom_call" | custom-call | tf_op jit(solution)/shard_map/pallas_call | solution.py:23
  85.7 14.6 %collective-permute-done.13.refs_1_ = bf16[256,1024]{1,0:T(8,128)(2,1)S(1)} collective-permute-done((bf16[256,1024]{1,0:T(8,128)(2,1)S(1)}, bf16[256,1024]{1,0:T(8,128)(2,1)S(1)}, u32[]{:S(2)}, u32[]{:S(2)}) %collective-permute-start.13) | collective-permute-done | bytes 524320 | tf_op jit(solution)/shard_map/ppermute | solution.py:259
  100.8 5.1 %shard_map.83 = (bf16[1024,2,256]{2,1,0:T(2,128)(2,1)}, f32[2,2,1024]{2,1,0:T(2,128)}) custom-call(s32[1]{0:T(128)} %constant.67.clone.1.at, bf16[256,1024]{1,0:T(8,128)(2,1)} %copy-done.6, bf16[256,1024]{1,0:T(8,128)(2,1)} %copy-done.7, bf16[256,1024]{1,0:T(8,128)(2,1)} %collective-permute-done.16.refs_2_, ...), custom_call_target="tpu_custom_call" | custom-call | tf_op jit(solution)/shard_map/pallas_call | solution.py:152
  106.2 1.5 %collective-permute-start.17 = (bf16[2,256,1024]{2,1,0:T(8,128)(2,1)}, bf16[2,256,1024]{2,1,0:T(8,128)(2,1)S(1)}, u32[]{:S(2)}, u32[]{:S(2)}) collective-permute-start(bf16[2,256,1024]{2,1,0:T(8,128)(2,1)} %shard_map.80), channel_id=1, source_target_pairs={{16,0},{17,1},{18,2},{19,3},{20,4},{21,5},{22,6},{23,7},{24,8},{25... | collective-permute-start | bytes 3145736 | tf_op jit(solution)/shard_map/ppermute | solution.py:259
  107.6 5.1 %shard_map.84 = (bf16[4096,2,256]{2,1,0:T(2,128)(2,1)}, f32[2,2,4096]{2,1,0:T(2,128)}) custom-call(s32[1]{0:T(128)} %bitcast.8.at, bf16[256,1024]{1,0:T(8,128)(2,1)} %copy-done.6, bf16[256,1024]{1,0:T(8,128)(2,1)} %copy-done.7, bf16[256,1024]{1,0:T(8,128)(2,1)} %collective-permute-done.16.refs_2_, bf16[256,1024]{1,0:T(8,128)(2,1)} %collective-permute-done.12.refs_3_, ...), custom_call_target="tpu_custom_call" | custom-call | tf_op jit(solution)/shard_map/pallas_call | solution.py:152
  112.7 2.6 %shard_map.85.refs_1_ = bf16[1024,1024]{1,0:T(8,128)(2,1)} custom-call(s32[1]{0:T(128)} %bitcast.group, bf16[2,256,1024]{2,1,0:T(8,128)(2,1)} %collective-permute-done.15.refs_0_, bf16[2,256,1024]{2,1,0:T(8,128)(2,1)} %collective-permute-done.20.refs_1_), custom_call_target="tpu_custom_call" | custom-call | tf_op jit(solution)/shard_map/pallas_call | solution.py:227
  115.3 7.0 %collective-permute-done.19.refs_3_ = bf16[256,1024]{1,0:T(8,128)(2,1)S(1)} collective-permute-done((bf16[256,1024]{1,0:T(8,128)(2,1)}, bf16[256,1024]{1,0:T(8,128)(2,1)S(1)}, u32[]{:S(2)}, u32[]{:S(2)}) %collective-permute-start.19) | collective-permute-done | bytes 524320 | tf_op jit(solution)/shard_map/ppermute | solution.py:259
  122.4 0.8 copy-done.5
  123.2 5.0 %shard_map.86 = (bf16[1024,2,256]{2,1,0:T(2,128)(2,1)}, f32[2,2,1024]{2,1,0:T(2,128)}) custom-call(s32[1]{0:T(128)} %constant.67.clone.1.at, bf16[256,1024]{1,0:T(8,128)(2,1)} %copy-done.2, bf16[256,1024]{1,0:T(8,128)(2,1)} %copy-done.3, bf16[256,1024]{1,0:T(8,128)(2,1)} %copy-done.4, bf16[256,1024]{1,0:T(8,128)(2,1)} %copy-done.5, ...), custom_call_target="tpu_custom_call" | custom-call | tf_op jit(solution)/shard_map/pallas_call | solution.py:152
  128.8 5.0 %shard_map.87 = (bf16[4096,2,256]{2,1,0:T(2,128)(2,1)}, f32[2,2,4096]{2,1,0:T(2,128)}) custom-call(s32[1]{0:T(128)} %bitcast.7.at, bf16[256,1024]{1,0:T(8,128)(2,1)} %copy-done.2, bf16[256,1024]{1,0:T(8,128)(2,1)} %copy-done.3, bf16[256,1024]{1,0:T(8,128)(2,1)} %copy-done.4, ...), custom_call_target="tpu_custom_call", output_to_operand_aliasing={{0}: (6, {}), {1}: (7, {})} | custom-call | tf_op jit(solution)/shard_map/pallas_call | solution.py:152
  133.8 0.6 copy-done.18
  134.4 2.1 %shard_map.88 = (bf16[4096,2,256]{2,1,0:T(2,128)(2,1)}, f32[2,2,4096]{2,1,0:T(2,128)}) custom-call(s32[1]{0:T(128)} %bitcast.6.at, bf16[1024,2,256]{2,1,0:T(2,128)(2,1)} %collective-permute-done.18.mantissa_ref, f32[2,2,1024]{2,1,0:T(2,128)} %copy-done.18, ...), custom_call_target="tpu_custom_call", output_to_operand_aliasing={{0}: (3, {}), {1}: (4, {})} | custom-call | tf_op jit(solution)/shard_map/pallas_call | solution.py:183
  136.5 1.0 copy-done.15
  137.5 2.0 %shard_map.89 = bf16[1024,1024]{1,0:T(8,128)(2,1)} custom-call(s32[1]{0:T(128)} %bitcast.group, bf16[2,256,1024]{2,1,0:T(8,128)(2,1)} %copy-done.15, bf16[1024,1024]{1,0:T(8,128)(2,1)} %shard_map.85.refs_1_), custom_call_target="tpu_custom_call", output_to_operand_aliasing={{}: (2, {})} | custom-call | tf_op jit(solution)/shard_map/pallas_call | solution.py:227
  139.6 1.0 copy-done.16
  140.6 2.1 %shard_map.90 = (bf16[4096,2,256]{2,1,0:T(2,128)(2,1)}, f32[2,2,4096]{2,1,0:T(2,128)}) custom-call(s32[1]{0:T(128)} %bitcast.10.at, bf16[1024,2,256]{2,1,0:T(2,128)(2,1)} %copy-done.16, f32[2,2,1024]{2,1,0:T(2,128)} %copy-done.17, bf16[4096,2,256]{2,1,0:T(2,128)(2,1)} %get-tuple-element.136.held_m, ...), custom_call_target="tpu_custom_call", output_to_operand_aliasing={{0}: (3, {}), {1}: (4, {})} | custom-call | tf_op jit(solution)/shard_map/pallas_call | solution.py:183
  (67 shorter events, 2.8 us)
Async XLA Ops:
  0.6 15.8 %collective-permute-start.1 = (bf16[1,4096,2,256]{3,2,1,0:T(2,128)(2,1)}, bf16[1,4096,2,256]{3,2,1,0:T(2,128)(2,1)S(1)}, u32[]{:S(2)}, u32[]{:S(2)}) collective-permute-start(bf16[1,4096,2,256]{3,2,1,0:T(2,128)(2,1)} %param.7), channel_id=1, source_target_pairs={{0,1},{1,0},{2,3},{3,2},{4,5},{5,4},{6,7},{7,6},{8,9},{9,8},{10,11... | collective-permute-start | bytes 12582920 | tf_op jit(solution)/shard_map/ppermute | solution.py:259
  3.5 29.2 %collective-permute-start.6 = (bf16[256,2048]{1,0:T(8,128)(2,1)}, bf16[256,2048]{1,0:T(8,128)(2,1)S(1)}, u32[]{:S(2)}, u32[]{:S(2)}) collective-permute-start(bf16[256,2048]{1,0:T(8,128)(2,1)} %slice.4), channel_id=1, source_target_pairs={{0,2},{1,3},{2,0},{3,1},{4,6},{5,7},{6,4},{7,5},{8,10},{9,11},{10,... | collective-permute-start | bytes 3145736 | tf_op jit(solution)/shard_map/ppermute | solution.py:259
  7.0 14.3 %copy-start.1 = (bf16[32,8,2,256]{3,1,2,0:T(8,128)(2,1)}, bf16[32,8,2,256]{3,1,2,0:T(8,128)(2,1)S(1)}, u32[]{:S(2)}) copy-start(bf16[32,8,2,256]{3,1,2,0:T(8,128)(2,1)S(1)} %copy.15) | copy-start | bytes 786436
  7.0 12.3 %collective-permute-start.2 = (bf16[256,512]{1,0:T(8,128)(2,1)S(1)}, bf16[256,512]{1,0:T(8,128)(2,1)S(1)}, u32[]{:S(2)}, u32[]{:S(2)}) collective-permute-start(bf16[256,512]{1,0:T(8,128)(2,1)S(1)} %bitcast.39), channel_id=1, source_target_pairs={{0,1},{1,0},{2,3},{3,2},{4,5},{5,4},{6,7},{7,6},{8,9},{9,8},{10,11... | collective-permute-start | bytes 786440 | tf_op jit(solution)/shard_map/ppermute | solution.py:259
  7.3 14.0 %collective-permute-start = (bf16[256,512]{1,0:T(8,128)(2,1)S(1)}, bf16[256,512]{1,0:T(8,128)(2,1)S(1)}, u32[]{:S(2)}, u32[]{:S(2)}) collective-permute-start(bf16[256,512]{1,0:T(8,128)(2,1)S(1)} %bitcast.40), channel_id=1, source_target_pairs={{0,4},{1,5},{2,6},{3,7},{4,0},{5,1},{6,2},{7,3},{8,12},{9,13},{10,... | collective-permute-start | bytes 786440 | tf_op jit(solution)/shard_map/ppermute | solution.py:259
  8.9 15.0 %collective-permute-start.4 = (bf16[256,512]{1,0:T(8,128)(2,1)S(1)}, bf16[256,512]{1,0:T(8,128)(2,1)S(1)}, u32[]{:S(2)}, u32[]{:S(2)}) collective-permute-start(bf16[256,512]{1,0:T(8,128)(2,1)S(1)} %bitcast.41), channel_id=1, source_target_pairs={{0,8},{1,9},{2,10},{3,11},{4,12},{5,13},{6,14},{7,15},{8,0},{9,1},... | collective-permute-start | bytes 786440 | tf_op jit(solution)/shard_map/ppermute | solution.py:259
  19.3 4.5 %copy-start.9 = (bf16[256,512]{1,0:T(8,128)(2,1)}, bf16[256,512]{1,0:T(8,128)(2,1)S(1)}, u32[]{:S(2)}) copy-start(bf16[256,512]{1,0:T(8,128)(2,1)S(1)} %collective-permute-done.2.refs_2_.refs_0_) | copy-start | bytes 786436
  21.3 2.6 %copy-start.8 = (bf16[256,512]{1,0:T(8,128)(2,1)}, bf16[256,512]{1,0:T(8,128)(2,1)S(1)}, u32[]{:S(2)}) copy-start(bf16[256,512]{1,0:T(8,128)(2,1)S(1)} %collective-permute-done.refs_1_) | copy-start | bytes 786436
  21.3 2.6 %collective-permute-start.3 = (bf16[256,512]{1,0:T(8,128)(2,1)S(1)}, bf16[256,512]{1,0:T(8,128)(2,1)S(1)}, u32[]{:S(2)}, u32[]{:S(2)}) collective-permute-start(bf16[256,512]{1,0:T(8,128)(2,1)S(1)} %collective-permute-done.refs_1_), channel_id=1, source_target_pairs={{0,1},{1,0},{2,3},{3,2},{4,5},{5,4},{6,7},{7,6},{8,9},{9,8},{10,11... | collective-permute-start | bytes 786440 | tf_op jit(solution)/shard_map/ppermute | solution.py:259
  21.3 15.1 %collective-permute-start.7 = (bf16[256,512]{1,0:T(8,128)(2,1)S(1)}, bf16[256,512]{1,0:T(8,128)(2,1)S(1)}, u32[]{:S(2)}, u32[]{:S(2)}) collective-permute-start(bf16[256,512]{1,0:T(8,128)(2,1)S(1)} %bitcast.42), channel_id=1, source_target_pairs={{0,12},{1,13},{2,14},{3,15},{4,8},{5,9},{6,10},{7,11},{8,4},{9,5},... | collective-permute-start | bytes 786440 | tf_op jit(solution)/shard_map/ppermute | solution.py:259
  23.8 8.7 %copy-start.10 = (bf16[256,512]{1,0:T(8,128)(2,1)}, bf16[256,512]{1,0:T(8,128)(2,1)S(1)}, u32[]{:S(2)}) copy-start(bf16[256,512]{1,0:T(8,128)(2,1)S(1)} %collective-permute-done.4.refs_0_.refs_2_) | copy-start | bytes 786436
  23.9 0.8 copy-start.12
  30.2 24.1 %collective-permute-start.5 = (bf16[2,256,1024]{2,1,0:T(8,128)(2,1)}, bf16[2,256,1024]{2,1,0:T(8,128)(2,1)}, u32[]{:S(2)}, u32[]{:S(2)}) collective-permute-start(bf16[2,256,1024]{2,1,0:T(8,128)(2,1)} %get-tuple-element.83), channel_id=1, source_target_pairs={{16,18},{17,19},{18,16},{19,17},{20,22},{21,23},{22,20},{23,21},{2... | collective-permute-start | bytes 3145736 | tf_op jit(solution)/shard_map/ppermute | solution.py:259
  32.5 8.7 %collective-permute-start.8 = (bf16[256,512]{1,0:T(8,128)(2,1)S(1)}, bf16[256,512]{1,0:T(8,128)(2,1)S(1)}, u32[]{:S(2)}, u32[]{:S(2)}) collective-permute-start(bf16[256,512]{1,0:T(8,128)(2,1)S(1)} %collective-permute-done.4.refs_0_.refs_2_), channel_id=1, source_target_pairs={{0,1},{1,0},{2,3},{3,2},{4,5},{5,4},{6,7},{7,6},{8,9},{9,8},{10,11... | collective-permute-start | bytes 786440 | tf_op jit(solution)/shard_map/ppermute | solution.py:259
  32.7 1.0 copy-start
  36.4 5.5 %copy-start.11 = (bf16[256,512]{1,0:T(8,128)(2,1)}, bf16[256,512]{1,0:T(8,128)(2,1)S(1)}, u32[]{:S(2)}) copy-start(bf16[256,512]{1,0:T(8,128)(2,1)S(1)} %collective-permute-done.7.refs_1_.refs_3_) | copy-start | bytes 786436
  36.4 5.5 %collective-permute-start.11 = (bf16[256,512]{1,0:T(8,128)(2,1)S(1)}, bf16[256,512]{1,0:T(8,128)(2,1)S(1)}, u32[]{:S(2)}, u32[]{:S(2)}) collective-permute-start(bf16[256,512]{1,0:T(8,128)(2,1)S(1)} %collective-permute-done.7.refs_1_.refs_3_), channel_id=1, source_target_pairs={{0,1},{1,0},{2,3},{3,2},{4,5},{5,4},{6,7},{7,6},{8,9},{9,8},{10,11... | collective-permute-start | bytes 786440 | tf_op jit(solution)/shard_map/ppermute | solution.py:259
  36.8 15.4 %collective-permute-start.10 = (bf16[256,1024]{1,0:T(8,128)(2,1)}, bf16[256,1024]{1,0:T(8,128)(2,1)S(1)}, u32[]{:S(2)}, u32[]{:S(2)}) collective-permute-start(bf16[256,1024]{1,0:T(8,128)(2,1)} %get-tuple-element.86), channel_id=1, source_target_pairs={{0,0},{1,4},{2,2},{3,6},{4,1},{5,5},{6,3},{7,7},{8,8},{9,12},{10,1... | collective-permute-start | bytes 1572872 | tf_op jit(solution)/shard_map/ppermute | solution.py:259
  41.3 0.7 copy-start.13
  41.3 8.2 %copy-start.19 = (bf16[256,1024]{1,0:T(8,128)(2,1)S(1)}, bf16[256,1024]{1,0:T(8,128)(2,1)}, u32[]{:S(2)}) copy-start(bf16[256,1024]{1,0:T(8,128)(2,1)} %get-tuple-element.104) | copy-start | bytes 1572868
  41.3 12.2 %collective-permute-start.9 = (bf16[256,1024]{1,0:T(8,128)(2,1)}, bf16[256,1024]{1,0:T(8,128)(2,1)S(1)}, u32[]{:S(2)}, u32[]{:S(2)}) collective-permute-start(bf16[256,1024]{1,0:T(8,128)(2,1)} %get-tuple-element.91), channel_id=1, source_target_pairs={{0,1},{1,5},{2,3},{3,7},{4,0},{5,4},{6,2},{7,6},{8,9},{9,13},{10,1... | collective-permute-start | bytes 1572872 | tf_op jit(solution)/shard_map/ppermute | solution.py:259
  42.0 0.7 copy-start.14
  48.2 30.2 %copy-start.21 = (s32[4]{0:T(128)S(1)}, s32[4]{0:T(128)}, u32[]{:S(2)}) copy-start(s32[4]{0:T(128)} %constant.72.clone) | copy-start | bytes 52
  48.2 30.7 %collective-permute-start.15 = (bf16[2,256,1024]{2,1,0:T(8,128)(2,1)}, bf16[2,256,1024]{2,1,0:T(8,128)(2,1)}, u32[]{:S(2)}, u32[]{:S(2)}) collective-permute-start(bf16[2,256,1024]{2,1,0:T(8,128)(2,1)} %get-tuple-element.103), channel_id=1, source_target_pairs={{16,0},{17,1},{18,2},{19,3},{20,4},{21,5},{22,6},{23,7},{24,8},{25... | collective-permute-start | bytes 3145736 | tf_op jit(solution)/shard_map/ppermute | solution.py:259
  49.5 27.1 %collective-permute-start.16 = (bf16[256,1024]{1,0:T(8,128)(2,1)S(1)}, bf16[256,1024]{1,0:T(8,128)(2,1)}, u32[]{:S(2)}, u32[]{:S(2)}) collective-permute-start(bf16[256,1024]{1,0:T(8,128)(2,1)S(1)} %copy-done.19), channel_id=1, source_target_pairs={{0,8},{1,12},{2,10},{3,14},{4,9},{5,13},{6,11},{7,15},{8,0},{9,4},... | collective-permute-start | bytes 1572872 | tf_op jit(solution)/shard_map/ppermute | solution.py:259
  52.3 33.4 %copy-start.6 = (bf16[256,1024]{1,0:T(8,128)(2,1)}, bf16[256,1024]{1,0:T(8,128)(2,1)S(1)}, u32[]{:S(2)}) copy-start(bf16[256,1024]{1,0:T(8,128)(2,1)S(1)} %collective-permute-done.10.refs_0_) | copy-start | bytes 1572868
  52.3 33.4 %collective-permute-start.14 = (bf16[256,1024]{1,0:T(8,128)(2,1)S(1)}, bf16[256,1024]{1,0:T(8,128)(2,1)S(1)}, u32[]{:S(2)}, u32[]{:S(2)}) collective-permute-start(bf16[256,1024]{1,0:T(8,128)(2,1)S(1)} %collective-permute-done.10.refs_0_), channel_id=1, source_target_pairs={{0,2},{1,3},{2,0},{3,1},{4,6},{5,7},{6,4},{7,5},{8,10},{9,11},{10,... | collective-permute-start | bytes 1572872 | tf_op jit(solution)/shard_map/ppermute | solution.py:259
  53.5 32.2 %copy-start.7 = (bf16[256,1024]{1,0:T(8,128)(2,1)}, bf16[256,1024]{1,0:T(8,128)(2,1)S(1)}, u32[]{:S(2)}) copy-start(bf16[256,1024]{1,0:T(8,128)(2,1)S(1)} %collective-permute-done.9.refs_1_) | copy-start | bytes 1572868
  53.5 46.8 %collective-permute-start.13 = (bf16[256,1024]{1,0:T(8,128)(2,1)S(1)}, bf16[256,1024]{1,0:T(8,128)(2,1)S(1)}, u32[]{:S(2)}, u32[]{:S(2)}) collective-permute-start(bf16[256,1024]{1,0:T(8,128)(2,1)S(1)} %collective-permute-done.9.refs_1_), channel_id=1, source_target_pairs={{0,2},{1,3},{2,0},{3,1},{4,6},{5,7},{6,4},{7,5},{8,10},{9,11},{10,... | collective-permute-start | bytes 1572872 | tf_op jit(solution)/shard_map/ppermute | solution.py:259
  76.5 36.2 %collective-permute-start.20 = (bf16[2,256,1024]{2,1,0:T(8,128)(2,1)}, bf16[2,256,1024]{2,1,0:T(8,128)(2,1)}, u32[]{:S(2)}, u32[]{:S(2)}) collective-permute-start(bf16[2,256,1024]{2,1,0:T(8,128)(2,1)} %get-tuple-element.118), channel_id=1, source_target_pairs={{16,2},{17,3},{18,0},{19,1},{20,6},{21,7},{22,4},{23,5},{24,10},{2... | collective-permute-start | bytes 3145736 | tf_op jit(solution)/shard_map/ppermute | solution.py:259
  77.8 22.5 %collective-permute-start.12 = (bf16[256,1024]{1,0:T(8,128)(2,1)}, bf16[256,1024]{1,0:T(8,128)(2,1)}, u32[]{:S(2)}, u32[]{:S(2)}) collective-permute-start(bf16[256,1024]{1,0:T(8,128)(2,1)} %get-tuple-element.101), channel_id=1, source_target_pairs={{0,9},{1,13},{2,11},{3,15},{4,8},{5,12},{6,10},{7,14},{8,1},{9,5},... | collective-permute-start | bytes 1572872 | tf_op jit(solution)/shard_map/ppermute | solution.py:259
  78.9 33.8 %collective-permute-start.21 = (bf16[256,1024]{1,0:T(8,128)(2,1)}, bf16[256,1024]{1,0:T(8,128)(2,1)S(1)}, u32[]{:S(2)}, u32[]{:S(2)}) collective-permute-start(bf16[256,1024]{1,0:T(8,128)(2,1)} %collective-permute-done.16.refs_2_), channel_id=1, source_target_pairs={{0,2},{1,3},{2,0},{3,1},{4,6},{5,7},{6,4},{7,5},{8,10},{9,11},{10,... | collective-permute-start | bytes 1572872 | tf_op jit(solution)/shard_map/ppermute | solution.py:259
  85.7 29.6 %copy-start.2 = (bf16[256,1024]{1,0:T(8,128)(2,1)}, bf16[256,1024]{1,0:T(8,128)(2,1)S(1)}, u32[]{:S(2)}) copy-start(bf16[256,1024]{1,0:T(8,128)(2,1)S(1)} %collective-permute-done.14.refs_0_) | copy-start | bytes 1572868
  100.3 15.0 %copy-start.3 = (bf16[256,1024]{1,0:T(8,128)(2,1)}, bf16[256,1024]{1,0:T(8,128)(2,1)S(1)}, u32[]{:S(2)}) copy-start(bf16[256,1024]{1,0:T(8,128)(2,1)S(1)} %collective-permute-done.13.refs_1_) | copy-start | bytes 1572868
  100.3 22.0 %collective-permute-start.19 = (bf16[256,1024]{1,0:T(8,128)(2,1)}, bf16[256,1024]{1,0:T(8,128)(2,1)S(1)}, u32[]{:S(2)}, u32[]{:S(2)}) collective-permute-start(bf16[256,1024]{1,0:T(8,128)(2,1)} %collective-permute-done.12.refs_3_), channel_id=1, source_target_pairs={{0,2},{1,3},{2,0},{3,1},{4,6},{5,7},{6,4},{7,5},{8,10},{9,11},{10,... | collective-permute-start | bytes 1572872 | tf_op jit(solution)/shard_map/ppermute | solution.py:259
  105.9 27.9 %collective-permute-start.18 = (bf16[1024,2,256]{2,1,0:T(2,128)(2,1)}, bf16[1024,2,256]{2,1,0:T(2,128)(2,1)}, u32[]{:S(2)}, u32[]{:S(2)}) collective-permute-start(bf16[1024,2,256]{2,1,0:T(2,128)(2,1)} %get-tuple-element.115), channel_id=1, source_target_pairs={{0,1},{1,0},{2,3},{3,2},{4,5},{5,4},{6,7},{7,6},{8,9},{9,8},{10,11... | collective-permute-start | bytes 3145736 | tf_op jit(solution)/shard_map/ppermute | solution.py:259
  106.2 30.3 %collective-permute-start.17 = (bf16[2,256,1024]{2,1,0:T(8,128)(2,1)}, bf16[2,256,1024]{2,1,0:T(8,128)(2,1)S(1)}, u32[]{:S(2)}, u32[]{:S(2)}) collective-permute-start(bf16[2,256,1024]{2,1,0:T(8,128)(2,1)} %shard_map.80), channel_id=1, source_target_pairs={{16,0},{17,1},{18,2},{19,3},{20,4},{21,5},{22,6},{23,7},{24,8},{25... | collective-permute-start | bytes 3145736 | tf_op jit(solution)/shard_map/ppermute | solution.py:259
  112.7 15.5 %copy-start.20 = (f32[2,2,1024]{2,1,0:T(2,128)S(1)}, f32[2,2,1024]{2,1,0:T(2,128)}, u32[]{:S(2)}) copy-start(f32[2,2,1024]{2,1,0:T(2,128)} %get-tuple-element.132) | copy-start | bytes 49156
  112.7 9.7 %copy-start.4 = (bf16[256,1024]{1,0:T(8,128)(2,1)}, bf16[256,1024]{1,0:T(8,128)(2,1)S(1)}, u32[]{:S(2)}) copy-start(bf16[256,1024]{1,0:T(8,128)(2,1)S(1)} %collective-permute-done.21.refs_2_) | copy-start | bytes 1572868
  122.4 0.8 copy-start.5
  128.2 11.4 %collective-permute-start.23 = (bf16[1024,2,256]{2,1,0:T(2,128)(2,1)}, bf16[1024,2,256]{2,1,0:T(2,128)(2,1)S(1)}, u32[]{:S(2)}, u32[]{:S(2)}) collective-permute-start(bf16[1024,2,256]{2,1,0:T(2,128)(2,1)} %get-tuple-element.127), channel_id=1, source_target_pairs={{0,1},{1,0},{2,3},{3,2},{4,5},{5,4},{6,7},{7,6},{8,9},{9,8},{10,11... | collective-permute-start | bytes 3145736 | tf_op jit(solution)/shard_map/ppermute | solution.py:259
  128.2 5.6 %collective-permute-start.22 = (f32[2,2,1024]{2,1,0:T(2,128)S(1)}, f32[2,2,1024]{2,1,0:T(2,128)S(1)}, u32[]{:S(2)}, u32[]{:S(2)}) collective-permute-start(f32[2,2,1024]{2,1,0:T(2,128)S(1)} %copy-done.20), channel_id=1, source_target_pairs={{0,1},{1,0},{2,3},{3,2},{4,5},{5,4},{6,7},{7,6},{8,9},{9,8},{10,11... | collective-permute-start | bytes 49160 | tf_op jit(solution)/shard_map/ppermute | solution.py:259
  128.7 10.9 %collective-permute-start.24 = (f32[2,2,1024]{2,1,0:T(2,128)}, f32[2,2,1024]{2,1,0:T(2,128)S(1)}, u32[]{:S(2)}, u32[]{:S(2)}) collective-permute-start(f32[2,2,1024]{2,1,0:T(2,128)} %get-tuple-element.141), channel_id=1, source_target_pairs={{0,1},{1,0},{2,3},{3,2},{4,5},{5,4},{6,7},{7,6},{8,9},{9,8},{10,11... | collective-permute-start | bytes 49160 | tf_op jit(solution)/shard_map/ppermute | solution.py:259
  133.8 0.6 copy-start.18
  136.5 1.0 copy-start.15
  139.6 1.0 copy-start.16
  139.6 1.0 copy-start.17
